TPU v7x, 32 devices: a whole 2x2x4 slice. The times are simulated.
32 devices in a mesh: sub: 16 (over z, y, x), sep: 2 (over core).
Axes of the slice: x: 2, y: 2, z: 4, core: 2. Of those that a mesh axis runs over, the one named last changes fastest.
Arguments:
- sources: bfloat16 [16, 2, 768, 256], P('sub', 'sep'), may hold values from -6 to 6
- inner_inv: bfloat16 [16, 2, 768, 768], P('sub', 'sep'), as said below
- coupling: bfloat16 [16, 2, 512, 768], P('sub', 'sep'), may hold values from -0.0546875 to 0.0546875
- boundary_map: int32 [16, 2, 512], P('sub', 'sep'), may hold values from 0 to 479, as said below
- sep_inv_0: bfloat16 [16, 64, 64], P('sub', 'sep'), as said below
- sep_inv_1: bfloat16 [16, 128, 128], P('sub', 'sep'), as said below
- sep_inv_2: bfloat16 [16, 256, 256], P('sub', 'sep'), as said below
- sep_inv_3: bfloat16 [16, 512, 512], P('sub', 'sep'), as said below
- sep_couple_0: bfloat16 [16, 128, 64], P('sub', 'sep'), as said below
- sep_couple_1: bfloat16 [16, 256, 128], P('sub', 'sep'), as said below
- sep_couple_2: bfloat16 [16, 512, 256], P('sub', 'sep'), as said below
Outputs:
- inner_solution: bfloat16 [16, 2, 768, 256], P('sub', 'sep')
- sep_solution: bfloat16 [16, 2, 480, 256], P('sub', 'sep')
Inputs may be any that keep to these rules, and one draw needn't show every extreme that they name: `boundary_map`: an entry m with (2^l - 1) * 32 <= m < (2^(l+1) - 1) * 32 names row m - (2^l - 1) * 32 of the leaf's own strip in the level-l separator above its subdomain. Every inner_inv[s, p] is lower triangular with a positive diagonal. Every sep_inv_0[s] is lower triangular with a positive diagonal, and equal for all s of one level-0 group. Every sep_inv_1[s] is lower triangular with a positive diagonal, and equal for all s of one level-1 group. Every sep_inv_2[s] is lower triangular with a positive diagonal, and equal for all s of one level-2 group. Every sep_inv_3[s] is lower triangular with a positive diagonal, and equal for all s of one level-3 group. sep_couple_0[s] is equal for all s of one level-0 group. sep_couple_1[s] is equal for all s of one level-1 group. sep_couple_2[s] is equal for all s of one level-2 group.
All inputs are finite; a program needn't handle non-finite values.
Results may differ from a plain program's by a relative error of at most 0.017.
Values may be sent and summed in bfloat16 or wider, within the bound.
No kernel may reach another device: no remote copies, remote signals or barrier semaphores. Data moves between devices by JAX's collectives and lax.ppermute only.
A program may use at most 64 MiB of HBM per device.

v0:
```python
import jax
import jax.numpy as jnp
from jax import lax
from jax.sharding import PartitionSpec as P


def swapped(block, axis, stride):
    count = lax.axis_size(axis)
    route = []
    for low in range(count):
        high = low | 1 << stride
        if high != low and high < count:
            route += [(low, high), (high, low)]
    return lax.ppermute(block, axis, route)


def row_fold(matrix, arrived):
    return jnp.dot(matrix, arrived, preferred_element_type=jnp.float32)


def transposed_product(matrix, rows):
    return lax.dot_general(
        matrix, rows, (((0,), (0,)), ((), ())), preferred_element_type=jnp.float32
    )


def local(
    sources,
    inner_inv,
    coupling,
    boundary_map,
    sep_inv_0,
    sep_inv_1,
    sep_inv_2,
    sep_inv_3,
    sep_couple_0,
    sep_couple_1,
    sep_couple_2,
):
    source_rows = sources[0, 0]
    inverse = inner_inv[0, 0]
    couple = coupling[0, 0]
    targets = boundary_map[0, 0]
    separators = [sep_inv_0[0], sep_inv_1[0], sep_inv_2[0], sep_inv_3[0]]
    parents = [sep_couple_0[0], sep_couple_1[0], sep_couple_2[0]]
    levels = len(separators)
    row_sizes = [matrix.shape[0] for matrix in separators]
    total_rows = sum(row_sizes)
    bit_count = lax.axis_size("sub").bit_length() - 1
    gathered = (
        lax.all_gather(separators[0], "sep", axis=0, tiled=True),
        lax.all_gather(separators[1], "sep", axis=0, tiled=True),
        lax.all_gather(separators[2], "sep", axis=0, tiled=True),
        lax.all_gather(separators[3], "sep", axis=0, tiled=True),
        lax.all_gather(parents[0], "sep", axis=0, tiled=True),
        lax.all_gather(parents[1], "sep", axis=0, tiled=True),
        lax.all_gather(parents[2], "sep", axis=0, tiled=True),
    )
    full_separator = list(gathered[:4])
    full_parent = list(gathered[4:])
    inner_half = jnp.dot(inverse, source_rows, preferred_element_type=jnp.float32).astype(
        jnp.bfloat16
    )
    boundary_half = jnp.dot(couple, inner_half, preferred_element_type=jnp.float32).astype(
        jnp.bfloat16
    )
    slot_ids = lax.broadcasted_iota(jnp.int32, (total_rows, targets.shape[0]), 0)
    onehot = (slot_ids == targets[None, :]).astype(jnp.bfloat16)
    leaf_rows = jnp.dot(onehot, boundary_half, preferred_element_type=jnp.float32)
    direct = lax.dot_general(
        inverse, inner_half, (((0,), (0,)), ((), ())), preferred_element_type=jnp.float32
    )
    forward_rows = []
    carried = leaf_rows
    for height in range(levels):
        for bit_index in range(2 * height, min(2 * height + 2, bit_count)):
            carried = carried + swapped(carried.astype(jnp.bfloat16), "sub", bit_index).astype(
                carried.dtype
            )
        size = row_sizes[height]
        rhs_rows = carried[:size]
        rhs_half = rhs_rows.astype(jnp.bfloat16)
        solve_solved = row_fold(
            separators[height], lax.all_gather(rhs_half, "sep", axis=0, tiled=True)
        )
        solved = solve_solved.astype(jnp.bfloat16)
        forward_rows.append(solved)
        carried = carried[size:]
        if height < levels - 1:
            child_term = row_fold(
                parents[height], lax.all_gather(solved, "sep", axis=0, tiled=True)
            )
            carried = carried.at[: row_sizes[height + 1]].add(child_term)
    backward_rows = [None] * levels
    full_forward = [None] * levels
    for height in range(levels):
        full_forward[height] = lax.all_gather(forward_rows[height], "sep", axis=0, tiled=True)
    full_down = None
    for height in reversed(range(levels)):
        if height == levels - 1:
            full_target = full_forward[height]
        else:
            back_term = transposed_product(full_parent[height], full_down)
            full_target = (full_forward[height].astype(jnp.float32) - back_term).astype(
                jnp.bfloat16
            )
        full_down = transposed_product(full_separator[height], full_target).astype(jnp.bfloat16)
        own_start = lax.axis_index("sep") * row_sizes[height]
        backward_rows[height] = lax.dynamic_slice_in_dim(full_down, own_start, row_sizes[height], 0)
    stacked = jnp.concatenate(backward_rows, axis=0)
    picked = jnp.take(stacked, targets, axis=0)
    lifted = lax.dot_general(
        couple, picked, (((0,), (0,)), ((), ())), preferred_element_type=jnp.float32
    ).astype(jnp.bfloat16)
    correction = lax.dot_general(
        inverse, lifted, (((0,), (0,)), ((), ())), preferred_element_type=jnp.float32
    )
    inner_solution = (direct - correction).astype(jnp.bfloat16)
    return (inner_solution[None, None], stacked[None, None])


def solution(mesh):
    placed = (
        P("sub", "sep", None, None),
        P("sub", "sep", None, None),
        P("sub", "sep", None, None),
        P("sub", "sep", None),
        P("sub", "sep", None),
        P("sub", "sep", None),
        P("sub", "sep", None),
        P("sub", "sep", None),
        P("sub", "sep", None),
        P("sub", "sep", None),
        P("sub", "sep", None),
    )
    return jax.shard_map(
        local,
        mesh=mesh,
        in_specs=placed,
        out_specs=(P("sub", "sep", None, None), P("sub", "sep", None, None)),
        check_vma=False,
    )
```

profile of v0, /device:TPU:0, one launch (start us, length us, event | category | flops | bytes accessed | tf_op | source)
XLA Modules:
  0.0 73.4 jit_solution(4816862553502671255)
XLA Ops:
  0.6 0.0 copy-start
  0.6 0.0 copy-start.15
  0.7 1.2 %copy-done = bf16[1,1,768,768]{3,2,1,0:T(8,128)(2,1)S(1)} copy-done((bf16[1,1,768,768]{3,2,1,0:T(8,128)(2,1)S(1)}, bf16[1,1,768,768]{3,2,1,0:T(8,128)(2,1)}, u32[]{:S(2)}) %copy-start) | copy-done | bytes 1179672
  1.9 1.5 %convolution_convert_fusion.1 = bf16[768,256]{1,0:T(8,128)(2,1)S(1)} fusion(bf16[1,1,768,768]{3,2,1,0:T(8,128)(2,1)S(1)} %copy-done, bf16[1,1,768,256]{3,2,1,0:T(8,128)(2,1)} %param.19), kind=kOutput, calls=%fused_computation.4 | convolution fusion | flops 302186496 | bytes 1966080 | tf_op jit(solution)/shard_map/dot_general | solution.py:61
  3.4 0.0 copy-start.5
  3.4 0.0 copy-start.4
  3.4 0.0 copy-start.9
  3.4 1.4 %fusion.64 = (bf16[480,256]{1,0:T(8,128)(2,1)}, f32[480,256]{1,0:T(8,128)S(1)}) fusion(bf16[768,256]{1,0:T(8,128)(2,1)S(1)} %convolution_convert_fusion.1, bf16[1,1,512,768]{3,2,1,0:T(8,128)(2,1)S(1)} %copy-done.2, s32[512]{0:T(512)S(1)} %bitcast.146), kind=kOutput, calls=%fused_computation.86 | convolution fusion | flops 327655424 | bytes 1918976 | tf_op jit(solution)/shard_map/dot_general | solution.py:69
  4.8 2.9 %collective-permute-start = (bf16[480,256]{1,0:T(8,128)(2,1)}, bf16[480,256]{1,0:T(8,128)(2,1)S(1)}, u32[]{:S(2)}, u32[]{:S(2)}) collective-permute-start(bf16[480,256]{1,0:T(8,128)(2,1)} %get-tuple-element.52), channel_id=1, source_target_pairs={{0,2},{2,0},{4,6},{6,4},{8,10},{10,8},{12,14},{14,12},{16,18},{18,... | collective-permute-start | bytes 737288 | tf_op jit(solution)/shard_map/ppermute | solution.py:14
  7.8 2.0 %all-gather.1 = bf16[1,512,256]{2,1,0:T(8,128)(2,1)S(1)} all-gather(bf16[1,256,256]{2,1,0:T(8,128)(2,1)S(1)} %copy-done.4), channel_id=3, replica_groups=mesh['sub'=16,'sep'=2] {'sep'}, dimensions={1}, use_global_device_ids=true | all-gather | bytes 393216 | tf_op jit(solution)/shard_map/all_gather | solution.py:57
  9.8 3.3 %all-gather.2 = bf16[1,256,256]{2,1,0:T(8,128)(2,1)} all-gather(bf16[1,128,256]{2,1,0:T(8,128)(2,1)} %param.25), channel_id=4, replica_groups=mesh['sub'=16,'sep'=2] {'sep'}, dimensions={1}, use_global_device_ids=true | all-gather | bytes 196608 | tf_op jit(solution)/shard_map/all_gather | solution.py:53
  13.1 2.0 %all-gather.3 = bf16[1,256,128]{2,1,0:T(8,128)(2,1)} all-gather(bf16[1,128,128]{2,1,0:T(8,128)(2,1)S(1)} %copy-done.9), channel_id=5, replica_groups=mesh['sub'=16,'sep'=2] {'sep'}, dimensions={1}, use_global_device_ids=true | all-gather | bytes 98304 | tf_op jit(solution)/shard_map/all_gather | solution.py:56
  15.1 0.7 compare_select_fusion
  15.8 0.0 collective-permute-done
  15.8 0.7 %fusion.25 = bf16[480,256]{1,0:T(8,128)(2,1)} fusion(f32[480,256]{1,0:T(8,128)S(1)} %get-tuple-element.53, bf16[480,256]{1,0:T(8,128)(2,1)S(1)} %collective-permute-done), kind=kLoop, calls=%fused_computation.46 | loop fusion | flops 368640 | bytes 983040 | tf_op jit(solution)/shard_map/convert_element_type | solution.py:77
  16.5 1.5 %collective-permute-start.1 = (bf16[480,256]{1,0:T(8,128)(2,1)}, bf16[480,256]{1,0:T(8,128)(2,1)}, u32[]{:S(2)}, u32[]{:S(2)}) collective-permute-start(bf16[480,256]{1,0:T(8,128)(2,1)} %fusion.25), channel_id=1, source_target_pairs={{0,4},{4,0},{2,6},{6,2},{8,12},{12,8},{10,14},{14,10},{16,20},{20,... | collective-permute-start | bytes 737288 | tf_op jit(solution)/shard_map/ppermute | solution.py:14
  18.0 2.0 %all-gather.4 = bf16[1,128,128]{2,1,0:T(8,128)(2,1)} all-gather(bf16[1,64,128]{2,1,0:T(8,128)(2,1)S(1)} %copy-done.10), channel_id=6, replica_groups=mesh['sub'=16,'sep'=2] {'sep'}, dimensions={1}, use_global_device_ids=true | all-gather | bytes 49152 | tf_op jit(solution)/shard_map/all_gather | solution.py:52
  20.0 0.6 pad_clamp_fusion
  20.6 2.2 %all-gather = bf16[1,512,512]{2,1,0:T(8,128)(2,1)S(1)} all-gather(bf16[1,256,512]{2,1,0:T(8,128)(2,1)S(1)} %copy-done.1), channel_id=2, replica_groups=mesh['sub'=16,'sep'=2] {'sep'}, dimensions={1}, use_global_device_ids=true | all-gather | bytes 786432 | tf_op jit(solution)/shard_map/all_gather | solution.py:54
  22.7 2.3 %collective-permute-done.1 = bf16[480,256]{1,0:T(8,128)(2,1)} collective-permute-done((bf16[480,256]{1,0:T(8,128)(2,1)}, bf16[480,256]{1,0:T(8,128)(2,1)}, u32[]{:S(2)}, u32[]{:S(2)}) %collective-permute-start.1) | collective-permute-done | bytes 245792 | tf_op jit(solution)/shard_map/ppermute | solution.py:14
  25.0 1.0 %convert_add_fusion = f32[480,256]{1,0:T(8,128)S(1)} fusion(bf16[480,256]{1,0:T(8,128)(2,1)} %collective-permute-done.1, f32[480,256]{1,0:T(8,128)S(1)} %get-tuple-element.53, bf16[480,256]{1,0:T(8,128)(2,1)S(1)} %collective-permute-done), kind=kLoop, calls=%fused_computation.40 | loop fusion | flops 491520 | bytes 1474560 | tf_op jit(solution)/shard_map/add | solution.py:77
  26.0 0.0 copy-start.6
  26.1 2.0 %all_gather.48 = bf16[64,256]{1,0:T(8,128)(2,1)S(1)} all-gather(bf16[32,256]{1,0:T(8,128)(2,1)S(1)} %slice.97), channel_id=1, replica_groups=mesh['sub'=16,'sep'=2] {'sep'}, dimensions={0}, use_global_device_ids=true | all-gather | bytes 49152 | tf_op jit(solution)/shard_map/all_gather | solution.py:84
  28.1 0.1 fusion.17
  28.2 1.8 %all_gather.49 = bf16[64,256]{1,0:T(8,128)(2,1)S(1)} all-gather(bf16[32,256]{1,0:T(8,128)(2,1)S(1)} %fusion.17), channel_id=1, replica_groups=mesh['sub'=16,'sep'=2] {'sep'}, dimensions={0}, use_global_device_ids=true | all-gather | bytes 49152 | tf_op jit(solution)/shard_map/all_gather | solution.py:97
  30.0 0.1 fusion.44
  30.2 0.5 copy-done.7
  30.7 0.0 copy-start.16
  30.7 1.6 %collective-permute-start.2 = (bf16[448,256]{1,0:T(8,128)(2,1)S(1)}, bf16[448,256]{1,0:T(8,128)(2,1)S(1)}, u32[]{:S(2)}, u32[]{:S(2)}) collective-permute-start(bf16[448,256]{1,0:T(8,128)(2,1)S(1)} %convert_element_type.117), channel_id=1, source_target_pairs={{0,8},{8,0},{2,10},{10,2},{4,12},{12,4},{6,14},{14,6},{16,24},{24,... | collective-permute-start | bytes 688136 | tf_op jit(solution)/shard_map/ppermute | solution.py:14
  32.3 0.5 fusion.3
  32.8 5.6 %collective-permute-done.2 = bf16[448,256]{1,0:T(8,128)(2,1)S(1)} collective-permute-done((bf16[448,256]{1,0:T(8,128)(2,1)S(1)}, bf16[448,256]{1,0:T(8,128)(2,1)S(1)}, u32[]{:S(2)}, u32[]{:S(2)}) %collective-permute-start.2) | collective-permute-done | bytes 229408 | tf_op jit(solution)/shard_map/ppermute | solution.py:14
  38.4 0.1 fusion.26
  38.5 0.0 copy-start.8
  38.5 2.7 %collective-permute-start.3 = (bf16[448,256]{1,0:T(8,128)(2,1)S(1)}, bf16[448,256]{1,0:T(8,128)(2,1)S(1)}, u32[]{:S(2)}, u32[]{:S(2)}) collective-permute-start(bf16[448,256]{1,0:T(8,128)(2,1)S(1)} %fusion.26), channel_id=1, source_target_pairs={{0,16},{16,0},{2,18},{18,2},{4,20},{20,4},{6,22},{22,6},{8,24},{24... | collective-permute-start | bytes 688136 | tf_op jit(solution)/shard_map/ppermute | solution.py:14
  41.1 1.9 %all-gather.6 = bf16[1,64,64]{2,1,0:T(8,128)(2,1)} all-gather(bf16[1,32,64]{2,1,0:T(8,128)(2,1)S(1)} %copy-done.13), channel_id=8, replica_groups=mesh['sub'=16,'sep'=2] {'sep'}, dimensions={1}, use_global_device_ids=true | all-gather | bytes 12288 | tf_op jit(solution)/shard_map/all_gather | solution.py:51
  43.1 2.0 %all-gather.5 = bf16[1,128,64]{2,1,0:T(8,128)(2,1)} all-gather(bf16[1,64,64]{2,1,0:T(8,128)(2,1)S(1)} %copy-done.11), channel_id=7, replica_groups=mesh['sub'=16,'sep'=2] {'sep'}, dimensions={1}, use_global_device_ids=true | all-gather | bytes 24576 | tf_op jit(solution)/shard_map/all_gather | solution.py:55
  45.0 0.5 compare_and_fusion
  45.5 5.7 %collective-permute-done.3 = bf16[448,256]{1,0:T(8,128)(2,1)S(1)} collective-permute-done((bf16[448,256]{1,0:T(8,128)(2,1)S(1)}, bf16[448,256]{1,0:T(8,128)(2,1)S(1)}, u32[]{:S(2)}, u32[]{:S(2)}) %collective-permute-start.3) | collective-permute-done | bytes 229408 | tf_op jit(solution)/shard_map/ppermute | solution.py:14
  51.2 0.1 convert_add_fusion.2
  51.3 1.9 %all_gather.50 = bf16[128,256]{1,0:T(8,128)(2,1)S(1)} all-gather(bf16[64,256]{1,0:T(8,128)(2,1)S(1)} %slice.96), channel_id=1, replica_groups=mesh['sub'=16,'sep'=2] {'sep'}, dimensions={0}, use_global_device_ids=true | all-gather | bytes 98304 | tf_op jit(solution)/shard_map/all_gather | solution.py:84
  53.2 0.1 fusion.15
  53.3 1.9 %all_gather.51 = bf16[128,256]{1,0:T(8,128)(2,1)S(1)} all-gather(bf16[64,256]{1,0:T(8,128)(2,1)S(1)} %fusion.15), channel_id=1, replica_groups=mesh['sub'=16,'sep'=2] {'sep'}, dimensions={0}, use_global_device_ids=true | all-gather | bytes 98304 | tf_op jit(solution)/shard_map/all_gather | solution.py:97
  55.1 0.1 fusion.36
  55.3 1.9 %all_gather.52 = bf16[256,256]{1,0:T(8,128)(2,1)S(1)} all-gather(bf16[128,256]{1,0:T(8,128)(2,1)S(1)} %fusion.36), channel_id=1, replica_groups=mesh['sub'=16,'sep'=2] {'sep'}, dimensions={0}, use_global_device_ids=true | all-gather | bytes 196608 | tf_op jit(solution)/shard_map/all_gather | solution.py:84
  57.2 0.2 fusion.12
  57.4 1.9 %all_gather.53 = bf16[256,256]{0,1:T(8,128)(2,1)S(1)} all-gather(bf16[128,256]{0,1:T(8,128)(2,1)S(1)} %fusion.12), channel_id=1, replica_groups=mesh['sub'=16,'sep'=2] {'sep'}, dimensions={0}, use_global_device_ids=true | all-gather | bytes 196608 | tf_op jit(solution)/shard_map/all_gather | solution.py:97
  59.3 0.2 fusion.27
  59.5 2.0 %all_gather.54 = bf16[512,256]{1,0:T(8,128)(2,1)S(1)} all-gather(bf16[256,256]{1,0:T(8,128)(2,1)S(1)} %fusion.27), channel_id=1, replica_groups=mesh['sub'=16,'sep'=2] {'sep'}, dimensions={0}, use_global_device_ids=true | all-gather | bytes 393216 | tf_op jit(solution)/shard_map/all_gather | solution.py:84
  61.5 0.3 fusion.9
  61.8 2.0 %all_gather.55 = bf16[512,256]{0,1:T(8,128)(2,1)S(1)} all-gather(bf16[256,256]{0,1:T(8,128)(2,1)S(1)} %fusion.9), channel_id=1, replica_groups=mesh['sub'=16,'sep'=2] {'sep'}, dimensions={0}, use_global_device_ids=true | all-gather | bytes 393216 | tf_op jit(solution)/shard_map/all_gather | solution.py:97
  63.8 0.3 convolution_convert_fusion.2
  64.1 1.3 %convolution_convert_fusion.5 = bf16[256,256]{1,0:T(8,128)(2,1)S(1)} fusion(bf16[256,512]{1,0:T(8,128)(2,1)S(1)} %convolution_convert_fusion.2, bf16[1,512,256]{2,1,0:T(8,128)(2,1)S(1)} %all-gather.1, bf16[256,256]{0,1:T(8,128)(2,1)S(1)} %all_gather.53, bf16[1,256,256]{2,1,0:T(8,128)(2,1)} %all-gather.2), kind=kOutput, calls=%fused_computation.18 | convolution fusion | flops 100925440 | bytes 917504 | tf_op jit(solution)/shard_map/dot_general | solution.py:22
  65.4 1.3 %convolution_convert_fusion.6 = bf16[256,128]{1,0:T(8,128)(2,1)S(1)} fusion(bf16[256,256]{1,0:T(8,128)(2,1)S(1)} %convolution_convert_fusion.5, bf16[128,256]{1,0:T(8,128)(2,1)} %copy-done.3, bf16[1,256,128]{2,1,0:T(8,128)(2,1)} %all-gather.3, bf16[1,128,128]{2,1,0:T(8,128)(2,1)} %all-gather.4), kind=kOutput, calls=%fused_computation.23 | convolution fusion | flops 25296896 | bytes 360448 | tf_op jit(solution)/shard_map/dot_general | solution.py:22
  66.7 1.1 %fusion.16 = bf16[256,64]{0,1:T(8,128)(2,1)S(1)} fusion(bf16[256,128]{1,0:T(8,128)(2,1)S(1)} %convolution_convert_fusion.6, bf16[64,256]{1,0:T(8,128)(2,1)} %copy-done.7, bf16[1,128,64]{2,1,0:T(8,128)(2,1)} %all-gather.5, bf16[1,64,64]{2,1,0:T(8,128)(2,1)S(1)} %copy-done.12), kind=kOutput, calls=%fused_computation.33 | convolution fusion | flops 6340608 | bytes 155648 | tf_op jit(solution)/shard_map/dot_general | solution.py:22
  67.8 0.1 copy.30
  68.0 0.1 dynamic-slice_bitcast_fusion.2
  68.1 0.2 fusion.80
  68.3 0.2 pad_maximum_fusion
  68.5 0.8 %copy.33 = bf16[1,1,480,256]{3,2,1,0:T(8,128)(2,1)} copy(bf16[1,1,480,256]{2,3,1,0:T(8,128)(2,1)S(1)} %fusion.80) | data formatting | bytes 491520
  69.4 0.1 copy.31
  69.5 0.0 copy-start.17
  69.5 2.0 %gather_fusion = bf16[512,256]{1,0:T(8,128)(2,1)S(1)} fusion(bf16[480,256]{1,0:T(8,128)(2,1)S(1)} %copy.31, s32[1024]{0:T(1024)S(1)} %copy-done.14), kind=kCustom, calls=%fused_computation | custom fusion | bytes 526336 | tf_op jit(solution)/shard_map/jit(_take)/gather | solution.py:111
  71.5 1.0 %fusion.1 = bf16[1,1,768,256]{2,3,1,0:T(8,128)(2,1)S(1)} fusion(f32[256,768]{1,0:T(8,128)S(1)} %fusion.3, bf16[1,1,768,768]{3,2,1,0:T(8,128)(2,1)S(1)} %copy-done, bf16[1,1,512,768]{3,2,1,0:T(8,128)(2,1)S(1)} %copy-done.2, bf16[512,256]{1,0:T(8,128)(2,1)S(1)} %gather_fusion, pred[512]{0:T(512)(128)(4,1)S(1)} %copy-done.17), kind=kOutput, calls=%fused_computation.5 | convolution fusion | flops 504037376 | bytes 3408384 | tf_op jit(solution)/shard_map/dot_general | solution.py:115
  72.5 0.9 %copy.32 = bf16[1,1,768,256]{3,2,1,0:T(8,128)(2,1)} copy(bf16[1,1,768,256]{2,3,1,0:T(8,128)(2,1)S(1)} %fusion.1) | data formatting | bytes 786432
  (32 shorter events, 0.2 us)
Async XLA Ops:
  0.6 1.3 %copy-start = (bf16[1,1,768,768]{3,2,1,0:T(8,128)(2,1)S(1)}, bf16[1,1,768,768]{3,2,1,0:T(8,128)(2,1)}, u32[]{:S(2)}) copy-start(bf16[1,1,768,768]{3,2,1,0:T(8,128)(2,1)} %param.20) | copy-start | bytes 3538948
  0.6 2.8 %copy-start.15 = (s32[1,1,512]{2,1,0:T(1,128)S(1)}, s32[1,1,512]{2,1,0:T(1,128)}, u32[]{:S(2)}) copy-start(s32[1,1,512]{2,1,0:T(1,128)} %param.22) | copy-start | bytes 6148
  0.7 2.8 %copy-start.2 = (bf16[1,1,512,768]{3,2,1,0:T(8,128)(2,1)S(1)}, bf16[1,1,512,768]{3,2,1,0:T(8,128)(2,1)}, u32[]{:S(2)}) copy-start(bf16[1,1,512,768]{3,2,1,0:T(8,128)(2,1)} %param.21) | copy-start | bytes 2359300
  3.4 1.4 %copy-start.5 = (bf16[768,256]{1,0:T(8,128)(2,1)}, bf16[768,256]{1,0:T(8,128)(2,1)S(1)}, u32[]{:S(2)}) copy-start(bf16[768,256]{1,0:T(8,128)(2,1)S(1)} %convolution_convert_fusion.1) | copy-start | bytes 1179652
  3.4 4.4 %copy-start.4 = (bf16[1,256,256]{2,1,0:T(8,128)(2,1)S(1)}, bf16[1,256,256]{2,1,0:T(8,128)(2,1)}, u32[]{:S(2)}) copy-start(bf16[1,256,256]{2,1,0:T(8,128)(2,1)} %param.29) | copy-start | bytes 393220
  3.4 9.7 %copy-start.9 = (bf16[1,128,128]{2,1,0:T(8,128)(2,1)S(1)}, bf16[1,128,128]{2,1,0:T(8,128)(2,1)}, u32[]{:S(2)}) copy-start(bf16[1,128,128]{2,1,0:T(8,128)(2,1)} %param.28) | copy-start | bytes 98308
  4.8 13.2 %copy-start.10 = (bf16[1,64,128]{2,1,0:T(8,128)(2,1)S(1)}, bf16[1,64,128]{2,1,0:T(8,128)(2,1)}, u32[]{:S(2)}) copy-start(bf16[1,64,128]{2,1,0:T(8,128)(2,1)} %param.24) | copy-start | bytes 49156
  4.8 15.7 %copy-start.1 = (bf16[1,256,512]{2,1,0:T(8,128)(2,1)S(1)}, bf16[1,256,512]{2,1,0:T(8,128)(2,1)}, u32[]{:S(2)}) copy-start(bf16[1,256,512]{2,1,0:T(8,128)(2,1)} %param.26) | copy-start | bytes 786436
  4.8 10.9 %collective-permute-start = (bf16[480,256]{1,0:T(8,128)(2,1)}, bf16[480,256]{1,0:T(8,128)(2,1)S(1)}, u32[]{:S(2)}, u32[]{:S(2)}) collective-permute-start(bf16[480,256]{1,0:T(8,128)(2,1)} %get-tuple-element.52), channel_id=1, source_target_pairs={{0,2},{2,0},{4,6},{6,4},{8,10},{10,8},{12,14},{14,12},{16,18},{18,... | collective-permute-start | bytes 737288 | tf_op jit(solution)/shard_map/ppermute | solution.py:14
  16.5 8.5 %collective-permute-start.1 = (bf16[480,256]{1,0:T(8,128)(2,1)}, bf16[480,256]{1,0:T(8,128)(2,1)}, u32[]{:S(2)}, u32[]{:S(2)}) collective-permute-start(bf16[480,256]{1,0:T(8,128)(2,1)} %fusion.25), channel_id=1, source_target_pairs={{0,4},{4,0},{2,6},{6,2},{8,12},{12,8},{10,14},{14,10},{16,20},{20,... | collective-permute-start | bytes 737288 | tf_op jit(solution)/shard_map/ppermute | solution.py:14
  22.7 5.3 %copy-start.13 = (bf16[1,32,64]{2,1,0:T(8,128)(2,1)S(1)}, bf16[1,32,64]{2,1,0:T(8,128)(2,1)}, u32[]{:S(2)}) copy-start(bf16[1,32,64]{2,1,0:T(8,128)(2,1)} %param.23) | copy-start | bytes 12292
  22.7 7.3 %copy-start.11 = (bf16[1,64,64]{2,1,0:T(8,128)(2,1)S(1)}, bf16[1,64,64]{2,1,0:T(8,128)(2,1)}, u32[]{:S(2)}) copy-start(bf16[1,64,64]{2,1,0:T(8,128)(2,1)} %param.27) | copy-start | bytes 24580
  26.0 6.3 %copy-start.6 = (bf16[768,256]{1,0:T(8,128)(2,1)S(1)}, bf16[768,256]{1,0:T(8,128)(2,1)}, u32[]{:S(2)}) copy-start(bf16[768,256]{1,0:T(8,128)(2,1)} %copy-done.5) | copy-start | bytes 1179652
  30.0 0.6 copy-start.7
  30.7 14.4 %copy-start.16 = (s32[1,1,512]{2,1,0:T(1,128)S(1)}, s32[1,1,512]{2,1,0:T(1,128)}, u32[]{:S(2)}) copy-start(s32[1,1,512]{2,1,0:T(1,128)} %param.22) | copy-start | bytes 6148
  30.7 7.7 %collective-permute-start.2 = (bf16[448,256]{1,0:T(8,128)(2,1)S(1)}, bf16[448,256]{1,0:T(8,128)(2,1)S(1)}, u32[]{:S(2)}, u32[]{:S(2)}) collective-permute-start(bf16[448,256]{1,0:T(8,128)(2,1)S(1)} %convert_element_type.117), channel_id=1, source_target_pairs={{0,8},{8,0},{2,10},{10,2},{4,12},{12,4},{6,14},{14,6},{16,24},{24,... | collective-permute-start | bytes 688136 | tf_op jit(solution)/shard_map/ppermute | solution.py:14
  38.5 18.7 %copy-start.8 = (bf16[1,128,256]{2,1,0:T(8,128)(2,1)S(1)}, bf16[1,128,256]{2,1,0:T(8,128)(2,1)}, u32[]{:S(2)}) copy-start(bf16[1,128,256]{2,1,0:T(8,128)(2,1)} %param.25) | copy-start | bytes 196612
  38.5 12.7 %collective-permute-start.3 = (bf16[448,256]{1,0:T(8,128)(2,1)S(1)}, bf16[448,256]{1,0:T(8,128)(2,1)S(1)}, u32[]{:S(2)}, u32[]{:S(2)}) collective-permute-start(bf16[448,256]{1,0:T(8,128)(2,1)S(1)} %fusion.26), channel_id=1, source_target_pairs={{0,16},{16,0},{2,18},{18,2},{4,20},{20,4},{6,22},{22,6},{8,24},{24... | collective-permute-start | bytes 688136 | tf_op jit(solution)/shard_map/ppermute | solution.py:14
  55.1 6.4 %copy-start.3 = (bf16[128,256]{1,0:T(8,128)(2,1)}, bf16[128,256]{1,0:T(8,128)(2,1)S(1)}, u32[]{:S(2)}) copy-start(bf16[128,256]{1,0:T(8,128)(2,1)S(1)} %all_gather.51) | copy-start | bytes 196612
  63.8 2.9 %copy-start.12 = (bf16[1,64,64]{2,1,0:T(8,128)(2,1)S(1)}, bf16[1,64,64]{2,1,0:T(8,128)(2,1)}, u32[]{:S(2)}) copy-start(bf16[1,64,64]{2,1,0:T(8,128)(2,1)} %all-gather.6) | copy-start | bytes 24580
  68.1 1.4 %copy-start.14 = (s32[1024]{0:T(1024)S(1)}, s32[1024]{0:T(1024)}, u32[]{:S(2)}) copy-start(s32[1024]{0:T(1024)} %pad_clamp_fusion) | copy-start | bytes 12292
  69.5 2.0 %copy-start.17 = (pred[512]{0:T(512)(128)(4,1)S(1)}, pred[512]{0:T(512)(128)(4,1)}, u32[]{:S(2)}) copy-start(pred[512]{0:T(512)(128)(4,1)} %compare_and_fusion) | copy-start | bytes 1540
where the time goes:
time: 73.9 us; the launch traced here: 73.4 us
  blocking collectives  30.6 us (41%)
  waiting for transfers between devices  13.5 us (18%)
  matrix products  9.52 us (13%)
  starting transfers between devices  8.75 us (12%)
  local copies, waits for them, and re-layouts  5.94 us (8%)
  other arithmetic  4.08 us (6%)
  between operations  0.96 us (1%)
    ppermute x4, waiting for transfers between devices, swapped(): return lax.ppermute(block, axis, route)  13.5 us
    ppermute x4, starting transfers between devices, swapped(): return lax.ppermute(block, axis, route)  8.75 us
    all_gather x4, blocking collectives, local(): lax.all_gather(rhs_half, 'sep', axis=0, tiled=True)  7.71 us
    all_gather x4, blocking collectives, local(): lax.all_gather(forward_rows[height], 'sep', axis=0, tiled=True)  7.57 us
    dot_general x4, matrix products, transposed_product(): lax.dot_general(matrix, rows, (((0,), (0,)), ((), ())), preferred_element...  3.96 us
    unnamed x38, local copies, waits for them, and re-layouts  3.56 us
    all_gather x1, blocking collectives, local(): lax.all_gather(separators[2], 'sep', axis=0, tiled=True)  3.34 us
    all_gather x1, blocking collectives, local(): lax.all_gather(separators[3], 'sep', axis=0, tiled=True)  2.17 us
  transfers between devices with their start and end apart: 4, of which 3 were waited for; matrix products, arithmetic and copies ran while one was open for 3% of the time, Pallas kernels for 0%

commit v1 on v0

v1 whole, which is shorter than its diff:
```python
import jax
import jax.numpy as jnp
from jax import lax
from jax.experimental import pallas as pl
from jax.experimental.pallas import tpu as pltpu
from jax.sharding import PartitionSpec as P

BLOCK = 256
CHIPS = 4
MIB = 1024 * 1024
VMEM = pl.BlockSpec(memory_space=pltpu.VMEM)
SMEM = pl.BlockSpec(memory_space=pltpu.SMEM)
HBM = pl.BlockSpec(memory_space=pltpu.HBM)


def bf16(x):
    return x.astype(jnp.bfloat16)


def dot(a, b):
    return jnp.dot(a, b, preferred_element_type=jnp.float32)


def dot_tn(a, b):
    return lax.dot_general(a, b, (((0,), (0,)), ((), ())), preferred_element_type=jnp.float32)


def call(kernel, name, outs, ins, specs, out_specs, flops, limit=16, scratch=()):
    ins = [pltpu.with_memory_space_constraint(x, pltpu.HBM) if s is HBM else x for x, s in zip(ins, specs)]
    moved = sum(x.size * x.dtype.itemsize for x in ins)
    return pl.pallas_call(
        kernel,
        out_shape=outs,
        in_specs=specs,
        out_specs=out_specs,
        scratch_shapes=list(scratch),
        compiler_params=pltpu.CompilerParams(vmem_limit_bytes=limit * MIB),
        cost_estimate=pl.CostEstimate(flops=flops, bytes_accessed=moved, transcendentals=0),
        name=name,
    )(*ins)


def struct(shape, dtype=jnp.bfloat16):
    return jax.ShapeDtypeStruct(shape, dtype)


def offsets(sizes):
    return [sum(sizes[:i]) for i in range(len(sizes))]


def places(sizes):
    return [sum(sizes[i + 1 :]) for i in range(len(sizes))]


def scatter_matrix(tgt, sizes):
    moved = tgt
    for start, place, size in zip(offsets(sizes), places(sizes), sizes):
        inside = (tgt >= start) & (tgt < start + size)
        moved = jnp.where(inside, tgt + (place - start), moved)
    slots = lax.broadcasted_iota(jnp.int32, (sum(sizes), tgt.shape[1]), 0)
    return bf16(jnp.where(slots == moved, 1.0, 0.0))


def leaf_forward(src, inv, cpl, tgt, separators, parents):
    inner, shots = src.shape
    count = inner // BLOCK
    sizes = [m.shape[0] for m in separators]
    s0, s1, s2, s3 = sizes
    o0, o1, o2, o3 = [m.shape[1] for m in separators]

    def kernel(src_hbm, inv_hbm, cpl_hbm, tgt_hbm, i0, i1, i2, i3, c0, c1, c2,
               half_ref, rows_ref, pack_ref, src, inv, cpl, edge_ref, small0, small1, tgt_ref, sems):
        copies = []
        for i in range(count):
            rows = pl.ds(i * BLOCK, BLOCK)
            cols = pl.ds(0, (i + 1) * BLOCK)
            group = [
                pltpu.make_async_copy(src_hbm.at[rows], src.at[rows], sems.at[3 * i]),
                pltpu.make_async_copy(inv_hbm.at[rows, cols], inv.at[rows, cols], sems.at[3 * i + 1]),
                pltpu.make_async_copy(cpl_hbm.at[:, rows], cpl.at[:, rows], sems.at[3 * i + 2]),
            ]
            for copy in group:
                copy.start()
            copies.append(group)
        base = 3 * count
        packs = [
            (i3, pack_ref.at[pl.ds(0, s3), :]),
            (c2, pack_ref.at[pl.ds(s3, s3), pl.ds(0, o2)]),
            (i2, pack_ref.at[pl.ds(s3, s2), pl.ds(o2, o2)]),
            (c1, pack_ref.at[pl.ds(s3 + s2, s2), pl.ds(o2, o1)]),
            (i1, pack_ref.at[pl.ds(s3 + s2, s1), pl.ds(o2 + o1, o1)]),
        ]
        packs += [(i0, small0), (c0, small1), (tgt_hbm, tgt_ref)]
        packs = [pltpu.make_async_copy(a, b, sems.at[base + i]) for i, (a, b) in enumerate(packs)]
        for copy in reversed(packs):
            copy.start()
        for copy in packs[-3:]:
            copy.wait()
        pack_ref[pl.ds(2 * s3, s0), pl.ds(0, o0)] = small0[...]
        pack_ref[pl.ds(s3 + s2 + s1, s1), pl.ds(o2 + o1, o0)] = small1[...]
        onehot = scatter_matrix(tgt_ref[...], sizes)
        for i in range(count):
            rows = pl.ds(i * BLOCK, BLOCK)
            cols = pl.ds(0, (i + 1) * BLOCK)
            copies[i][0].wait()
            copies[i][1].wait()
            half = bf16(dot(inv[rows, cols], src[cols, :]))
            half_ref[rows, :] = half
            copies[i][2].wait()
            term = dot(cpl[:, rows], half)
            if i == 0:
                edge_ref[...] = term
            else:
                edge_ref[...] += term
        rows_ref[...] = bf16(dot(onehot, bf16(edge_ref[...])))
        for copy in packs[:-3]:
            copy.wait()

    return call(
        kernel,
        "leaf_forward",
        (
            struct((inner, shots)),
            struct((sum(sizes), shots)),
            struct((2 * s3 + s0, o3)),
        ),
        (src, inv, cpl, tgt, *separators, *parents),
        [HBM] * 11,
        (VMEM, VMEM, VMEM),
        600_000_000,
        scratch=[
            pltpu.VMEM(src.shape, jnp.bfloat16),
            pltpu.VMEM(inv.shape, jnp.bfloat16),
            pltpu.VMEM(cpl.shape, jnp.bfloat16),
            pltpu.VMEM((cpl.shape[0], shots), jnp.float32),
            pltpu.VMEM((s0, o0), jnp.bfloat16),
            pltpu.VMEM((s1, o0), jnp.bfloat16),
            pltpu.VMEM(tgt.shape, jnp.int32),
            pltpu.SemaphoreType.DMA((3 * count + 8,)),
        ],
    )


def ordered(first, own, other):
    return jnp.concatenate([jnp.where(first, own, other), jnp.where(first, other, own)], 0)


def shares(sizes):
    s0, s1, s2, s3 = sizes
    return (s3 + s2 + 2 * s1) // CHIPS, s0 // 2


def fold_lowest(where, rows, small, far_small, sizes):
    s0, s1, s2, s3 = sizes
    main, side = shares(sizes)
    total = sum(sizes)

    def kernel(where_ref, rows_ref, inv_ref, cpl_ref, far_inv_ref, far_cpl_ref, *outs):
        out_refs, buf = outs[:CHIPS], outs[CHIPS]
        first = where_ref[0] == 0
        inv = ordered(first, inv_ref[...], far_inv_ref[...])
        lowest = rows_ref[pl.ds(total - s0, s0), :]
        up = bf16(dot(inv, ordered(first, lowest, jnp.zeros_like(lowest))))
        own = rows_ref[pl.ds(s3 + s2, s1), :].astype(jnp.float32) + dot(cpl_ref[...], up)
        far = dot(far_cpl_ref[...], up)
        folded = [rows_ref[pl.ds(0, s3 + s2), :], bf16(own), bf16(far)]
        folded = jnp.concatenate(folded, 0)
        for q in range(CHIPS):
            buf[q, pl.ds(0, main), :] = folded[q * main : (q + 1) * main]
            if q < 2:
                buf[q, pl.ds(main, side), :] = lowest[q * side : (q + 1) * side]
            else:
                buf[q, pl.ds(main, side), :] = jnp.zeros((side, rows.shape[1]), jnp.bfloat16)
        for k in range(CHIPS):
            out_refs[k][...] = buf[where_ref[1] ^ k]

    share = struct((main + side, rows.shape[1]))
    return call(
        kernel,
        "fold_lowest",
        (share,) * CHIPS,
        (where, rows, *small, *far_small),
        [SMEM] + [VMEM] * 5,
        (VMEM,) * CHIPS,
        10_000_000,
        limit=4,
        scratch=[pltpu.VMEM((CHIPS, main + side, rows.shape[1]), jnp.bfloat16)],
    )


def solve_operator(strip, pack, far_pack, separators, parents):
    s = [m.shape[0] for m in separators]
    o = [m.shape[1] for m in separators]
    total = sum(s)

    def kernel(strip_ref, own_ref, far_ref, out_ref):
        first = strip_ref[0] == 0

        def whole(row, rows, col, cols):
            at = (pl.ds(row, rows), pl.ds(col, cols))
            return ordered(first, own_ref[at], far_ref[at])

        x3 = whole(0, s[3], 0, o[3])
        c2 = whole(s[3], s[3], 0, o[2])
        x2 = whole(s[3], s[2], o[2], o[2])
        c1 = whole(s[3] + s[2], s[2], o[2], o[1])
        x1 = whole(s[3] + s[2], s[1], o[2] + o[1], o[1])
        c0 = whole(s[3] + s[2] + s[1], s[1], o[2] + o[1], o[0])
        x0 = whole(2 * s[3], s[0], 0, o[0])
        t3 = bf16(dot(x3, c2))
        t2 = bf16(dot(x2, c1))
        t1 = bf16(dot(x1, c0))
        n32 = bf16(dot(t3, x2))
        n21 = bf16(dot(t2, x1))
        n10 = bf16(dot(t1, x0))
        n31 = bf16(dot(t3, n21))
        n20 = bf16(dot(t2, n10))
        n30 = bf16(dot(t3, n20))

        def turned(x, sign):
            y = x.astype(jnp.float32).T
            half = y.shape[0] // 2
            return bf16(sign * jnp.where(first, y[:half], y[half:]))

        m3 = jnp.concatenate([turned(x3, 1.0), turned(n32, -1.0), turned(n31, 1.0), turned(n30, -1.0)], 0)
        m2 = jnp.concatenate([turned(x2, 1.0), turned(n21, -1.0), turned(n20, 1.0)], 0)
        m1 = jnp.concatenate([turned(x1, 1.0), turned(n10, -1.0)], 0)
        m0 = turned(x0, 1.0)
        top, mid, low = s[3], s[3] + s[2], s[3] + s[2] + s[1]
        a, b, c = o[3], o[3] + o[2], o[3] + o[2] + o[1]
        out_ref[:, pl.ds(0, a)] = bf16(dot(m3, x3))
        second = dot(m3, n32)
        out_ref[pl.ds(0, top), pl.ds(a, o[2])] = bf16(second[:top])
        out_ref[pl.ds(top, total - top), pl.ds(a, o[2])] = bf16(second[top:] + dot(m2, x2))
        third = dot(m3, n31)
        out_ref[pl.ds(0, top), pl.ds(b, o[1])] = bf16(third[:top])
        rest = third[top:] + dot(m2, n21)
        out_ref[pl.ds(top, s[2]), pl.ds(b, o[1])] = bf16(rest[: s[2]])
        out_ref[pl.ds(mid, total - mid), pl.ds(b, o[1])] = bf16(rest[s[2] :] + dot(m1, x1))
        out_ref[pl.ds(0, low), pl.ds(c, o[0])] = jnp.zeros((low, o[0]), jnp.bfloat16)
        out_ref[pl.ds(low, s[0]), pl.ds(c, o[0])] = bf16(dot(m0, x0))

    return call(
        kernel,
        "solve_operator",
        struct((total, sum(o))),
        (strip, pack, far_pack),
        [SMEM, VMEM, VMEM],
        VMEM,
        1_000_000_000,
    )


def leaf_backward(inv, cpl, tgt, half, sizes):
    inner, shots = half.shape
    count = inner // BLOCK
    total = sum(sizes)

    def kernel(inv_ref, cpl_ref, tgt_ref, half_ref, direct_ref, lift_ref, reach_ref):
        onehot = scatter_matrix(tgt_ref[...], sizes)
        for i in range(count):
            cols = pl.ds(i * BLOCK, BLOCK)
            reach_ref[:, cols] = bf16(dot(onehot, cpl_ref[:, cols]))
        for j in range(count):
            rows = pl.ds(j * BLOCK, inner - j * BLOCK)
            cols = pl.ds(j * BLOCK, BLOCK)
            block = inv_ref[rows, cols]
            direct_ref[cols, :] = dot_tn(block, half_ref[rows, :])
            lift_ref[cols, :] = bf16(dot(reach_ref[:, rows], block).T)

    return call(
        kernel,
        "leaf_backward",
        (struct((inner, shots), jnp.float32), struct((inner, total))),
        (inv, cpl, tgt, half),
        [VMEM] * 4,
        (VMEM, VMEM),
        1_000_000_000,
        scratch=[pltpu.VMEM((total, inner), jnp.bfloat16)],
    )


def finish(where, shared, far_shared, solve, lift, direct, sizes):
    s0, s1, s2, s3 = sizes
    main, side = shares(sizes)
    each = main + side
    total = sum(sizes)
    shots = shared.shape[1]

    def kernel(where_ref, own_ref, far_ref, solve_ref, lift_ref, direct_ref, inner_ref, sep_ref, own_buf, far_buf, rhs):
        first = where_ref[0] == 0
        for k in range(CHIPS):
            q = where_ref[1] ^ k
            own_buf[q] = own_ref[pl.ds(k * each, each), :]
            far_buf[q] = far_ref[pl.ds(k * each, each), :]

        def put(at, span, own, far):
            size = own.shape[0]
            rhs[pl.ds(at, size), :] = jnp.where(first, own, far)
            rhs[pl.ds(at + span, size), :] = jnp.where(first, far, own)

        def pieces(start, size):
            while size > 0:
                q, low = divmod(start, main)
                count = min(size, main - low)
                yield q, low, count
                start, size = start + count, size - count

        start = at = 0
        for span in (s3, s2):
            for q, low, count in pieces(start, span):
                put(at, span, own_buf[q, pl.ds(low, count), :], far_buf[q, pl.ds(low, count), :])
                at += count
            at += span
            start += span
        for (q, low, count), (q2, low2, _) in zip(pieces(start, s1), pieces(start + s1, s1)):
            own, far = [b[q, pl.ds(low, count), :].astype(jnp.float32) for b in (own_buf, far_buf)]
            own2, far2 = [b[q2, pl.ds(low2, count), :].astype(jnp.float32) for b in (own_buf, far_buf)]
            put(at, s1, bf16(own + far2), bf16(far + own2))
            at += count
        at += s1
        for q in range(2):
            put(at, s0, own_buf[q, pl.ds(main, side), :], far_buf[q, pl.ds(main, side), :])
            at += side
        down = bf16(dot(solve_ref[...], rhs[...]))
        for begin, place, size in zip(offsets(sizes), places(sizes), sizes):
            sep_ref[pl.ds(begin, size), :] = down[place : place + size]
        inner_ref[...] = bf16(direct_ref[...] - dot(lift_ref[...], down))

    return call(
        kernel,
        "finish",
        (struct(direct.shape), struct((total, shots))),
        (where, shared, far_shared, solve, lift, direct),
        [SMEM] + [VMEM] * 5,
        (VMEM, VMEM),
        500_000_000,
        scratch=[
            pltpu.VMEM((CHIPS, each, shots), jnp.bfloat16),
            pltpu.VMEM((CHIPS, each, shots), jnp.bfloat16),
            pltpu.VMEM((2 * total, shots), jnp.bfloat16),
        ],
    )


def other_strip(x):
    return lax.ppermute(x, "sep", [(0, 1), (1, 0)])


def partner(x, mask):
    return lax.ppermute(x, "sub", [(s, s ^ mask) for s in range(lax.axis_size("sub"))])


def added(*terms):
    return bf16(sum(t.astype(jnp.float32) for t in terms))


def local(sources, inner_inv, coupling, boundary_map, *blocks):
    src, inv, cpl, tgt = sources[0, 0], inner_inv[0, 0], coupling[0, 0], boundary_map[0]
    separators = [m[0] for m in blocks[:4]]
    parents = [m[0] for m in blocks[4:]]
    sizes = [m.shape[0] for m in separators]
    main, _ = shares(sizes)
    sub = lax.axis_index("sub")
    where = jnp.stack([lax.axis_index("sep"), lax.rem(sub, CHIPS)]).astype(jnp.int32)
    small = (separators[0], parents[0])
    far_small = tuple(other_strip(m) for m in small)
    half, rows, pack = leaf_forward(src, inv, cpl, tgt, separators, parents)
    parts = fold_lowest(where, rows, small, far_small, sizes)
    share = added(parts[0], *[partner(parts[k], k) for k in range(1, CHIPS)])
    direct, lift = leaf_backward(inv, cpl, tgt, half, sizes)
    far_pack = other_strip(pack)
    solve = solve_operator(where, pack, far_pack, separators, parents)
    top = share[:main]
    along = [partner(top, CHIPS * k) for k in range(1, CHIPS)]
    along, direct, lift, solve = lax.optimization_barrier((along, direct, lift, solve))
    share = jnp.concatenate([added(top, *along), share[main:]], 0)
    shared = jnp.concatenate([share] + [partner(share, k) for k in range(1, CHIPS)], 0)
    inner, sep = finish(where, shared, other_strip(shared), solve, lift, direct, sizes)
    return (inner[None, None], sep[None, None])


def local_any(sources, inner_inv, coupling, boundary_map, *blocks):
    src, inv, cpl, tgt = sources[0, 0], inner_inv[0, 0], coupling[0, 0], boundary_map[0, 0]
    separators = [m[0] for m in blocks[:4]]
    parents = [m[0] for m in blocks[4:]]
    sizes = [m.shape[0] for m in separators]
    levels = len(sizes)
    bits = lax.axis_size("sub").bit_length() - 1

    def both(x):
        return lax.all_gather(x, "sep", axis=0, tiled=True)

    half = bf16(dot(inv, src))
    edge = bf16(dot(cpl, half))
    slots = lax.broadcasted_iota(jnp.int32, (sum(sizes), tgt.shape[0]), 0)
    carried = dot(bf16(slots == tgt[None, :]), edge)
    ups = []
    for level, size in enumerate(sizes):
        for bit in range(2 * level, min(2 * level + 2, bits)):
            sent = partner(bf16(carried), 1 << bit)
            carried = carried + sent.astype(jnp.float32)
        up = both(bf16(dot(separators[level], both(bf16(carried[:size])))))
        ups.append(up)
        carried = carried[size:]
        if level < levels - 1:
            carried = carried.at[: sizes[level + 1]].add(dot(parents[level], up))
    own, down = [None] * levels, None
    for level in reversed(range(levels)):
        target = ups[level]
        if down is not None:
            target = bf16(target.astype(jnp.float32) - dot_tn(both(parents[level]), down))
        down = bf16(dot_tn(both(separators[level]), target))
        own[level] = lax.dynamic_slice_in_dim(down, lax.axis_index("sep") * sizes[level], sizes[level], 0)
    sep = jnp.concatenate(own, 0)
    lifted = bf16(dot_tn(cpl, jnp.take(sep, tgt, axis=0)))
    inner = bf16(dot_tn(inv, half) - dot_tn(inv, lifted))
    return (inner[None, None], sep[None, None])


def solution(mesh):
    whole = P("sub", "sep", None, None)
    placed = (whole,) * 2 + (whole, P("sub", "sep", None)) + (P("sub", "sep", None),) * 7
    two_stages = mesh.shape["sub"] == CHIPS * CHIPS
    return jax.shard_map(
        local if two_stages else local_any,
        mesh=mesh,
        in_specs=placed,
        out_specs=(whole, whole),
        check_vma=False,
    )
```

time: 73.9 us -> 38.9 us (0.53)
  blocking collectives: 30.6 us -> 0 us
  Pallas kernels: 0 us -> 10.2 us
  matrix products: 9.52 us -> 0 us
  starting transfers between devices: 8.75 us -> 13.5 us
  local copies, waits for them, and re-layouts: 5.94 us -> 1.78 us
  other arithmetic: 4.08 us -> 0.16 us
  waiting for transfers between devices: 13.5 us -> 12.3 us
    all_gather x15 -> x0, blocking collectives: 30.6 us -> none  [the longest x4 7.71 us: local(): lax.all_gather(rhs_half, 'sep', axis=0, tiled=True)]
    pallas_call x0 -> x5, Pallas kernels: none -> 10.2 us  [call(): pl.pallas_call(kernel, out_shape=outs, in_specs=specs, out_specs=out_spec...]
    dot_general x15 -> x0, matrix products: 9.52 us -> none  [the longest x4 3.96 us: transposed_product(): lax.dot_general(matrix, rows, (((0,), (0,)), ((), ())), preferred_element...]
    ppermute x4 -> x13, starting transfers between devices: 8.75 us -> 13.5 us  [the longest x9 12.5 us: partner(): lax.ppermute(x, 'sub', [(s, s ^ mask) for s in range(lax.axis_size('sub'))])]
    gather x1 -> x0, local copies, waits for them, and re-layouts: 1.95 us -> none  [local(): picked = jnp.take(stacked, targets, axis=0)]
    unnamed x38 -> x16, local copies, waits for them, and re-layouts: 3.56 us -> 1.76 us
    ppermute x4 -> x13, waiting for transfers between devices: 13.5 us -> 12.3 us  [the longest x9 9.74 us: partner(): lax.ppermute(x, 'sub', [(s, s ^ mask) for s in range(lax.axis_size('sub'))])]
    add x2 -> x0, other arithmetic: 1.07 us -> none  [local(): carried + swapped(carried.astype(jnp.bfloat16), 'sub', bit_index).astype(...]
  transfers between devices with their start and end apart: 4 -> 13, of which waited for: 3 -> 9; matrix products, arithmetic and copies ran while one was open for 3% -> 0% of each run, Pallas kernels for 0% -> 11%
where the time goes in v1:
time: 38.9 us; the launch traced here: 38.8 us
  starting transfers between devices  13.5 us (35%)
  waiting for transfers between devices  12.3 us (32%)
  Pallas kernels  10.2 us (26%)
  local copies, waits for them, and re-layouts  1.78 us (5%)
  between operations  0.79 us (2%)
    ppermute x9, starting transfers between devices, partner(): lax.ppermute(x, 'sub', [(s, s ^ mask) for s in range(lax.axis_size('sub'))])  12.5 us
    pallas_call x5, Pallas kernels, call(): pl.pallas_call(kernel, out_shape=outs, in_specs=specs, out_specs=out_spec...  10.2 us
    ppermute x9, waiting for transfers between devices, partner(): lax.ppermute(x, 'sub', [(s, s ^ mask) for s in range(lax.axis_size('sub'))])  9.74 us
    ppermute x4, waiting for transfers between devices, other_strip(): return lax.ppermute(x, 'sep', [(0, 1), (1, 0)])  2.6 us
    unnamed x16, local copies, waits for them, and re-layouts  1.76 us
    ppermute x4, starting transfers between devices, other_strip(): return lax.ppermute(x, 'sep', [(0, 1), (1, 0)])  1.03 us
  transfers between devices with their start and end apart: 13, of which 9 were waited for; matrix products, arithmetic and copies ran while one was open for 0% of the time, Pallas kernels for 11%

profile of v1, /device:TPU:0, one launch (start us, length us, event | category | flops | bytes accessed | tf_op | source)
XLA Modules:
  0.0 38.8 jit_solution(9728897071844071488)
XLA Ops:
  0.6 0.0 copy-start.3
  0.6 0.0 copy-start.2
  0.7 0.0 copy-start
  0.7 0.0 copy-start.1
  0.7 0.0 copy-start.4
  0.7 3.5 %leaf_forward.1 = (bf16[768,256]{1,0:T(8,128)(2,1)S(1)}, bf16[480,256]{1,0:T(8,128)(2,1)S(1)}, bf16[544,512]{1,0:T(8,128)(2,1)S(1)}) custom-call(bf16[768,256]{1,0:T(8,128)(2,1)} %bitcast.27, bf16[768,768]{1,0:T(8,128)(2,1)} %bitcast.15, bf16[512,768]{1,0:T(8,128)(2,1)} %bitcast.17, s32[1,512]{1,0:T(1,128)} %bitcast.25, bf16[32,64]{1,0:T(8,128)(2,1)} %bitcast.22, ...), custom_call_target="tpu_custom_call" | custom-call | flops 600000000 | bytes 2881536 | tf_op jit(solution)/shard_map/leaf_forward/pallas_call | solution.py:31
  4.2 0.0 copy-start.5
  4.2 0.7 %copy-done.5 = bf16[768,256]{1,0:T(8,128)(2,1)} copy-done((bf16[768,256]{1,0:T(8,128)(2,1)}, bf16[768,256]{1,0:T(8,128)(2,1)S(1)}, u32[]{:S(2)}) %copy-start.5) | copy-done | bytes 393240
  5.0 0.5 %collective-permute-start.8 = (bf16[544,512]{1,0:T(8,128)(2,1)S(1)}, bf16[544,512]{1,0:T(8,128)(2,1)S(1)}, u32[]{:S(2)}, u32[]{:S(2)}) collective-permute-start(bf16[544,512]{1,0:T(8,128)(2,1)S(1)} %get-tuple-element.27.own_ref), channel_id=1, source_target_pairs={{0,1},{1,0},{2,3},{3,2},{4,5},{5,4},{6,7},{7,6},{8,9},{9,8},{10,11... | collective-permute-start | bytes 1671176 | tf_op jit(solution)/shard_map/ppermute | solution.py:347
  5.4 0.0 copy-done.3
  5.4 0.1 collective-permute-start
  5.5 0.0 copy-done.2
  5.5 0.5 %collective-permute-start.1 = (bf16[64,64]{1,0:T(8,128)(2,1)S(1)}, bf16[64,64]{1,0:T(8,128)(2,1)S(1)}, u32[]{:S(2)}, u32[]{:S(2)}) collective-permute-start(bf16[64,64]{1,0:T(8,128)(2,1)S(1)} %bitcast.20), channel_id=1, source_target_pairs={{0,1},{1,0},{2,3},{3,2},{4,5},{5,4},{6,7},{7,6},{8,9},{9,8},{10,11... | collective-permute-start | bytes 24584 | tf_op jit(solution)/shard_map/ppermute | solution.py:347
  5.9 0.1 pad_add_fusion.where_ref.strip_ref
  6.0 1.0 %collective-permute-done.far_inv_ref = bf16[32,64]{1,0:T(8,128)(2,1)S(1)} collective-permute-done((bf16[32,64]{1,0:T(8,128)(2,1)S(1)}, bf16[32,64]{1,0:T(8,128)(2,1)S(1)}, u32[]{:S(2)}, u32[]{:S(2)}) %collective-permute-start) | collective-permute-done | bytes 4128 | tf_op jit(solution)/shard_map/ppermute | solution.py:347
  7.0 0.0 collective-permute-done.1.far_cpl_ref
  7.0 0.8 %fold_lowest.1 = (bf16[144,256]{1,0:T(8,128)(2,1)S(1)}, bf16[144,256]{1,0:T(8,128)(2,1)S(1)}, bf16[144,256]{1,0:T(8,128)(2,1)S(1)}, bf16[144,256]{1,0:T(8,128)(2,1)S(1)}) custom-call(s32[2]{0:T(128)S(1)} %pad_add_fusion.where_ref.strip_ref, bf16[480,256]{1,0:T(8,128)(2,1)S(1)} %get-tuple-element.19.rows_ref, bf16[32,64]{1,0:T(8,128)(2,1)S(1)} %bitcast.24, ...), custom_call_target="tpu_custom_call" | custom-call | flops 10000000 | bytes 270344 | tf_op jit(solution)/shard_map/fold_lowest/pallas_call | solution.py:31
  7.9 2.9 %collective-permute-start.2 = (bf16[144,256]{1,0:T(8,128)(2,1)S(1)}, bf16[144,256]{1,0:T(8,128)(2,1)S(1)}, u32[]{:S(2)}, u32[]{:S(2)}) collective-permute-start(bf16[144,256]{1,0:T(8,128)(2,1)S(1)} %get-tuple-element.21), channel_id=1, source_target_pairs={{0,2},{2,0},{4,6},{6,4},{8,10},{10,8},{12,14},{14,12},{16,18},{18,... | collective-permute-start | bytes 221192 | tf_op jit(solution)/shard_map/ppermute | solution.py:351
  10.8 1.5 %collective-permute-start.3 = (bf16[144,256]{1,0:T(8,128)(2,1)S(1)}, bf16[144,256]{1,0:T(8,128)(2,1)S(1)}, u32[]{:S(2)}, u32[]{:S(2)}) collective-permute-start(bf16[144,256]{1,0:T(8,128)(2,1)S(1)} %get-tuple-element.22), channel_id=1, source_target_pairs={{0,4},{2,6},{4,0},{6,2},{8,12},{10,14},{12,8},{14,10},{16,20},{18,... | collective-permute-start | bytes 221192 | tf_op jit(solution)/shard_map/ppermute | solution.py:351
  12.3 0.0 collective-permute-start.4
  12.3 0.0 copy-done
  12.3 0.0 copy-done.1
  12.3 0.0 copy-done.4
  12.4 0.0 copy-start.6
  12.4 1.0 %copy-done.6 = bf16[768,256]{1,0:T(8,128)(2,1)S(1)} copy-done((bf16[768,256]{1,0:T(8,128)(2,1)S(1)}, bf16[768,256]{1,0:T(8,128)(2,1)}, u32[]{:S(2)}) %copy-start.6) | copy-done | bytes 393240
  13.3 1.2 %leaf_backward.1 = (f32[768,256]{1,0:T(8,128)S(1)}, bf16[768,480]{1,0:T(8,128)(2,1)S(1)}) custom-call(bf16[768,768]{1,0:T(8,128)(2,1)S(1)} %bitcast.16, bf16[512,768]{1,0:T(8,128)(2,1)S(1)} %bitcast.18, s32[1,512]{1,0:T(1,128)S(1)} %bitcast.26, bf16[768,256]{1,0:T(8,128)(2,1)S(1)} %copy-done.6), custom_call_target="tpu_custom_call" | custom-call | flops 1000000000 | bytes 2361344 | tf_op jit(solution)/shard_map/leaf_backward/pallas_call | solution.py:31
  14.6 0.0 collective-permute-done.2
  14.6 0.6 %collective-permute-done.3 = bf16[144,256]{1,0:T(8,128)(2,1)S(1)} collective-permute-done((bf16[144,256]{1,0:T(8,128)(2,1)S(1)}, bf16[144,256]{1,0:T(8,128)(2,1)S(1)}, u32[]{:S(2)}, u32[]{:S(2)}) %collective-permute-start.3) | collective-permute-done | bytes 73760 | tf_op jit(solution)/shard_map/ppermute | solution.py:351
  15.2 2.4 %collective-permute-done.4 = bf16[144,256]{1,0:T(8,128)(2,1)S(1)} collective-permute-done((bf16[144,256]{1,0:T(8,128)(2,1)S(1)}, bf16[144,256]{1,0:T(8,128)(2,1)S(1)}, u32[]{:S(2)}, u32[]{:S(2)}) %collective-permute-start.4) | collective-permute-done | bytes 73760 | tf_op jit(solution)/shard_map/ppermute | solution.py:351
  17.6 2.7 %collective-permute-start.6 = (bf16[128,256]{1,0:T(8,128)(2,1)S(1)}, bf16[128,256]{1,0:T(8,128)(2,1)S(1)}, u32[]{:S(2)}, u32[]{:S(2)}) collective-permute-start(bf16[128,256]{1,0:T(8,128)(2,1)S(1)} %slice.8), channel_id=1, source_target_pairs={{0,16},{2,18},{4,20},{6,22},{8,24},{10,26},{12,28},{14,30},{16,0},... | collective-permute-start | bytes 196616 | tf_op jit(solution)/shard_map/ppermute | solution.py:351
  20.3 1.6 %collective-permute-start.5 = (bf16[128,256]{1,0:T(8,128)(2,1)S(1)}, bf16[128,256]{1,0:T(8,128)(2,1)S(1)}, u32[]{:S(2)}, u32[]{:S(2)}) collective-permute-start(bf16[128,256]{1,0:T(8,128)(2,1)S(1)} %slice.8), channel_id=1, source_target_pairs={{0,8},{2,10},{4,12},{6,14},{8,0},{10,2},{12,4},{14,6},{16,24},{18,... | collective-permute-start | bytes 196616 | tf_op jit(solution)/shard_map/ppermute | solution.py:351
  21.9 0.2 collective-permute-start.7
  22.1 0.0 collective-permute-done.8.far_ref
  22.1 2.2 %solve_operator.1.solve_ref = bf16[480,960]{1,0:T(8,128)(2,1)S(1)} custom-call(s32[2]{0:T(128)S(1)} %pad_add_fusion.where_ref.strip_ref, bf16[544,512]{1,0:T(8,128)(2,1)S(1)} %get-tuple-element.27.own_ref, bf16[544,512]{1,0:T(8,128)(2,1)S(1)} %collective-permute-done.8.far_ref), custom_call_target="tpu_custom_call" | custom-call | flops 1000000000 | bytes 1114120 | tf_op jit(solution)/shard_map/solve_operator/pallas_call | solution.py:31
  24.3 0.1 collective-permute-done.6
  24.4 1.0 %collective-permute-done.5 = bf16[128,256]{1,0:T(8,128)(2,1)S(1)} collective-permute-done((bf16[128,256]{1,0:T(8,128)(2,1)S(1)}, bf16[128,256]{1,0:T(8,128)(2,1)S(1)}, u32[]{:S(2)}, u32[]{:S(2)}) %collective-permute-start.5) | collective-permute-done | bytes 65568 | tf_op jit(solution)/shard_map/ppermute | solution.py:351
  25.4 2.5 %collective-permute-done.7 = bf16[128,256]{1,0:T(8,128)(2,1)S(1)} collective-permute-done((bf16[128,256]{1,0:T(8,128)(2,1)S(1)}, bf16[128,256]{1,0:T(8,128)(2,1)S(1)}, u32[]{:S(2)}, u32[]{:S(2)}) %collective-permute-start.7) | collective-permute-done | bytes 65568 | tf_op jit(solution)/shard_map/ppermute | solution.py:351
  28.0 0.6 %collective-permute-start.9 = (bf16[144,256]{1,0:T(8,128)(2,1)S(1)}, bf16[144,256]{1,0:T(8,128)(2,1)S(1)}, u32[]{:S(2)}, u32[]{:S(2)}) collective-permute-start(bf16[144,256]{1,0:T(8,128)(2,1)S(1)} %pad_maximum_fusion), channel_id=1, source_target_pairs={{0,2},{2,0},{4,6},{6,4},{8,10},{10,8},{12,14},{14,12},{16,18},{18,... | collective-permute-start | bytes 221192 | tf_op jit(solution)/shard_map/ppermute | solution.py:351
  28.6 1.6 %collective-permute-start.11 = (bf16[144,256]{1,0:T(8,128)(2,1)S(1)}, bf16[144,256]{1,0:T(8,128)(2,1)S(1)}, u32[]{:S(2)}, u32[]{:S(2)}) collective-permute-start(bf16[144,256]{1,0:T(8,128)(2,1)S(1)} %pad_maximum_fusion), channel_id=1, source_target_pairs={{0,6},{2,4},{4,2},{6,0},{8,14},{10,12},{12,10},{14,8},{16,22},{18,... | collective-permute-start | bytes 221192 | tf_op jit(solution)/shard_map/ppermute | solution.py:351
  30.2 1.3 %collective-permute-start.10 = (bf16[144,256]{1,0:T(8,128)(2,1)S(1)}, bf16[144,256]{1,0:T(8,128)(2,1)S(1)}, u32[]{:S(2)}, u32[]{:S(2)}) collective-permute-start(bf16[144,256]{1,0:T(8,128)(2,1)S(1)} %pad_maximum_fusion), channel_id=1, source_target_pairs={{0,4},{2,6},{4,0},{6,2},{8,12},{10,14},{12,8},{14,10},{16,20},{18,... | collective-permute-start | bytes 221192 | tf_op jit(solution)/shard_map/ppermute | solution.py:351
  31.5 0.9 %collective-permute-done.9 = bf16[144,256]{1,0:T(8,128)(2,1)S(1)} collective-permute-done((bf16[144,256]{1,0:T(8,128)(2,1)S(1)}, bf16[144,256]{1,0:T(8,128)(2,1)S(1)}, u32[]{:S(2)}, u32[]{:S(2)}) %collective-permute-start.9) | collective-permute-done | bytes 73760 | tf_op jit(solution)/shard_map/ppermute | solution.py:351
  32.4 2.2 %collective-permute-done.10 = bf16[144,256]{1,0:T(8,128)(2,1)S(1)} collective-permute-done((bf16[144,256]{1,0:T(8,128)(2,1)S(1)}, bf16[144,256]{1,0:T(8,128)(2,1)S(1)}, u32[]{:S(2)}, u32[]{:S(2)}) %collective-permute-start.10) | collective-permute-done | bytes 73760 | tf_op jit(solution)/shard_map/ppermute | solution.py:351
  34.6 0.0 collective-permute-done.11
  34.7 0.1 collective-permute-start.12
  34.7 1.6 %collective-permute-done.12.far_ref = bf16[576,256]{1,0:T(8,128)(2,1)S(1)} collective-permute-done((bf16[576,256]{1,0:T(8,128)(2,1)S(1)}, bf16[576,256]{1,0:T(8,128)(2,1)S(1)}, u32[]{:S(2)}, u32[]{:S(2)}) %collective-permute-start.12) | collective-permute-done | bytes 294944 | tf_op jit(solution)/shard_map/ppermute | solution.py:347
  36.3 2.5 %finish.1 = (bf16[768,256]{1,0:T(8,128)(2,1)}, bf16[480,256]{1,0:T(8,128)(2,1)}) custom-call(s32[2]{0:T(128)S(1)} %pad_add_fusion.where_ref.strip_ref, bf16[576,256]{1,0:T(8,128)(2,1)S(1)} %constant_dynamic-update-slice_fusion.own_ref, bf16[576,256]{1,0:T(8,128)(2,1)S(1)} %collective-permute-done.12.far_ref, bf16[480,960]{1,0:T(8,128)(2,1)S(1)} %solve_operator.1.solve_ref, ...), custom_call_target="tpu_custom_call" | custom-call | flops 500000000 | bytes 3035144 | tf_op jit(solution)/shard_map/finish/pallas_call | solution.py:31
  (8 shorter events, 0.1 us)
Async XLA Ops:
  0.6 4.8 %copy-start.3 = (bf16[1,32,64]{2,1,0:T(8,128)(2,1)S(1)}, bf16[1,32,64]{2,1,0:T(8,128)(2,1)}, u32[]{:S(2)}) copy-start(bf16[1,32,64]{2,1,0:T(8,128)(2,1)} %param.15) | copy-start | bytes 12292
  0.6 4.8 %copy-start.2 = (bf16[1,64,64]{2,1,0:T(8,128)(2,1)S(1)}, bf16[1,64,64]{2,1,0:T(8,128)(2,1)}, u32[]{:S(2)}) copy-start(bf16[1,64,64]{2,1,0:T(8,128)(2,1)} %param.19) | copy-start | bytes 24580
  0.7 11.7 %copy-start = (bf16[1,1,768,768]{3,2,1,0:T(8,128)(2,1)S(1)}, bf16[1,1,768,768]{3,2,1,0:T(8,128)(2,1)}, u32[]{:S(2)}) copy-start(bf16[1,1,768,768]{3,2,1,0:T(8,128)(2,1)} %param.12) | copy-start | bytes 3538948
  0.7 11.7 %copy-start.1 = (bf16[1,1,512,768]{3,2,1,0:T(8,128)(2,1)S(1)}, bf16[1,1,512,768]{3,2,1,0:T(8,128)(2,1)}, u32[]{:S(2)}) copy-start(bf16[1,1,512,768]{3,2,1,0:T(8,128)(2,1)} %param.13) | copy-start | bytes 2359300
  0.7 11.7 %copy-start.4 = (s32[1,1,512]{2,1,0:T(1,128)S(1)}, s32[1,1,512]{2,1,0:T(1,128)}, u32[]{:S(2)}) copy-start(s32[1,1,512]{2,1,0:T(1,128)} %param.14) | copy-start | bytes 6148
  4.2 0.7 %copy-start.5 = (bf16[768,256]{1,0:T(8,128)(2,1)}, bf16[768,256]{1,0:T(8,128)(2,1)S(1)}, u32[]{:S(2)}) copy-start(bf16[768,256]{1,0:T(8,128)(2,1)S(1)} %get-tuple-element.24.half_ref) | copy-start | bytes 1179652
  5.0 17.1 %collective-permute-start.8 = (bf16[544,512]{1,0:T(8,128)(2,1)S(1)}, bf16[544,512]{1,0:T(8,128)(2,1)S(1)}, u32[]{:S(2)}, u32[]{:S(2)}) collective-permute-start(bf16[544,512]{1,0:T(8,128)(2,1)S(1)} %get-tuple-element.27.own_ref), channel_id=1, source_target_pairs={{0,1},{1,0},{2,3},{3,2},{4,5},{5,4},{6,7},{7,6},{8,9},{9,8},{10,11... | collective-permute-start | bytes 1671176 | tf_op jit(solution)/shard_map/ppermute | solution.py:347
  5.4 1.6 %collective-permute-start = (bf16[32,64]{1,0:T(8,128)(2,1)S(1)}, bf16[32,64]{1,0:T(8,128)(2,1)S(1)}, u32[]{:S(2)}, u32[]{:S(2)}) collective-permute-start(bf16[32,64]{1,0:T(8,128)(2,1)S(1)} %bitcast.23), channel_id=1, source_target_pairs={{0,1},{1,0},{2,3},{3,2},{4,5},{5,4},{6,7},{7,6},{8,9},{9,8},{10,11... | collective-permute-start | bytes 12296 | tf_op jit(solution)/shard_map/ppermute | solution.py:347
  5.5 1.6 %collective-permute-start.1 = (bf16[64,64]{1,0:T(8,128)(2,1)S(1)}, bf16[64,64]{1,0:T(8,128)(2,1)S(1)}, u32[]{:S(2)}, u32[]{:S(2)}) collective-permute-start(bf16[64,64]{1,0:T(8,128)(2,1)S(1)} %bitcast.20), channel_id=1, source_target_pairs={{0,1},{1,0},{2,3},{3,2},{4,5},{5,4},{6,7},{7,6},{8,9},{9,8},{10,11... | collective-permute-start | bytes 24584 | tf_op jit(solution)/shard_map/ppermute | solution.py:347
  7.9 6.7 %collective-permute-start.2 = (bf16[144,256]{1,0:T(8,128)(2,1)S(1)}, bf16[144,256]{1,0:T(8,128)(2,1)S(1)}, u32[]{:S(2)}, u32[]{:S(2)}) collective-permute-start(bf16[144,256]{1,0:T(8,128)(2,1)S(1)} %get-tuple-element.21), channel_id=1, source_target_pairs={{0,2},{2,0},{4,6},{6,4},{8,10},{10,8},{12,14},{14,12},{16,18},{18,... | collective-permute-start | bytes 221192 | tf_op jit(solution)/shard_map/ppermute | solution.py:351
  10.8 4.4 %collective-permute-start.3 = (bf16[144,256]{1,0:T(8,128)(2,1)S(1)}, bf16[144,256]{1,0:T(8,128)(2,1)S(1)}, u32[]{:S(2)}, u32[]{:S(2)}) collective-permute-start(bf16[144,256]{1,0:T(8,128)(2,1)S(1)} %get-tuple-element.22), channel_id=1, source_target_pairs={{0,4},{2,6},{4,0},{6,2},{8,12},{10,14},{12,8},{14,10},{16,20},{18,... | collective-permute-start | bytes 221192 | tf_op jit(solution)/shard_map/ppermute | solution.py:351
  12.3 5.3 %collective-permute-start.4 = (bf16[144,256]{1,0:T(8,128)(2,1)S(1)}, bf16[144,256]{1,0:T(8,128)(2,1)S(1)}, u32[]{:S(2)}, u32[]{:S(2)}) collective-permute-start(bf16[144,256]{1,0:T(8,128)(2,1)S(1)} %get-tuple-element.23), channel_id=1, source_target_pairs={{0,6},{2,4},{4,2},{6,0},{8,14},{10,12},{12,10},{14,8},{16,22},{18,... | collective-permute-start | bytes 221192 | tf_op jit(solution)/shard_map/ppermute | solution.py:351
  12.4 1.0 %copy-start.6 = (bf16[768,256]{1,0:T(8,128)(2,1)S(1)}, bf16[768,256]{1,0:T(8,128)(2,1)}, u32[]{:S(2)}) copy-start(bf16[768,256]{1,0:T(8,128)(2,1)} %copy-done.5) | copy-start | bytes 1179652
  17.6 6.7 %collective-permute-start.6 = (bf16[128,256]{1,0:T(8,128)(2,1)S(1)}, bf16[128,256]{1,0:T(8,128)(2,1)S(1)}, u32[]{:S(2)}, u32[]{:S(2)}) collective-permute-start(bf16[128,256]{1,0:T(8,128)(2,1)S(1)} %slice.8), channel_id=1, source_target_pairs={{0,16},{2,18},{4,20},{6,22},{8,24},{10,26},{12,28},{14,30},{16,0},... | collective-permute-start | bytes 196616 | tf_op jit(solution)/shard_map/ppermute | solution.py:351
  20.3 5.1 %collective-permute-start.5 = (bf16[128,256]{1,0:T(8,128)(2,1)S(1)}, bf16[128,256]{1,0:T(8,128)(2,1)S(1)}, u32[]{:S(2)}, u32[]{:S(2)}) collective-permute-start(bf16[128,256]{1,0:T(8,128)(2,1)S(1)} %slice.8), channel_id=1, source_target_pairs={{0,8},{2,10},{4,12},{6,14},{8,0},{10,2},{12,4},{14,6},{16,24},{18,... | collective-permute-start | bytes 196616 | tf_op jit(solution)/shard_map/ppermute | solution.py:351
  21.9 6.1 %collective-permute-start.7 = (bf16[128,256]{1,0:T(8,128)(2,1)S(1)}, bf16[128,256]{1,0:T(8,128)(2,1)S(1)}, u32[]{:S(2)}, u32[]{:S(2)}) collective-permute-start(bf16[128,256]{1,0:T(8,128)(2,1)S(1)} %slice.8), channel_id=1, source_target_pairs={{0,24},{2,26},{4,28},{6,30},{8,16},{10,18},{12,20},{14,22},{16,8},... | collective-permute-start | bytes 196616 | tf_op jit(solution)/shard_map/ppermute | solution.py:351
  28.0 4.4 %collective-permute-start.9 = (bf16[144,256]{1,0:T(8,128)(2,1)S(1)}, bf16[144,256]{1,0:T(8,128)(2,1)S(1)}, u32[]{:S(2)}, u32[]{:S(2)}) collective-permute-start(bf16[144,256]{1,0:T(8,128)(2,1)S(1)} %pad_maximum_fusion), channel_id=1, source_target_pairs={{0,2},{2,0},{4,6},{6,4},{8,10},{10,8},{12,14},{14,12},{16,18},{18,... | collective-permute-start | bytes 221192 | tf_op jit(solution)/shard_map/ppermute | solution.py:351
  28.6 6.1 %collective-permute-start.11 = (bf16[144,256]{1,0:T(8,128)(2,1)S(1)}, bf16[144,256]{1,0:T(8,128)(2,1)S(1)}, u32[]{:S(2)}, u32[]{:S(2)}) collective-permute-start(bf16[144,256]{1,0:T(8,128)(2,1)S(1)} %pad_maximum_fusion), channel_id=1, source_target_pairs={{0,6},{2,4},{4,2},{6,0},{8,14},{10,12},{12,10},{14,8},{16,22},{18,... | collective-permute-start | bytes 221192 | tf_op jit(solution)/shard_map/ppermute | solution.py:351
  30.2 4.4 %collective-permute-start.10 = (bf16[144,256]{1,0:T(8,128)(2,1)S(1)}, bf16[144,256]{1,0:T(8,128)(2,1)S(1)}, u32[]{:S(2)}, u32[]{:S(2)}) collective-permute-start(bf16[144,256]{1,0:T(8,128)(2,1)S(1)} %pad_maximum_fusion), channel_id=1, source_target_pairs={{0,4},{2,6},{4,0},{6,2},{8,12},{10,14},{12,8},{14,10},{16,20},{18,... | collective-permute-start | bytes 221192 | tf_op jit(solution)/shard_map/ppermute | solution.py:351
  34.7 1.6 %collective-permute-start.12 = (bf16[576,256]{1,0:T(8,128)(2,1)S(1)}, bf16[576,256]{1,0:T(8,128)(2,1)S(1)}, u32[]{:S(2)}, u32[]{:S(2)}) collective-permute-start(bf16[576,256]{1,0:T(8,128)(2,1)S(1)} %constant_dynamic-update-slice_fusion.own_ref), channel_id=1, source_target_pairs={{0,1},{1,0},{2,3},{3,2},{4,5},{5,4},{6,7},{7,6},{8,9},{9,8},{10,11... | collective-permute-start | bytes 884744 | tf_op jit(solution)/shard_map/ppermute | solution.py:347

commit v2 on v1

v2 whole, which is shorter than its diff:
```python
import jax
import jax.numpy as jnp
from jax import lax
from jax.experimental import pallas as pl
from jax.experimental.pallas import tpu as pltpu
from jax.sharding import PartitionSpec as P

BLOCK = 256
CHIPS = 4
MIB = 1024 * 1024
VMEM = pl.BlockSpec(memory_space=pltpu.VMEM)
HBM = pl.BlockSpec(memory_space=pltpu.HBM)


def bf16(x):
    return x.astype(jnp.bfloat16)


def dot(a, b):
    return jnp.dot(a, b, preferred_element_type=jnp.float32)


def dot_tn(a, b):
    return lax.dot_general(a, b, (((0,), (0,)), ((), ())), preferred_element_type=jnp.float32)


def call(kernel, name, outs, ins, specs, out_specs, flops, limit=16, scratch=()):
    ins = [pltpu.with_memory_space_constraint(x, pltpu.HBM) if s is HBM else x for x, s in zip(ins, specs)]
    moved = sum(x.size * x.dtype.itemsize for x in ins)
    return pl.pallas_call(
        kernel,
        out_shape=outs,
        in_specs=specs,
        out_specs=out_specs,
        scratch_shapes=list(scratch),
        compiler_params=pltpu.CompilerParams(vmem_limit_bytes=limit * MIB),
        cost_estimate=pl.CostEstimate(flops=flops, bytes_accessed=moved, transcendentals=0),
        name=name,
    )(*ins)


def in_plane():
    return lax.rem(lax.axis_index("sub"), CHIPS)


def struct(shape, dtype=jnp.bfloat16):
    return jax.ShapeDtypeStruct(shape, dtype)


def offsets(sizes):
    return [sum(sizes[:i]) for i in range(len(sizes))]


def places(sizes):
    return [sum(sizes[i + 1 :]) for i in range(len(sizes))]


def moved_rows(tgt, sizes, order):
    moved = tgt
    for start, place, size in zip(offsets(sizes), order, sizes):
        inside = (tgt >= start) & (tgt < start + size)
        moved = jnp.where(inside, tgt + (place - start), moved)
    return moved


def scatter_matrix(moved, rows, start=0):
    slots = lax.broadcasted_iota(jnp.int32, (rows, moved.shape[1]), 0)
    return bf16(jnp.where(slots + start == moved, 1.0, 0.0))


def leaf_forward(src, inv, cpl, tgt, separators, parents):
    inner, shots = src.shape
    count = inner // BLOCK
    sizes = [m.shape[0] for m in separators]
    s0, s1, s2, s3 = sizes
    o0, o1, o2, o3 = [m.shape[1] for m in separators]
    part, _ = share_rows(sizes)

    def kernel(src_hbm, inv_hbm, cpl_hbm, tgt_hbm, i0, i1, i2, i3, c0, c1, c2,
               half_ref, share0, share1, share2, share3, pack_ref,
               src, inv, cpl, edge_ref, small0, small1, tgt_ref, sems):
        moves = [(tgt_hbm, tgt_ref)]
        for i in range(count):
            rows = pl.ds(i * BLOCK, BLOCK)
            cols = pl.ds(0, (i + 1) * BLOCK)
            moves.append((src_hbm.at[rows], src.at[rows]))
            moves.append((inv_hbm.at[rows, cols], inv.at[rows, cols]))
            moves.append((cpl_hbm.at[:, rows], cpl.at[:, rows]))
        leaf = len(moves)
        moves += [
            (i0, small0),
            (c0, small1),
            (i3, pack_ref.at[pl.ds(0, s3), :]),
            (c2, pack_ref.at[pl.ds(s3, s3), pl.ds(0, o2)]),
            (i2, pack_ref.at[pl.ds(s3, s2), pl.ds(o2, o2)]),
            (c1, pack_ref.at[pl.ds(s3 + s2, s2), pl.ds(o2, o1)]),
            (i1, pack_ref.at[pl.ds(s3 + s2, s1), pl.ds(o2 + o1, o1)]),
        ]
        copies = [pltpu.make_async_copy(x, y, sems.at[i]) for i, (x, y) in enumerate(moves)]
        for copy in copies:
            copy.start()
        copies[0].wait()
        moved = moved_rows(tgt_ref[...], sizes, (CHIPS * part, s3 + s2, s3, 0))
        picks = [scatter_matrix(moved, part, part * (in_plane() ^ k)) for k in range(CHIPS)]
        picks.append(scatter_matrix(moved, s0, CHIPS * part))
        for i in range(count):
            rows = pl.ds(i * BLOCK, BLOCK)
            cols = pl.ds(0, (i + 1) * BLOCK)
            copies[3 * i + 1].wait()
            copies[3 * i + 2].wait()
            half = bf16(dot(inv[rows, cols], src[cols, :]))
            half_ref[rows, :] = half
            copies[3 * i + 3].wait()
            term = dot(cpl[:, rows], half)
            if i == 0:
                edge_ref[...] = term
            else:
                edge_ref[...] += term
        edge = bf16(edge_ref[...])
        lowest = bf16(dot(picks[CHIPS], edge))
        for pick, share in zip(picks, (share0, share1, share2, share3)):
            share[pl.ds(0, part), :] = bf16(dot(pick, edge))
            share[pl.ds(part, s0), :] = lowest
        for copy in copies[leaf:]:
            copy.wait()
        pack_ref[pl.ds(2 * s3, s0), pl.ds(0, o0)] = small0[...]
        pack_ref[pl.ds(s3 + s2 + s1, s1), pl.ds(o2 + o1, o0)] = small1[...]

    return call(
        kernel,
        "leaf_forward",
        (
            struct((inner, shots)),
            *[struct((part + s0, shots))] * CHIPS,
            struct((2 * s3 + s0, o3)),
        ),
        (src, inv, cpl, tgt, *separators, *parents),
        [HBM] * 11,
        (VMEM,) * (CHIPS + 2),
        600_000_000,
        scratch=[
            pltpu.VMEM(src.shape, jnp.bfloat16),
            pltpu.VMEM(inv.shape, jnp.bfloat16),
            pltpu.VMEM(cpl.shape, jnp.bfloat16),
            pltpu.VMEM((cpl.shape[0], shots), jnp.float32),
            pltpu.VMEM((s0, o0), jnp.bfloat16),
            pltpu.VMEM((s1, o0), jnp.bfloat16),
            pltpu.VMEM(tgt.shape, jnp.int32),
            pltpu.SemaphoreType.DMA((3 * count + 8,)),
        ],
    )


def share_rows(sizes):
    return sum(sizes[1:]) // CHIPS, sizes[1] // CHIPS


def ordered(first, own, other):
    return jnp.concatenate([jnp.where(first, own, other), jnp.where(first, other, own)], 0)


def plane_sum(pieces, pack, far_pack, separators, parents):
    sizes = [m.shape[0] for m in separators]
    s0, s1, s2, s3 = sizes
    o0, o1, o2, _ = [m.shape[1] for m in separators]
    part, side = share_rows(sizes)
    shots = pieces[0].shape[1]

    def kernel(a, b, c, d, pack_ref, far_pack_ref, share_ref, low_ref):
        first = lax.axis_index("sep") == 0
        total = sum(x[...].astype(jnp.float32) for x in (a, b, c, d))
        low = bf16(total[part:])
        low_ref[...] = low
        share_ref[pl.ds(0, part - s1), :] = bf16(total[: part - s1])
        inv_at = (pl.ds(2 * s3, s0), pl.ds(0, o0))
        cpl_at = (pl.ds(s3 + s2 + s1, s1), pl.ds(o2 + o1, o0))
        inv = ordered(first, pack_ref[inv_at], far_pack_ref[inv_at])
        up = bf16(dot(inv, ordered(first, low, jnp.zeros_like(low))))
        own, far = dot(pack_ref[cpl_at], up), dot(far_pack_ref[cpl_at], up)
        me = in_plane()
        end = total[part - s1 : part] + jnp.where(me == CHIPS - 1, own, 0.0)
        share_ref[pl.ds(part - s1, s1), :] = bf16(end)
        kept = far[:side]
        for q in range(1, CHIPS):
            kept = jnp.where(me == q, far[q * side : (q + 1) * side], kept)
        share_ref[pl.ds(part, side), :] = bf16(kept)

    return call(
        kernel,
        "plane_sum",
        (struct((part + side, shots)), struct((s0, shots))),
        (*pieces, pack, far_pack),
        [VMEM] * 6,
        (VMEM, VMEM),
        10_000_000,
        limit=4,
    )


def exchange_columns(cols):
    i = lax.broadcasted_iota(jnp.int32, (cols, cols), 0)
    j = lax.broadcasted_iota(jnp.int32, (cols, cols), 1)
    return bf16(jnp.where((i - j == cols // 2) | (j - i == cols // 2), 1.0, 0.0))


def solve_operator(pack, far_pack, lift, separators, parents):
    s = [m.shape[0] for m in separators]
    o = [m.shape[1] for m in separators]
    total = sum(s)
    inner = lift.shape[0]
    width = sum(s) + s[1]

    def kernel(own_ref, far_ref, lift_ref, out_ref, far_out_ref):
        first = lax.axis_index("sep") == 0

        def whole(row, rows, col, cols):
            at = (pl.ds(row, rows), pl.ds(col, cols))
            return ordered(first, own_ref[at], far_ref[at])

        def own_columns(x):
            half = x.shape[1] // 2
            if half % 128:
                return jnp.where(first, x, bf16(dot(x, exchange_columns(2 * half))))
            return jnp.where(first, x, jnp.concatenate([x[:, half:], x[:, :half]], 1))

        x3 = own_columns(whole(0, s[3], 0, o[3]))
        c2 = whole(s[3], s[3], 0, o[2])
        x2 = whole(s[3], s[2], o[2], o[2])
        c1 = whole(s[3] + s[2], s[2], o[2], o[1])
        x1 = whole(s[3] + s[2], s[1], o[2] + o[1], o[1])
        c0 = whole(s[3] + s[2] + s[1], s[1], o[2] + o[1], o[0])
        x0 = own_columns(whole(2 * s[3], s[0], 0, o[0]))
        t3 = bf16(dot(whole(0, s[3], 0, o[3]), c2))
        t2 = bf16(dot(x2, c1))
        t1 = bf16(dot(x1, c0))
        x2, x1 = own_columns(x2), own_columns(x1)
        n32 = bf16(dot(t3, x2))
        n21 = bf16(dot(t2, x1))
        n10 = bf16(dot(t1, x0))
        n31 = bf16(dot(t3, n21))
        n20 = bf16(dot(t2, n10))
        n30 = bf16(dot(t3, n20))

        def turned(x, sign):
            y = x.astype(jnp.float32).T
            return bf16(sign * y[: y.shape[0] // 2])

        m3 = jnp.concatenate([turned(x3, 1.0), turned(n32, -1.0), turned(n31, 1.0), turned(n30, -1.0)], 0)
        m2 = jnp.concatenate([turned(x2, 1.0), turned(n21, -1.0), turned(n20, 1.0)], 0)
        m1 = jnp.concatenate([turned(x1, 1.0), turned(n10, -1.0)], 0)
        m0 = turned(x0, 1.0)
        top, mid, low = s[3], s[3] + s[2], s[3] + s[2] + s[1]
        a3 = bf16(dot(m3, x3))
        out_ref[pl.ds(0, total), pl.ds(0, top)] = a3[:, :top]
        far_out_ref[pl.ds(0, total), pl.ds(0, top)] = a3[:, top:]
        a2 = dot(m3, n32)
        a2 = bf16(jnp.concatenate([a2[:top], a2[top:] + dot(m2, x2)], 0))
        out_ref[pl.ds(0, total), pl.ds(top, s[2])] = a2[:, : s[2]]
        far_out_ref[pl.ds(0, total), pl.ds(top, s[2])] = a2[:, s[2] :]
        a1 = dot(m3, n31)
        rest = a1[top:] + dot(m2, n21)
        a1 = bf16(jnp.concatenate([a1[:top], rest[: s[2]], rest[s[2] :] + dot(m1, x1)], 0))
        out_ref[pl.ds(0, total), pl.ds(mid, o[1])] = a1
        far_out_ref[pl.ds(0, total), pl.ds(mid, o[1])] = bf16(dot(a1, exchange_columns(o[1])))
        a0 = bf16(dot(m0, x0))
        for ref, block in ((out_ref, a0), (far_out_ref, bf16(dot(a0, exchange_columns(o[0]))))):
            ref[pl.ds(0, low), pl.ds(mid + o[1], s[0])] = jnp.zeros((low, s[0]), jnp.bfloat16)
            ref[pl.ds(low, s[0]), pl.ds(mid + o[1], s[0])] = block[:, : s[0]]
            ref[pl.ds(total, inner), :] = bf16(-dot(lift_ref[...], ref[pl.ds(0, total), :]))

    shape = struct((total + inner, width))
    return call(
        kernel,
        "solve_operator",
        (shape, shape),
        (pack, far_pack, lift),
        [VMEM] * 3,
        (VMEM, VMEM),
        2_000_000_000,
    )


def leaf_backward(inv, cpl, tgt, half, sizes):
    inner, shots = half.shape
    count = inner // BLOCK
    total = sum(sizes)

    def kernel(inv_ref, cpl_ref, tgt_ref, half_ref, direct_ref, lift_ref, reach_ref):
        onehot = scatter_matrix(moved_rows(tgt_ref[...], sizes, places(sizes)), total)
        for i in range(count):
            cols = pl.ds(i * BLOCK, BLOCK)
            reach_ref[:, cols] = bf16(dot(onehot, cpl_ref[:, cols]))
        for j in range(count):
            rows = pl.ds(j * BLOCK, inner - j * BLOCK)
            cols = pl.ds(j * BLOCK, BLOCK)
            block = inv_ref[rows, cols]
            direct_ref[cols, :] = dot_tn(block, half_ref[rows, :])
            lift_ref[cols, :] = bf16(dot(reach_ref[:, rows], block).T)

    return call(
        kernel,
        "leaf_backward",
        (struct((inner, shots), jnp.float32), struct((inner, total))),
        (inv, cpl, tgt, half),
        [VMEM] * 4,
        (VMEM, VMEM),
        1_000_000_000,
        scratch=[pltpu.VMEM((total, inner), jnp.bfloat16)],
    )


def collect(rows, shared_ref, sizes):
    part, side = share_rows(sizes)
    each = part + side
    for q in range(CHIPS):
        at = pl.multiple_of((in_plane() ^ q) * each, each)
        rows[pl.ds(q * part, part), :] = shared_ref[pl.ds(at, part), :]
        rows[pl.ds(CHIPS * part + q * side, side), :] = shared_ref[pl.ds(at + part, side), :]


def own_part(shared, low, far_low, solve, far_solve, direct, sizes):
    total, s0 = sum(sizes), sizes[0]
    inner, shots = direct.shape
    height, width = solve.shape
    upper = width - s0

    def kernel(shared_ref, low_ref, far_low_ref, solve_ref, far_ref, direct_ref, out_ref, rhs):
        collect(rhs, shared_ref, sizes)
        rhs[pl.ds(upper, s0), :] = low_ref[...]
        sum_ = dot(solve_ref[...], rhs[...]) + dot(far_ref[:, pl.ds(upper, s0)], far_low_ref[...])
        out_ref[pl.ds(0, total), :] = sum_[:total]
        out_ref[pl.ds(total, inner), :] = sum_[total:] + direct_ref[...]

    return call(
        kernel,
        "own_part",
        struct((height, shots), jnp.float32),
        (shared, low, far_low, solve, far_solve, direct),
        [VMEM] * 6,
        VMEM,
        400_000_000,
        scratch=[pltpu.VMEM((width, shots), jnp.bfloat16)],
    )


def finish(shared, solve, own, sizes):
    total = sum(sizes)
    shots = shared.shape[1]
    upper = shared.shape[0]
    inner = own.shape[0] - total
    count = inner // BLOCK

    def kernel(shared_ref, solve_ref, own_ref, inner_hbm, sep_hbm, rhs, inner_buf, sep_buf, sems):
        collect(rhs, shared_ref, sizes)

        def block(start, size):
            rows = pl.ds(start, size)
            return bf16(own_ref[rows, :] + dot(solve_ref[rows, pl.ds(0, upper)], rhs[...]))

        down = block(0, total)
        for begin, place, size in zip(offsets(sizes), places(sizes), sizes):
            sep_buf[pl.ds(begin, size), :] = down[place : place + size]
        copies = [pltpu.make_async_copy(sep_buf, sep_hbm, sems.at[count])]
        copies[0].start()
        for i in range(count):
            rows = pl.ds(i * BLOCK, BLOCK)
            inner_buf[rows, :] = block(total + i * BLOCK, BLOCK)
            copies.append(pltpu.make_async_copy(inner_buf.at[rows], inner_hbm.at[rows], sems.at[i]))
            copies[-1].start()
        for copy in copies:
            copy.wait()

    return call(
        kernel,
        "finish",
        (struct((inner, shots)), struct((total, shots))),
        (shared, solve, own),
        [VMEM] * 3,
        (HBM, HBM),
        400_000_000,
        scratch=[
            pltpu.VMEM((upper, shots), jnp.bfloat16),
            pltpu.VMEM((inner, shots), jnp.bfloat16),
            pltpu.VMEM((total, shots), jnp.bfloat16),
            pltpu.SemaphoreType.DMA((count + 1,)),
        ],
    )


def other_strip(x):
    return lax.ppermute(x, "sep", [(0, 1), (1, 0)])


def partner(x, mask):
    return lax.ppermute(x, "sub", [(s, s ^ mask) for s in range(lax.axis_size("sub"))])


def added(*terms):
    return bf16(sum(t.astype(jnp.float32) for t in terms))


def local(sources, inner_inv, coupling, boundary_map, *blocks):
    src, inv, cpl, tgt = sources[0, 0], inner_inv[0, 0], coupling[0, 0], boundary_map[0]
    separators = [m[0] for m in blocks[:4]]
    parents = [m[0] for m in blocks[4:]]
    sizes = [m.shape[0] for m in separators]
    half, *parts, pack = leaf_forward(src, inv, cpl, tgt, separators, parents)
    pieces = parts[:1] + [partner(parts[k], k) for k in range(1, CHIPS)]
    direct, lift = leaf_backward(inv, cpl, tgt, half, sizes)
    far_pack = other_strip(pack)
    share, low = plane_sum(pieces, pack, far_pack, separators, parents)
    far_low = other_strip(low)
    solve, far_solve = solve_operator(pack, far_pack, lift, separators, parents)
    along = [partner(share, CHIPS * k) for k in range(1, CHIPS)]
    along, far_low, direct, solve, far_solve = lax.optimization_barrier((along, far_low, direct, solve, far_solve))
    share = added(share, *along)
    shared = jnp.concatenate([share] + [partner(share, k) for k in range(1, CHIPS)], 0)
    own = own_part(shared, low, far_low, solve, far_solve, direct, sizes)
    inner, sep = finish(other_strip(shared), far_solve, own, sizes)
    return (inner[None, None], sep[None, None])


def local_any(sources, inner_inv, coupling, boundary_map, *blocks):
    src, inv, cpl, tgt = sources[0, 0], inner_inv[0, 0], coupling[0, 0], boundary_map[0, 0]
    separators = [m[0] for m in blocks[:4]]
    parents = [m[0] for m in blocks[4:]]
    sizes = [m.shape[0] for m in separators]
    levels = len(sizes)
    bits = lax.axis_size("sub").bit_length() - 1

    def both(x):
        return lax.all_gather(x, "sep", axis=0, tiled=True)

    half = bf16(dot(inv, src))
    edge = bf16(dot(cpl, half))
    slots = lax.broadcasted_iota(jnp.int32, (sum(sizes), tgt.shape[0]), 0)
    carried = dot(bf16(slots == tgt[None, :]), edge)
    ups = []
    for level, size in enumerate(sizes):
        for bit in range(2 * level, min(2 * level + 2, bits)):
            sent = partner(bf16(carried), 1 << bit)
            carried = carried + sent.astype(jnp.float32)
        up = both(bf16(dot(separators[level], both(bf16(carried[:size])))))
        ups.append(up)
        carried = carried[size:]
        if level < levels - 1:
            carried = carried.at[: sizes[level + 1]].add(dot(parents[level], up))
    own, down = [None] * levels, None
    for level in reversed(range(levels)):
        target = ups[level]
        if down is not None:
            target = bf16(target.astype(jnp.float32) - dot_tn(both(parents[level]), down))
        down = bf16(dot_tn(both(separators[level]), target))
        own[level] = lax.dynamic_slice_in_dim(down, lax.axis_index("sep") * sizes[level], sizes[level], 0)
    sep = jnp.concatenate(own, 0)
    lifted = bf16(dot_tn(cpl, jnp.take(sep, tgt, axis=0)))
    inner = bf16(dot_tn(inv, half) - dot_tn(inv, lifted))
    return (inner[None, None], sep[None, None])


def solution(mesh):
    whole = P("sub", "sep", None, None)
    placed = (whole,) * 2 + (whole, P("sub", "sep", None)) + (P("sub", "sep", None),) * 7
    two_stages = mesh.shape["sub"] == CHIPS * CHIPS
    return jax.shard_map(
        local if two_stages else local_any,
        mesh=mesh,
        in_specs=placed,
        out_specs=(whole, whole),
        check_vma=False,
    )
```

time: 38.9 us -> 32.3 us (0.83)
  waiting for transfers between devices: 12.3 us -> 9.15 us
  local copies, waits for them, and re-layouts: 1.78 us -> 0.01 us
  starting transfers between devices: 13.5 us -> 12.7 us
  Pallas kernels: 10.2 us -> 9.51 us
    ppermute x4 -> x3, waiting for transfers between devices: 2.6 us -> 0.7 us  [other_strip(): return lax.ppermute(x, 'sep', [(0, 1), (1, 0)])]
    unnamed x16 -> x6, local copies, waits for them, and re-layouts: 1.76 us -> 0.01 us
    ppermute x9, waiting for transfers between devices: 9.74 us -> 8.45 us  [partner(): lax.ppermute(x, 'sub', [(s, s ^ mask) for s in range(lax.axis_size('sub'))])]
    pallas_call x5 -> x6, Pallas kernels: 10.2 us -> 9.51 us  [call(): pl.pallas_call(kernel, out_shape=outs, in_specs=specs, out_specs=out_spec...]
    ppermute x4 -> x3, starting transfers between devices: 1.03 us -> 0.59 us  [other_strip(): return lax.ppermute(x, 'sep', [(0, 1), (1, 0)])]
  transfers between devices with their start and end apart: 13 -> 12, of which waited for: 9 -> 8; matrix products, arithmetic and copies ran while one was open for 0% -> 0% of each run, Pallas kernels for 11% -> 15%
where the time goes in v2:
time: 32.3 us; the launch traced here: 32.1 us
  starting transfers between devices  12.7 us (39%)
  Pallas kernels  9.51 us (29%)
  waiting for transfers between devices  9.15 us (28%)
  between operations  0.73 us (2%)
    ppermute x9, starting transfers between devices, partner(): lax.ppermute(x, 'sub', [(s, s ^ mask) for s in range(lax.axis_size('sub'))])  12.1 us
    pallas_call x6, Pallas kernels, call(): pl.pallas_call(kernel, out_shape=outs, in_specs=specs, out_specs=out_spec...  9.51 us
    ppermute x9, waiting for transfers between devices, partner(): lax.ppermute(x, 'sub', [(s, s ^ mask) for s in range(lax.axis_size('sub'))])  8.45 us
    ppermute x3, waiting for transfers between devices, other_strip(): return lax.ppermute(x, 'sep', [(0, 1), (1, 0)])  0.7 us
  transfers between devices with their start and end apart: 12, of which 8 were waited for; matrix products, arithmetic and copies ran while one was open for 0% of the time, Pallas kernels for 15%

profile of v2, /device:TPU:0, one launch (start us, length us, event | category | flops | bytes accessed | tf_op | source)
XLA Modules:
  0.0 32.1 jit_solution(2594839832316773361)
XLA Ops:
  0.6 0.0 copy-start.2
  0.6 0.0 copy-start.1
  0.7 0.0 copy-start
  0.7 3.1 %leaf_forward.1 = (bf16[768,256]{1,0:T(8,128)(2,1)S(1)}, bf16[144,256]{1,0:T(8,128)(2,1)S(1)}, bf16[144,256]{1,0:T(8,128)(2,1)S(1)}, bf16[144,256]{1,0:T(8,128)(...) custom-call(bf16[768,256]{1,0:T(8,128)(2,1)} %bitcast.19, bf16[768,768]{1,0:T(8,128)(2,1)} %bitcast.13, ...), custom_call_target="tpu_custom_call" | custom-call | flops 600000000 | bytes 2881536 | tf_op jit(solution)/shard_map/leaf_forward/pallas_call | solution.py:30
  3.7 0.5 %collective-permute-start.3 = (bf16[544,512]{1,0:T(8,128)(2,1)S(1)}, bf16[544,512]{1,0:T(8,128)(2,1)S(1)}, u32[]{:S(2)}, u32[]{:S(2)}) collective-permute-start(bf16[544,512]{1,0:T(8,128)(2,1)S(1)} %get-tuple-element.27.pack_ref.own_ref), channel_id=1, source_target_pairs={{0,1},{1,0},{2,3},{3,2},{4,5},{5,4},{6,7},{7,6},{8,9},{9,8},{10,11... | collective-permute-start | bytes 1671176 | tf_op jit(solution)/shard_map/ppermute | solution.py:391
  4.2 2.6 %collective-permute-start = (bf16[144,256]{1,0:T(8,128)(2,1)S(1)}, bf16[144,256]{1,0:T(8,128)(2,1)S(1)}, u32[]{:S(2)}, u32[]{:S(2)}) collective-permute-start(bf16[144,256]{1,0:T(8,128)(2,1)S(1)} %get-tuple-element.24), channel_id=1, source_target_pairs={{0,2},{2,0},{4,6},{6,4},{8,10},{10,8},{12,14},{14,12},{16,18},{18,... | collective-permute-start | bytes 221192 | tf_op jit(solution)/shard_map/ppermute | solution.py:395
  6.8 1.5 %collective-permute-start.1 = (bf16[144,256]{1,0:T(8,128)(2,1)S(1)}, bf16[144,256]{1,0:T(8,128)(2,1)S(1)}, u32[]{:S(2)}, u32[]{:S(2)}) collective-permute-start(bf16[144,256]{1,0:T(8,128)(2,1)S(1)} %get-tuple-element.25), channel_id=1, source_target_pairs={{0,4},{2,6},{4,0},{6,2},{8,12},{10,14},{12,8},{14,10},{16,20},{18,... | collective-permute-start | bytes 221192 | tf_op jit(solution)/shard_map/ppermute | solution.py:395
  8.3 0.0 collective-permute-start.2
  8.4 0.0 copy-done.2
  8.4 0.0 copy-done.1
  8.4 0.0 copy-done
  8.4 1.2 %leaf_backward.1 = (f32[768,256]{1,0:T(8,128)S(1)}, bf16[768,480]{1,0:T(8,128)(2,1)S(1)}) custom-call(bf16[768,768]{1,0:T(8,128)(2,1)S(1)} %bitcast.14, bf16[512,768]{1,0:T(8,128)(2,1)S(1)} %bitcast.16, s32[1,512]{1,0:T(1,128)S(1)} %bitcast.18, bf16[768,256]{1,0:T(8,128)(2,1)S(1)} %get-tuple-element.30.half_ref), custom_call_target="tpu_custom_call" | custom-call | flops 1000000000 | bytes 2361344 | tf_op jit(solution)/shard_map/leaf_backward/pallas_call | solution.py:30
  9.6 0.1 collective-permute-done.b
  9.7 1.5 %collective-permute-done.1.c = bf16[144,256]{1,0:T(8,128)(2,1)S(1)} collective-permute-done((bf16[144,256]{1,0:T(8,128)(2,1)S(1)}, bf16[144,256]{1,0:T(8,128)(2,1)S(1)}, u32[]{:S(2)}, u32[]{:S(2)}) %collective-permute-start.1) | collective-permute-done | bytes 73760 | tf_op jit(solution)/shard_map/ppermute | solution.py:395
  11.2 2.4 %collective-permute-done.2.d = bf16[144,256]{1,0:T(8,128)(2,1)S(1)} collective-permute-done((bf16[144,256]{1,0:T(8,128)(2,1)S(1)}, bf16[144,256]{1,0:T(8,128)(2,1)S(1)}, u32[]{:S(2)}, u32[]{:S(2)}) %collective-permute-start.2) | collective-permute-done | bytes 73760 | tf_op jit(solution)/shard_map/ppermute | solution.py:395
  13.6 0.0 collective-permute-done.3.far_pack_ref.far_ref
  13.6 0.3 plane_sum.1
  13.9 3.7 %collective-permute-start.6 = (bf16[128,256]{1,0:T(8,128)(2,1)S(1)}, bf16[128,256]{1,0:T(8,128)(2,1)S(1)}, u32[]{:S(2)}, u32[]{:S(2)}) collective-permute-start(bf16[128,256]{1,0:T(8,128)(2,1)S(1)} %get-tuple-element.28), channel_id=1, source_target_pairs={{0,24},{2,26},{4,28},{6,30},{8,16},{10,18},{12,20},{14,22},{16,8},... | collective-permute-start | bytes 196616 | tf_op jit(solution)/shard_map/ppermute | solution.py:395
  17.5 0.0 collective-permute-start.5
  17.5 0.8 %collective-permute-start.4 = (bf16[128,256]{1,0:T(8,128)(2,1)S(1)}, bf16[128,256]{1,0:T(8,128)(2,1)S(1)}, u32[]{:S(2)}, u32[]{:S(2)}) collective-permute-start(bf16[128,256]{1,0:T(8,128)(2,1)S(1)} %get-tuple-element.28), channel_id=1, source_target_pairs={{0,8},{2,10},{4,12},{6,14},{8,0},{10,2},{12,4},{14,6},{16,24},{18,... | collective-permute-start | bytes 196616 | tf_op jit(solution)/shard_map/ppermute | solution.py:395
  18.3 0.0 collective-permute-start.7
  18.3 2.9 %solve_operator.1 = (bf16[1248,544]{1,0:T(8,128)(2,1)S(1)}, bf16[1248,544]{1,0:T(8,128)(2,1)S(1)}) custom-call(bf16[544,512]{1,0:T(8,128)(2,1)S(1)} %get-tuple-element.27.pack_ref.own_ref, bf16[544,512]{1,0:T(8,128)(2,1)S(1)} %collective-permute-done.3.far_pack_ref.far_ref, bf16[768,480]{1,0:T(8,128)(2,1)S(1)} %get-tuple-element.32.lift_ref), custom_call_target="tpu_custom_call" | custom-call | flops 2000000000 | bytes 1851392 | tf_op jit(solution)/shard_map/solve_operator/pallas_call | solution.py:30
  21.2 0.0 collective-permute-done.7.far_low_ref
  21.2 0.0 collective-permute-done.6
  21.2 1.6 %collective-permute-done.5 = bf16[128,256]{1,0:T(8,128)(2,1)S(1)} collective-permute-done((bf16[128,256]{1,0:T(8,128)(2,1)S(1)}, bf16[128,256]{1,0:T(8,128)(2,1)S(1)}, u32[]{:S(2)}, u32[]{:S(2)}) %collective-permute-start.5) | collective-permute-done | bytes 65568 | tf_op jit(solution)/shard_map/ppermute | solution.py:395
  22.8 0.0 collective-permute-done.4
  22.8 0.7 %collective-permute-start.10 = (bf16[128,256]{1,0:T(8,128)(2,1)S(1)}, bf16[128,256]{1,0:T(8,128)(2,1)S(1)}, u32[]{:S(2)}, u32[]{:S(2)}) collective-permute-start(bf16[128,256]{1,0:T(8,128)(2,1)S(1)} %add_convert_fusion), channel_id=1, source_target_pairs={{0,6},{2,4},{4,2},{6,0},{8,14},{10,12},{12,10},{14,8},{16,22},{18,... | collective-permute-start | bytes 196616 | tf_op jit(solution)/shard_map/ppermute | solution.py:395
  23.6 1.4 %collective-permute-start.9 = (bf16[128,256]{1,0:T(8,128)(2,1)S(1)}, bf16[128,256]{1,0:T(8,128)(2,1)S(1)}, u32[]{:S(2)}, u32[]{:S(2)}) collective-permute-start(bf16[128,256]{1,0:T(8,128)(2,1)S(1)} %add_convert_fusion), channel_id=1, source_target_pairs={{0,4},{2,6},{4,0},{6,2},{8,12},{10,14},{12,8},{14,10},{16,20},{18,... | collective-permute-start | bytes 196616 | tf_op jit(solution)/shard_map/ppermute | solution.py:395
  25.0 1.4 %collective-permute-start.8 = (bf16[128,256]{1,0:T(8,128)(2,1)S(1)}, bf16[128,256]{1,0:T(8,128)(2,1)S(1)}, u32[]{:S(2)}, u32[]{:S(2)}) collective-permute-start(bf16[128,256]{1,0:T(8,128)(2,1)S(1)} %add_convert_fusion), channel_id=1, source_target_pairs={{0,2},{2,0},{4,6},{6,4},{8,10},{10,8},{12,14},{14,12},{16,18},{18,... | collective-permute-start | bytes 196616 | tf_op jit(solution)/shard_map/ppermute | solution.py:395
  26.4 1.8 %collective-permute-done.10 = bf16[128,256]{1,0:T(8,128)(2,1)S(1)} collective-permute-done((bf16[128,256]{1,0:T(8,128)(2,1)S(1)}, bf16[128,256]{1,0:T(8,128)(2,1)S(1)}, u32[]{:S(2)}, u32[]{:S(2)}) %collective-permute-start.10) | collective-permute-done | bytes 65568 | tf_op jit(solution)/shard_map/ppermute | solution.py:395
  28.2 0.4 %collective-permute-done.9 = bf16[128,256]{1,0:T(8,128)(2,1)S(1)} collective-permute-done((bf16[128,256]{1,0:T(8,128)(2,1)S(1)}, bf16[128,256]{1,0:T(8,128)(2,1)S(1)}, u32[]{:S(2)}, u32[]{:S(2)}) %collective-permute-start.9) | collective-permute-done | bytes 65568 | tf_op jit(solution)/shard_map/ppermute | solution.py:395
  28.5 0.7 %collective-permute-done.8 = bf16[128,256]{1,0:T(8,128)(2,1)S(1)} collective-permute-done((bf16[128,256]{1,0:T(8,128)(2,1)S(1)}, bf16[128,256]{1,0:T(8,128)(2,1)S(1)}, u32[]{:S(2)}, u32[]{:S(2)}) %collective-permute-start.8) | collective-permute-done | bytes 65568 | tf_op jit(solution)/shard_map/ppermute | solution.py:395
  29.3 0.1 collective-permute-start.11
  29.4 0.8 %own_part.1.own_ref = f32[1248,256]{1,0:T(8,128)S(1)} custom-call(bf16[512,256]{1,0:T(8,128)(2,1)S(1)} %pad_maximum_fusion.shared_ref, bf16[32,256]{1,0:T(8,128)(2,1)S(1)} %get-tuple-element.29.low_ref, bf16[32,256]{1,0:T(8,128)(2,1)S(1)} %collective-permute-done.7.far_low_ref, bf16[1248,544]{1,0:T(8,128)(2,1)S(1)} %get-tuple-element.40.solve_ref, ...), custom_call_target="tpu_custom_call" | custom-call | flops 400000000 | bytes 3796992 | tf_op jit(solution)/shard_map/own_part/pallas_call | solution.py:30
  30.2 0.7 %collective-permute-done.11.shared_ref = bf16[512,256]{1,0:T(8,128)(2,1)S(1)} collective-permute-done((bf16[512,256]{1,0:T(8,128)(2,1)S(1)}, bf16[512,256]{1,0:T(8,128)(2,1)S(1)}, u32[]{:S(2)}, u32[]{:S(2)}) %collective-permute-start.11) | collective-permute-done | bytes 262176 | tf_op jit(solution)/shard_map/ppermute | solution.py:391
  30.9 1.2 %finish.1 = (bf16[768,256]{1,0:T(8,128)(2,1)}, bf16[480,256]{1,0:T(8,128)(2,1)}) custom-call(bf16[512,256]{1,0:T(8,128)(2,1)S(1)} %collective-permute-done.11.shared_ref, bf16[1248,544]{1,0:T(8,128)(2,1)S(1)} %get-tuple-element.38.far_ref.solve_ref, f32[1248,256]{1,0:T(8,128)S(1)} %own_part.1.own_ref), custom_call_target="tpu_custom_call" | custom-call | flops 400000000 | bytes 2897920 | tf_op jit(solution)/shard_map/finish/pallas_call | solution.py:30
  (2 shorter events, 0.1 us)
Async XLA Ops:
  0.6 7.7 %copy-start.2 = (s32[1,1,512]{2,1,0:T(1,128)S(1)}, s32[1,1,512]{2,1,0:T(1,128)}, u32[]{:S(2)}) copy-start(s32[1,1,512]{2,1,0:T(1,128)} %param.14) | copy-start | bytes 6148
  0.6 7.7 %copy-start.1 = (bf16[1,1,512,768]{3,2,1,0:T(8,128)(2,1)S(1)}, bf16[1,1,512,768]{3,2,1,0:T(8,128)(2,1)}, u32[]{:S(2)}) copy-start(bf16[1,1,512,768]{3,2,1,0:T(8,128)(2,1)} %param.13) | copy-start | bytes 2359300
  0.7 7.7 %copy-start = (bf16[1,1,768,768]{3,2,1,0:T(8,128)(2,1)S(1)}, bf16[1,1,768,768]{3,2,1,0:T(8,128)(2,1)}, u32[]{:S(2)}) copy-start(bf16[1,1,768,768]{3,2,1,0:T(8,128)(2,1)} %param.12) | copy-start | bytes 3538948
  3.7 9.9 %collective-permute-start.3 = (bf16[544,512]{1,0:T(8,128)(2,1)S(1)}, bf16[544,512]{1,0:T(8,128)(2,1)S(1)}, u32[]{:S(2)}, u32[]{:S(2)}) collective-permute-start(bf16[544,512]{1,0:T(8,128)(2,1)S(1)} %get-tuple-element.27.pack_ref.own_ref), channel_id=1, source_target_pairs={{0,1},{1,0},{2,3},{3,2},{4,5},{5,4},{6,7},{7,6},{8,9},{9,8},{10,11... | collective-permute-start | bytes 1671176 | tf_op jit(solution)/shard_map/ppermute | solution.py:391
  4.2 5.4 %collective-permute-start = (bf16[144,256]{1,0:T(8,128)(2,1)S(1)}, bf16[144,256]{1,0:T(8,128)(2,1)S(1)}, u32[]{:S(2)}, u32[]{:S(2)}) collective-permute-start(bf16[144,256]{1,0:T(8,128)(2,1)S(1)} %get-tuple-element.24), channel_id=1, source_target_pairs={{0,2},{2,0},{4,6},{6,4},{8,10},{10,8},{12,14},{14,12},{16,18},{18,... | collective-permute-start | bytes 221192 | tf_op jit(solution)/shard_map/ppermute | solution.py:395
  6.8 4.4 %collective-permute-start.1 = (bf16[144,256]{1,0:T(8,128)(2,1)S(1)}, bf16[144,256]{1,0:T(8,128)(2,1)S(1)}, u32[]{:S(2)}, u32[]{:S(2)}) collective-permute-start(bf16[144,256]{1,0:T(8,128)(2,1)S(1)} %get-tuple-element.25), channel_id=1, source_target_pairs={{0,4},{2,6},{4,0},{6,2},{8,12},{10,14},{12,8},{14,10},{16,20},{18,... | collective-permute-start | bytes 221192 | tf_op jit(solution)/shard_map/ppermute | solution.py:395
  8.3 5.3 %collective-permute-start.2 = (bf16[144,256]{1,0:T(8,128)(2,1)S(1)}, bf16[144,256]{1,0:T(8,128)(2,1)S(1)}, u32[]{:S(2)}, u32[]{:S(2)}) collective-permute-start(bf16[144,256]{1,0:T(8,128)(2,1)S(1)} %get-tuple-element.26), channel_id=1, source_target_pairs={{0,6},{2,4},{4,2},{6,0},{8,14},{10,12},{12,10},{14,8},{16,22},{18,... | collective-permute-start | bytes 221192 | tf_op jit(solution)/shard_map/ppermute | solution.py:395
  13.9 7.3 %collective-permute-start.6 = (bf16[128,256]{1,0:T(8,128)(2,1)S(1)}, bf16[128,256]{1,0:T(8,128)(2,1)S(1)}, u32[]{:S(2)}, u32[]{:S(2)}) collective-permute-start(bf16[128,256]{1,0:T(8,128)(2,1)S(1)} %get-tuple-element.28), channel_id=1, source_target_pairs={{0,24},{2,26},{4,28},{6,30},{8,16},{10,18},{12,20},{14,22},{16,8},... | collective-permute-start | bytes 196616 | tf_op jit(solution)/shard_map/ppermute | solution.py:395
  17.5 5.2 %collective-permute-start.5 = (bf16[128,256]{1,0:T(8,128)(2,1)S(1)}, bf16[128,256]{1,0:T(8,128)(2,1)S(1)}, u32[]{:S(2)}, u32[]{:S(2)}) collective-permute-start(bf16[128,256]{1,0:T(8,128)(2,1)S(1)} %get-tuple-element.28), channel_id=1, source_target_pairs={{0,16},{2,18},{4,20},{6,22},{8,24},{10,26},{12,28},{14,30},{16,0},... | collective-permute-start | bytes 196616 | tf_op jit(solution)/shard_map/ppermute | solution.py:395
  17.5 5.2 %collective-permute-start.4 = (bf16[128,256]{1,0:T(8,128)(2,1)S(1)}, bf16[128,256]{1,0:T(8,128)(2,1)S(1)}, u32[]{:S(2)}, u32[]{:S(2)}) collective-permute-start(bf16[128,256]{1,0:T(8,128)(2,1)S(1)} %get-tuple-element.28), channel_id=1, source_target_pairs={{0,8},{2,10},{4,12},{6,14},{8,0},{10,2},{12,4},{14,6},{16,24},{18,... | collective-permute-start | bytes 196616 | tf_op jit(solution)/shard_map/ppermute | solution.py:395
  18.3 2.9 %collective-permute-start.7 = (bf16[32,256]{1,0:T(8,128)(2,1)S(1)}, bf16[32,256]{1,0:T(8,128)(2,1)S(1)}, u32[]{:S(2)}, u32[]{:S(2)}) collective-permute-start(bf16[32,256]{1,0:T(8,128)(2,1)S(1)} %get-tuple-element.29.low_ref), channel_id=1, source_target_pairs={{0,1},{1,0},{2,3},{3,2},{4,5},{5,4},{6,7},{7,6},{8,9},{9,8},{10,11... | collective-permute-start | bytes 49160 | tf_op jit(solution)/shard_map/ppermute | solution.py:391
  22.8 5.3 %collective-permute-start.10 = (bf16[128,256]{1,0:T(8,128)(2,1)S(1)}, bf16[128,256]{1,0:T(8,128)(2,1)S(1)}, u32[]{:S(2)}, u32[]{:S(2)}) collective-permute-start(bf16[128,256]{1,0:T(8,128)(2,1)S(1)} %add_convert_fusion), channel_id=1, source_target_pairs={{0,6},{2,4},{4,2},{6,0},{8,14},{10,12},{12,10},{14,8},{16,22},{18,... | collective-permute-start | bytes 196616 | tf_op jit(solution)/shard_map/ppermute | solution.py:395
  23.6 5.0 %collective-permute-start.9 = (bf16[128,256]{1,0:T(8,128)(2,1)S(1)}, bf16[128,256]{1,0:T(8,128)(2,1)S(1)}, u32[]{:S(2)}, u32[]{:S(2)}) collective-permute-start(bf16[128,256]{1,0:T(8,128)(2,1)S(1)} %add_convert_fusion), channel_id=1, source_target_pairs={{0,4},{2,6},{4,0},{6,2},{8,12},{10,14},{12,8},{14,10},{16,20},{18,... | collective-permute-start | bytes 196616 | tf_op jit(solution)/shard_map/ppermute | solution.py:395
  25.0 4.3 %collective-permute-start.8 = (bf16[128,256]{1,0:T(8,128)(2,1)S(1)}, bf16[128,256]{1,0:T(8,128)(2,1)S(1)}, u32[]{:S(2)}, u32[]{:S(2)}) collective-permute-start(bf16[128,256]{1,0:T(8,128)(2,1)S(1)} %add_convert_fusion), channel_id=1, source_target_pairs={{0,2},{2,0},{4,6},{6,4},{8,10},{10,8},{12,14},{14,12},{16,18},{18,... | collective-permute-start | bytes 196616 | tf_op jit(solution)/shard_map/ppermute | solution.py:395
  29.3 1.6 %collective-permute-start.11 = (bf16[512,256]{1,0:T(8,128)(2,1)S(1)}, bf16[512,256]{1,0:T(8,128)(2,1)S(1)}, u32[]{:S(2)}, u32[]{:S(2)}) collective-permute-start(bf16[512,256]{1,0:T(8,128)(2,1)S(1)} %pad_maximum_fusion.shared_ref), channel_id=1, source_target_pairs={{0,1},{1,0},{2,3},{3,2},{4,5},{5,4},{6,7},{7,6},{8,9},{9,8},{10,11... | collective-permute-start | bytes 786440 | tf_op jit(solution)/shard_map/ppermute | solution.py:391

commit v3 on v2

--- a/solution.py
+++ b/solution.py
@@ -7,6 +7,9 @@
 
 BLOCK = 256
 CHIPS = 4
+IN_PLANE = (3, 1, 2)
+ALONG = (1, 3, 2)
+AROUND = ((2, False), (1, False), (3, True))
 MIB = 1024 * 1024
 VMEM = pl.BlockSpec(memory_space=pltpu.VMEM)
 HBM = pl.BlockSpec(memory_space=pltpu.HBM)
@@ -102,7 +105,7 @@
         copies[0].wait()
         moved = moved_rows(tgt_ref[...], sizes, (CHIPS * part, s3 + s2, s3, 0))
         picks = [scatter_matrix(moved, part, part * (in_plane() ^ k)) for k in range(CHIPS)]
-        picks.append(scatter_matrix(moved, s0, CHIPS * part))
+        picks = jnp.concatenate([*picks, scatter_matrix(moved, s0, CHIPS * part)], 0)
         for i in range(count):
             rows = pl.ds(i * BLOCK, BLOCK)
             cols = pl.ds(0, (i + 1) * BLOCK)
@@ -117,10 +120,10 @@
             else:
                 edge_ref[...] += term
         edge = bf16(edge_ref[...])
-        lowest = bf16(dot(picks[CHIPS], edge))
-        for pick, share in zip(picks, (share0, share1, share2, share3)):
-            share[pl.ds(0, part), :] = bf16(dot(pick, edge))
-            share[pl.ds(part, s0), :] = lowest
+        out = bf16(dot(picks, edge))
+        for k, share in enumerate((share0, share1, share2, share3)):
+            share[pl.ds(0, part), :] = out[k * part : (k + 1) * part]
+            share[pl.ds(part, s0), :] = out[CHIPS * part :]
         for copy in copies[leaf:]:
             copy.wait()
         pack_ref[pl.ds(2 * s3, s0), pl.ds(0, o0)] = small0[...]
@@ -203,14 +206,21 @@
     return bf16(jnp.where((i - j == cols // 2) | (j - i == cols // 2), 1.0, 0.0))
 
 
-def solve_operator(pack, far_pack, lift, separators, parents):
+def solve_operator(pack, far_pack, separators, parents):
     s = [m.shape[0] for m in separators]
     o = [m.shape[1] for m in separators]
     total = sum(s)
-    inner = lift.shape[0]
-    width = sum(s) + s[1]
-
-    def kernel(own_ref, far_ref, lift_ref, out_ref, far_out_ref):
+    part, side = share_rows(s)
+    width = CHIPS * (part + side)
+
+    def share_order():
+        i = lax.broadcasted_iota(jnp.int32, (width, width), 0)
+        j = lax.broadcasted_iota(jnp.int32, (width, width), 1)
+        q, r = j // (part + side), j % (part + side)
+        from_ = jnp.where(r < part, q * part + r, CHIPS * part + q * side + r - part)
+        return bf16(jnp.where(i == from_, 1.0, 0.0))
+
+    def kernel(own_ref, far_ref, out_ref, far_out_ref, low_ref, levels, far_levels):
         first = lax.axis_index("sep") == 0
 
         def whole(row, rows, col, cols):
@@ -251,32 +261,60 @@
         m0 = turned(x0, 1.0)
         top, mid, low = s[3], s[3] + s[2], s[3] + s[2] + s[1]
         a3 = bf16(dot(m3, x3))
-        out_ref[pl.ds(0, total), pl.ds(0, top)] = a3[:, :top]
-        far_out_ref[pl.ds(0, total), pl.ds(0, top)] = a3[:, top:]
+        levels[:, pl.ds(0, top)] = a3[:, :top]
+        far_levels[:, pl.ds(0, top)] = a3[:, top:]
         a2 = dot(m3, n32)
         a2 = bf16(jnp.concatenate([a2[:top], a2[top:] + dot(m2, x2)], 0))
-        out_ref[pl.ds(0, total), pl.ds(top, s[2])] = a2[:, : s[2]]
-        far_out_ref[pl.ds(0, total), pl.ds(top, s[2])] = a2[:, s[2] :]
+        levels[:, pl.ds(top, s[2])] = a2[:, : s[2]]
+        far_levels[:, pl.ds(top, s[2])] = a2[:, s[2] :]
         a1 = dot(m3, n31)
         rest = a1[top:] + dot(m2, n21)
         a1 = bf16(jnp.concatenate([a1[:top], rest[: s[2]], rest[s[2] :] + dot(m1, x1)], 0))
-        out_ref[pl.ds(0, total), pl.ds(mid, o[1])] = a1
-        far_out_ref[pl.ds(0, total), pl.ds(mid, o[1])] = bf16(dot(a1, exchange_columns(o[1])))
-        a0 = bf16(dot(m0, x0))
-        for ref, block in ((out_ref, a0), (far_out_ref, bf16(dot(a0, exchange_columns(o[0]))))):
-            ref[pl.ds(0, low), pl.ds(mid + o[1], s[0])] = jnp.zeros((low, s[0]), jnp.bfloat16)
-            ref[pl.ds(low, s[0]), pl.ds(mid + o[1], s[0])] = block[:, : s[0]]
+        levels[:, pl.ds(mid, o[1])] = a1
+        far_levels[:, pl.ds(mid, o[1])] = bf16(dot(a1, exchange_columns(o[1])))
+        order = share_order()
+        out_ref[...] = bf16(dot(levels[...], order))
+        far_out_ref[...] = bf16(dot(far_levels[...], order))
+        low_ref[pl.ds(0, low), :] = jnp.zeros((low, o[0]), jnp.bfloat16)
+        low_ref[pl.ds(low, s[0]), :] = bf16(dot(m0, x0))
+
+    shape = struct((total, width))
+    return call(
+        kernel,
+        "solve_operator",
+        (shape, shape, struct((total, o[0]))),
+        (pack, far_pack),
+        [VMEM] * 2,
+        (VMEM,) * 3,
+        1_000_000_000,
+        scratch=[pltpu.VMEM((total, width), jnp.bfloat16)] * 2,
+    )
+
+
+def correction_operator(solve, far_solve, low_solve, lift, sizes):
+    total, width = solve.shape
+    inner = lift.shape[0]
+    each = sum(share_rows(sizes))
+
+    def kernel(solve_ref, far_ref, low_solve_ref, lift_ref, held_ref, other_ref, low_ref):
+        for i, (mask, own) in enumerate(((0, True), *AROUND)):
+            cols = pl.ds(i * each, each)
+            at = pl.ds(pl.multiple_of((in_plane() ^ mask) * each, each), each)
+            held_ref[pl.ds(0, total), cols] = (solve_ref if own else far_ref)[:, at]
+            other_ref[pl.ds(0, total), cols] = (far_ref if own else solve_ref)[:, at]
+        low_ref[pl.ds(0, total), :] = low_solve_ref[...]
+        for ref in (held_ref, other_ref, low_ref):
             ref[pl.ds(total, inner), :] = bf16(-dot(lift_ref[...], ref[pl.ds(0, total), :]))
 
     shape = struct((total + inner, width))
     return call(
         kernel,
-        "solve_operator",
-        (shape, shape),
-        (pack, far_pack, lift),
-        [VMEM] * 3,
-        (VMEM, VMEM),
-        2_000_000_000,
+        "correction_operator",
+        (shape, shape, struct((total + inner, low_solve.shape[1]))),
+        (solve, far_solve, low_solve, lift),
+        [VMEM] * 4,
+        (VMEM,) * 3,
+        1_000_000_000,
     )
 
 
@@ -309,53 +347,37 @@
     )
 
 
-def collect(rows, shared_ref, sizes):
-    part, side = share_rows(sizes)
-    each = part + side
-    for q in range(CHIPS):
-        at = pl.multiple_of((in_plane() ^ q) * each, each)
-        rows[pl.ds(q * part, part), :] = shared_ref[pl.ds(at, part), :]
-        rows[pl.ds(CHIPS * part + q * side, side), :] = shared_ref[pl.ds(at + part, side), :]
-
-
-def own_part(shared, low, far_low, solve, far_solve, direct, sizes):
-    total, s0 = sum(sizes), sizes[0]
+def own_part(held, low, far_low, operator, low_operator, direct, sizes):
+    total = sum(sizes)
     inner, shots = direct.shape
-    height, width = solve.shape
-    upper = width - s0
-
-    def kernel(shared_ref, low_ref, far_low_ref, solve_ref, far_ref, direct_ref, out_ref, rhs):
-        collect(rhs, shared_ref, sizes)
-        rhs[pl.ds(upper, s0), :] = low_ref[...]
-        sum_ = dot(solve_ref[...], rhs[...]) + dot(far_ref[:, pl.ds(upper, s0)], far_low_ref[...])
-        out_ref[pl.ds(0, total), :] = sum_[:total]
-        out_ref[pl.ds(total, inner), :] = sum_[total:] + direct_ref[...]
+
+    def kernel(held_ref, low_ref, far_low_ref, operator_ref, low_operator_ref, direct_ref, out_ref):
+        low = jnp.concatenate([low_ref[...], far_low_ref[...]], 0)
+        out = dot(operator_ref[...], held_ref[...]) + dot(low_operator_ref[...], low)
+        out_ref[pl.ds(0, total), :] = out[:total]
+        out_ref[pl.ds(total, inner), :] = out[total:] + direct_ref[...]
 
     return call(
         kernel,
         "own_part",
-        struct((height, shots), jnp.float32),
-        (shared, low, far_low, solve, far_solve, direct),
+        struct((total + inner, shots), jnp.float32),
+        (held, low, far_low, operator, low_operator, direct),
         [VMEM] * 6,
         VMEM,
         400_000_000,
-        scratch=[pltpu.VMEM((width, shots), jnp.bfloat16)],
-    )
-
-
-def finish(shared, solve, own, sizes):
+    )
+
+
+def finish(held, operator, own, sizes):
     total = sum(sizes)
-    shots = shared.shape[1]
-    upper = shared.shape[0]
+    shots = held.shape[1]
     inner = own.shape[0] - total
     count = inner // BLOCK
 
-    def kernel(shared_ref, solve_ref, own_ref, inner_hbm, sep_hbm, rhs, inner_buf, sep_buf, sems):
-        collect(rhs, shared_ref, sizes)
-
+    def kernel(held_ref, operator_ref, own_ref, inner_hbm, sep_hbm, inner_buf, sep_buf, sems):
         def block(start, size):
             rows = pl.ds(start, size)
-            return bf16(own_ref[rows, :] + dot(solve_ref[rows, pl.ds(0, upper)], rhs[...]))
+            return bf16(own_ref[rows, :] + dot(operator_ref[rows, :], held_ref[...]))
 
         down = block(0, total)
         for begin, place, size in zip(offsets(sizes), places(sizes), sizes):
@@ -374,12 +396,11 @@
         kernel,
         "finish",
         (struct((inner, shots)), struct((total, shots))),
-        (shared, solve, own),
+        (held, operator, own),
         [VMEM] * 3,
         (HBM, HBM),
         400_000_000,
         scratch=[
-            pltpu.VMEM((upper, shots), jnp.bfloat16),
             pltpu.VMEM((inner, shots), jnp.bfloat16),
             pltpu.VMEM((total, shots), jnp.bfloat16),
             pltpu.SemaphoreType.DMA((count + 1,)),
@@ -393,6 +414,13 @@
 
 def partner(x, mask):
     return lax.ppermute(x, "sub", [(s, s ^ mask) for s in range(lax.axis_size("sub"))])
+
+
+def partner_strip(x, mask):
+    route = []
+    for s in range(lax.axis_size("sub")):
+        route += [(2 * s, 2 * (s ^ mask) + 1), (2 * s + 1, 2 * (s ^ mask))]
+    return lax.ppermute(x, ("sub", "sep"), route)
 
 
 def added(*terms):
@@ -405,18 +433,22 @@
     parents = [m[0] for m in blocks[4:]]
     sizes = [m.shape[0] for m in separators]
     half, *parts, pack = leaf_forward(src, inv, cpl, tgt, separators, parents)
-    pieces = parts[:1] + [partner(parts[k], k) for k in range(1, CHIPS)]
+    pieces = parts[:1] + [partner(parts[k], k) for k in IN_PLANE]
     direct, lift = leaf_backward(inv, cpl, tgt, half, sizes)
     far_pack = other_strip(pack)
     share, low = plane_sum(pieces, pack, far_pack, separators, parents)
     far_low = other_strip(low)
-    solve, far_solve = solve_operator(pack, far_pack, lift, separators, parents)
-    along = [partner(share, CHIPS * k) for k in range(1, CHIPS)]
-    along, far_low, direct, solve, far_solve = lax.optimization_barrier((along, far_low, direct, solve, far_solve))
+    solve = solve_operator(pack, far_pack, separators, parents)
+    along = [partner(share, CHIPS * k) for k in ALONG]
+    along, far_low, direct, lift, solve = lax.optimization_barrier((along, far_low, direct, lift, solve))
     share = added(share, *along)
-    shared = jnp.concatenate([share] + [partner(share, k) for k in range(1, CHIPS)], 0)
-    own = own_part(shared, low, far_low, solve, far_solve, direct, sizes)
-    inner, sep = finish(other_strip(shared), far_solve, own, sizes)
+    operators = correction_operator(*solve, lift, sizes)
+    around = [partner(share, mask) if own else partner_strip(share, mask) for mask, own in AROUND]
+    around, operators = lax.optimization_barrier((around, operators))
+    held_operator, other_operator, low_operator = operators
+    held = jnp.concatenate([share, *around], 0)
+    own = own_part(held, low, far_low, held_operator, low_operator, direct, sizes)
+    inner, sep = finish(other_strip(held), other_operator, own, sizes)
     return (inner[None, None], sep[None, None])
 
 

time: 32.3 us -> 31.5 us (0.975)
  waiting for transfers between devices: 9.15 us -> 8.32 us
  Pallas kernels: 9.51 us -> 9.84 us
    ppermute x9 -> x7, waiting for transfers between devices: 8.45 us -> 6.23 us  [partner(): lax.ppermute(x, 'sub', [(s, s ^ mask) for s in range(lax.axis_size('sub'))])]
    ppermute x0 -> x2, waiting for transfers between devices: none -> 1.35 us  [partner_strip(): return lax.ppermute(x, ('sub', 'sep'), route)]
    ppermute x9 -> x7, starting transfers between devices: 12.1 us -> 10.8 us  [partner(): lax.ppermute(x, 'sub', [(s, s ^ mask) for s in range(lax.axis_size('sub'))])]
    ppermute x0 -> x2, starting transfers between devices: none -> 0.91 us  [partner_strip(): return lax.ppermute(x, ('sub', 'sep'), route)]
    pallas_call x6 -> x7, Pallas kernels: 9.51 us -> 9.84 us  [call(): pl.pallas_call(kernel, out_shape=outs, in_specs=specs, out_specs=out_spec...]
  transfers between devices with their start and end apart: 12 -> 12, of which waited for: 8 -> 8; matrix products, arithmetic and copies ran while one was open for 0% -> 0% of each run, Pallas kernels for 15% -> 17%
where the time goes in v3:
time: 31.5 us; the launch traced here: 31.4 us
  starting transfers between devices  12.4 us (39%)
  Pallas kernels  9.84 us (31%)
  waiting for transfers between devices  8.32 us (26%)
  between operations  0.73 us (2%)
    ppermute x7, starting transfers between devices, partner(): lax.ppermute(x, 'sub', [(s, s ^ mask) for s in range(lax.axis_size('sub'))])  10.8 us
    pallas_call x7, Pallas kernels, call(): pl.pallas_call(kernel, out_shape=outs, in_specs=specs, out_specs=out_spec...  9.84 us
    ppermute x7, waiting for transfers between devices, partner(): lax.ppermute(x, 'sub', [(s, s ^ mask) for s in range(lax.axis_size('sub'))])  6.23 us
    ppermute x2, waiting for transfers between devices, partner_strip(): return lax.ppermute(x, ('sub', 'sep'), route)  1.35 us
    ppermute x2, starting transfers between devices, partner_strip(): return lax.ppermute(x, ('sub', 'sep'), route)  0.91 us
    ppermute x3, starting transfers between devices, other_strip(): return lax.ppermute(x, 'sep', [(0, 1), (1, 0)])  0.74 us
    ppermute x3, waiting for transfers between devices, other_strip(): return lax.ppermute(x, 'sep', [(0, 1), (1, 0)])  0.74 us
  transfers between devices with their start and end apart: 12, of which 8 were waited for; matrix products, arithmetic and copies ran while one was open for 0% of the time, Pallas kernels for 17%

profile of v3, /device:TPU:0, one launch (start us, length us, event | category | flops | bytes accessed | tf_op | source)
XLA Modules:
  0.0 31.4 jit_solution(4230461357306241903)
XLA Ops:
  0.6 0.0 copy-start
  0.6 0.0 copy-start.1
  0.7 0.0 copy-start.2
  0.7 3.0 %leaf_forward.1 = (bf16[768,256]{1,0:T(8,128)(2,1)S(1)}, bf16[144,256]{1,0:T(8,128)(2,1)S(1)}, bf16[144,256]{1,0:T(8,128)(2,1)S(1)}, bf16[144,256]{1,0:T(8,128)(...) custom-call(bf16[768,256]{1,0:T(8,128)(2,1)} %bitcast.19, bf16[768,768]{1,0:T(8,128)(2,1)} %bitcast.13, ...), custom_call_target="tpu_custom_call" | custom-call | flops 600000000 | bytes 2881536 | tf_op jit(solution)/shard_map/leaf_forward/pallas_call | solution.py:33
  3.7 0.5 %collective-permute-start.3 = (bf16[544,512]{1,0:T(8,128)(2,1)S(1)}, bf16[544,512]{1,0:T(8,128)(2,1)S(1)}, u32[]{:S(2)}, u32[]{:S(2)}) collective-permute-start(bf16[544,512]{1,0:T(8,128)(2,1)S(1)} %get-tuple-element.39.pack_ref.own_ref), channel_id=1, source_target_pairs={{0,1},{1,0},{2,3},{3,2},{4,5},{5,4},{6,7},{7,6},{8,9},{9,8},{10,11... | collective-permute-start | bytes 1671176 | tf_op jit(solution)/shard_map/ppermute | solution.py:412
  4.2 3.5 %collective-permute-start = (bf16[144,256]{1,0:T(8,128)(2,1)S(1)}, bf16[144,256]{1,0:T(8,128)(2,1)S(1)}, u32[]{:S(2)}, u32[]{:S(2)}) collective-permute-start(bf16[144,256]{1,0:T(8,128)(2,1)S(1)} %get-tuple-element.36), channel_id=1, source_target_pairs={{0,6},{2,4},{4,2},{6,0},{8,14},{10,12},{12,10},{14,8},{16,22},{18,... | collective-permute-start | bytes 221192 | tf_op jit(solution)/shard_map/ppermute | solution.py:416
  7.7 0.5 %collective-permute-start.1 = (bf16[144,256]{1,0:T(8,128)(2,1)S(1)}, bf16[144,256]{1,0:T(8,128)(2,1)S(1)}, u32[]{:S(2)}, u32[]{:S(2)}) collective-permute-start(bf16[144,256]{1,0:T(8,128)(2,1)S(1)} %get-tuple-element.37), channel_id=1, source_target_pairs={{0,2},{2,0},{4,6},{6,4},{8,10},{10,8},{12,14},{14,12},{16,18},{18,... | collective-permute-start | bytes 221192 | tf_op jit(solution)/shard_map/ppermute | solution.py:416
  8.3 0.1 collective-permute-start.2
  8.4 0.0 copy-done
  8.4 0.0 copy-done.1
  8.4 0.0 copy-done.2
  8.4 1.2 %leaf_backward.1 = (f32[768,256]{1,0:T(8,128)S(1)}, bf16[768,480]{1,0:T(8,128)(2,1)S(1)}) custom-call(bf16[768,768]{1,0:T(8,128)(2,1)S(1)} %bitcast.14, bf16[512,768]{1,0:T(8,128)(2,1)S(1)} %bitcast.16, s32[1,512]{1,0:T(1,128)S(1)} %bitcast.18, bf16[768,256]{1,0:T(8,128)(2,1)S(1)} %get-tuple-element.42.half_ref), custom_call_target="tpu_custom_call" | custom-call | flops 1000000000 | bytes 2361344 | tf_op jit(solution)/shard_map/leaf_backward/pallas_call | solution.py:33
  9.6 1.1 %collective-permute-done.b = bf16[144,256]{1,0:T(8,128)(2,1)S(1)} collective-permute-done((bf16[144,256]{1,0:T(8,128)(2,1)S(1)}, bf16[144,256]{1,0:T(8,128)(2,1)S(1)}, u32[]{:S(2)}, u32[]{:S(2)}) %collective-permute-start) | collective-permute-done | bytes 73760 | tf_op jit(solution)/shard_map/ppermute | solution.py:416
  10.7 1.7 %collective-permute-done.1.c = bf16[144,256]{1,0:T(8,128)(2,1)S(1)} collective-permute-done((bf16[144,256]{1,0:T(8,128)(2,1)S(1)}, bf16[144,256]{1,0:T(8,128)(2,1)S(1)}, u32[]{:S(2)}, u32[]{:S(2)}) %collective-permute-start.1) | collective-permute-done | bytes 73760 | tf_op jit(solution)/shard_map/ppermute | solution.py:416
  12.4 0.2 collective-permute-done.2.d
  12.6 0.0 collective-permute-done.3.far_pack_ref.far_ref
  12.6 0.3 plane_sum.1
  12.9 2.6 %collective-permute-start.6 = (bf16[128,256]{1,0:T(8,128)(2,1)S(1)}, bf16[128,256]{1,0:T(8,128)(2,1)S(1)}, u32[]{:S(2)}, u32[]{:S(2)}) collective-permute-start(bf16[128,256]{1,0:T(8,128)(2,1)S(1)} %get-tuple-element.40), channel_id=1, source_target_pairs={{0,16},{2,18},{4,20},{6,22},{8,24},{10,26},{12,28},{14,30},{16,0},... | collective-permute-start | bytes 196616 | tf_op jit(solution)/shard_map/ppermute | solution.py:416
  15.6 1.4 %collective-permute-start.5 = (bf16[128,256]{1,0:T(8,128)(2,1)S(1)}, bf16[128,256]{1,0:T(8,128)(2,1)S(1)}, u32[]{:S(2)}, u32[]{:S(2)}) collective-permute-start(bf16[128,256]{1,0:T(8,128)(2,1)S(1)} %get-tuple-element.40), channel_id=1, source_target_pairs={{0,24},{2,26},{4,28},{6,30},{8,16},{10,18},{12,20},{14,22},{16,8},... | collective-permute-start | bytes 196616 | tf_op jit(solution)/shard_map/ppermute | solution.py:416
  16.9 0.2 collective-permute-start.4
  17.1 0.0 collective-permute-start.7
  17.1 2.1 %solve_operator.1 = (bf16[480,512]{1,0:T(8,128)(2,1)S(1)}, bf16[480,512]{1,0:T(8,128)(2,1)S(1)}, bf16[480,64]{1,0:T(8,128)(2,1)S(1)}) custom-call(bf16[544,512]{1,0:T(8,128)(2,1)S(1)} %get-tuple-element.39.pack_ref.own_ref, bf16[544,512]{1,0:T(8,128)(2,1)S(1)} %collective-permute-done.3.far_pack_ref.far_ref), custom_call_target="tpu_custom_call" | custom-call | flops 1000000000 | bytes 1114112 | tf_op jit(solution)/shard_map/solve_operator/pallas_call | solution.py:33
  19.3 0.0 collective-permute-done.7.far_low_ref
  19.3 0.0 collective-permute-done.6
  19.3 2.5 %collective-permute-done.5 = bf16[128,256]{1,0:T(8,128)(2,1)S(1)} collective-permute-done((bf16[128,256]{1,0:T(8,128)(2,1)S(1)}, bf16[128,256]{1,0:T(8,128)(2,1)S(1)}, u32[]{:S(2)}, u32[]{:S(2)}) %collective-permute-start.5) | collective-permute-done | bytes 65568 | tf_op jit(solution)/shard_map/ppermute | solution.py:416
  21.8 0.1 collective-permute-done.4
  21.9 2.4 %collective-permute-start.10 = (bf16[128,256]{1,0:T(8,128)(2,1)S(1)}, bf16[128,256]{1,0:T(8,128)(2,1)S(1)}, u32[]{:S(2)}, u32[]{:S(2)}) collective-permute-start(bf16[128,256]{1,0:T(8,128)(2,1)S(1)} %add_convert_fusion), channel_id=1, source_target_pairs={{0,6},{2,4},{4,2},{6,0},{8,14},{10,12},{12,10},{14,8},{16,22},{18,... | collective-permute-start | bytes 196616 | tf_op jit(solution)/shard_map/ppermute | solution.py:416
  24.3 0.0 collective-permute-start.9
  24.3 0.9 %collective-permute-start.8 = (bf16[128,256]{1,0:T(8,128)(2,1)S(1)}, bf16[128,256]{1,0:T(8,128)(2,1)S(1)}, u32[]{:S(2)}, u32[]{:S(2)}) collective-permute-start(bf16[128,256]{1,0:T(8,128)(2,1)S(1)} %add_convert_fusion), channel_id=1, source_target_pairs={{0,5},{1,4},{2,7},{3,6},{4,1},{5,0},{6,3},{7,2},{8,13},{9,12},{10,... | collective-permute-start | bytes 196616 | tf_op jit(solution)/shard_map/ppermute | solution.py:423
  25.2 1.3 %correction_operator.1 = (bf16[1248,512]{1,0:T(8,128)(2,1)S(1)}, bf16[1248,512]{1,0:T(8,128)(2,1)S(1)}, bf16[1248,64]{1,0:T(8,128)(2,1)S(1)}) custom-call(bf16[480,512]{1,0:T(8,128)(2,1)S(1)} %get-tuple-element.51.solve_ref, bf16[480,512]{1,0:T(8,128)(2,1)S(1)} %get-tuple-element.52.far_ref, bf16[480,64]{1,0:T(8,128)(2,1)S(1)} %get-tuple-element.53.low_solve_ref, ...), custom_call_target="tpu_custom_call" | custom-call | flops 1000000000 | bytes 1781760 | tf_op jit(solution)/shard_map/correction_operator/pallas_call | solution.py:33
  26.5 0.6 %collective-permute-done.10 = bf16[128,256]{1,0:T(8,128)(2,1)S(1)} collective-permute-done((bf16[128,256]{1,0:T(8,128)(2,1)S(1)}, bf16[128,256]{1,0:T(8,128)(2,1)S(1)}, u32[]{:S(2)}, u32[]{:S(2)}) %collective-permute-start.10) | collective-permute-done | bytes 65568 | tf_op jit(solution)/shard_map/ppermute | solution.py:416
  27.1 1.4 %collective-permute-done.9 = bf16[128,256]{1,0:T(8,128)(2,1)S(1)} collective-permute-done((bf16[128,256]{1,0:T(8,128)(2,1)S(1)}, bf16[128,256]{1,0:T(8,128)(2,1)S(1)}, u32[]{:S(2)}, u32[]{:S(2)}) %collective-permute-start.9) | collective-permute-done | bytes 65568 | tf_op jit(solution)/shard_map/ppermute | solution.py:423
  28.5 0.0 collective-permute-done.8
  28.5 0.2 collective-permute-start.11
  28.7 0.6 %own_part.1.own_ref = f32[1248,256]{1,0:T(8,128)S(1)} custom-call(bf16[512,256]{1,0:T(8,128)(2,1)S(1)} %pad_maximum_fusion.held_ref, bf16[32,256]{1,0:T(8,128)(2,1)S(1)} %get-tuple-element.41.low_ref, bf16[32,256]{1,0:T(8,128)(2,1)S(1)} %collective-permute-done.7.far_low_ref, bf16[1248,512]{1,0:T(8,128)(2,1)S(1)} %get-tuple-element.63.operator_ref, ...), custom_call_target="tpu_custom_call" | custom-call | flops 400000000 | bytes 2519040 | tf_op jit(solution)/shard_map/own_part/pallas_call | solution.py:33
  29.4 0.7 %collective-permute-done.11.held_ref = bf16[512,256]{1,0:T(8,128)(2,1)S(1)} collective-permute-done((bf16[512,256]{1,0:T(8,128)(2,1)S(1)}, bf16[512,256]{1,0:T(8,128)(2,1)S(1)}, u32[]{:S(2)}, u32[]{:S(2)}) %collective-permute-start.11) | collective-permute-done | bytes 262176 | tf_op jit(solution)/shard_map/ppermute | solution.py:412
  30.1 1.2 %finish.1 = (bf16[768,256]{1,0:T(8,128)(2,1)}, bf16[480,256]{1,0:T(8,128)(2,1)}) custom-call(bf16[512,256]{1,0:T(8,128)(2,1)S(1)} %collective-permute-done.11.held_ref, bf16[1248,512]{1,0:T(8,128)(2,1)S(1)} %get-tuple-element.61.operator_ref, f32[1248,256]{1,0:T(8,128)S(1)} %own_part.1.own_ref), custom_call_target="tpu_custom_call" | custom-call | flops 400000000 | bytes 2818048 | tf_op jit(solution)/shard_map/finish/pallas_call | solution.py:33
  (2 shorter events, 0.1 us)
Async XLA Ops:
  0.6 7.7 %copy-start = (bf16[1,1,768,768]{3,2,1,0:T(8,128)(2,1)S(1)}, bf16[1,1,768,768]{3,2,1,0:T(8,128)(2,1)}, u32[]{:S(2)}) copy-start(bf16[1,1,768,768]{3,2,1,0:T(8,128)(2,1)} %param.12) | copy-start | bytes 3538948
  0.6 7.7 %copy-start.1 = (bf16[1,1,512,768]{3,2,1,0:T(8,128)(2,1)S(1)}, bf16[1,1,512,768]{3,2,1,0:T(8,128)(2,1)}, u32[]{:S(2)}) copy-start(bf16[1,1,512,768]{3,2,1,0:T(8,128)(2,1)} %param.13) | copy-start | bytes 2359300
  0.7 7.7 %copy-start.2 = (s32[1,1,512]{2,1,0:T(1,128)S(1)}, s32[1,1,512]{2,1,0:T(1,128)}, u32[]{:S(2)}) copy-start(s32[1,1,512]{2,1,0:T(1,128)} %param.14) | copy-start | bytes 6148
  3.7 8.9 %collective-permute-start.3 = (bf16[544,512]{1,0:T(8,128)(2,1)S(1)}, bf16[544,512]{1,0:T(8,128)(2,1)S(1)}, u32[]{:S(2)}, u32[]{:S(2)}) collective-permute-start(bf16[544,512]{1,0:T(8,128)(2,1)S(1)} %get-tuple-element.39.pack_ref.own_ref), channel_id=1, source_target_pairs={{0,1},{1,0},{2,3},{3,2},{4,5},{5,4},{6,7},{7,6},{8,9},{9,8},{10,11... | collective-permute-start | bytes 1671176 | tf_op jit(solution)/shard_map/ppermute | solution.py:412
  4.2 6.5 %collective-permute-start = (bf16[144,256]{1,0:T(8,128)(2,1)S(1)}, bf16[144,256]{1,0:T(8,128)(2,1)S(1)}, u32[]{:S(2)}, u32[]{:S(2)}) collective-permute-start(bf16[144,256]{1,0:T(8,128)(2,1)S(1)} %get-tuple-element.36), channel_id=1, source_target_pairs={{0,6},{2,4},{4,2},{6,0},{8,14},{10,12},{12,10},{14,8},{16,22},{18,... | collective-permute-start | bytes 221192 | tf_op jit(solution)/shard_map/ppermute | solution.py:416
  7.7 4.7 %collective-permute-start.1 = (bf16[144,256]{1,0:T(8,128)(2,1)S(1)}, bf16[144,256]{1,0:T(8,128)(2,1)S(1)}, u32[]{:S(2)}, u32[]{:S(2)}) collective-permute-start(bf16[144,256]{1,0:T(8,128)(2,1)S(1)} %get-tuple-element.37), channel_id=1, source_target_pairs={{0,2},{2,0},{4,6},{6,4},{8,10},{10,8},{12,14},{14,12},{16,18},{18,... | collective-permute-start | bytes 221192 | tf_op jit(solution)/shard_map/ppermute | solution.py:416
  8.3 4.4 %collective-permute-start.2 = (bf16[144,256]{1,0:T(8,128)(2,1)S(1)}, bf16[144,256]{1,0:T(8,128)(2,1)S(1)}, u32[]{:S(2)}, u32[]{:S(2)}) collective-permute-start(bf16[144,256]{1,0:T(8,128)(2,1)S(1)} %get-tuple-element.38), channel_id=1, source_target_pairs={{0,4},{2,6},{4,0},{6,2},{8,12},{10,14},{12,8},{14,10},{16,20},{18,... | collective-permute-start | bytes 221192 | tf_op jit(solution)/shard_map/ppermute | solution.py:416
  12.9 6.4 %collective-permute-start.6 = (bf16[128,256]{1,0:T(8,128)(2,1)S(1)}, bf16[128,256]{1,0:T(8,128)(2,1)S(1)}, u32[]{:S(2)}, u32[]{:S(2)}) collective-permute-start(bf16[128,256]{1,0:T(8,128)(2,1)S(1)} %get-tuple-element.40), channel_id=1, source_target_pairs={{0,16},{2,18},{4,20},{6,22},{8,24},{10,26},{12,28},{14,30},{16,0},... | collective-permute-start | bytes 196616 | tf_op jit(solution)/shard_map/ppermute | solution.py:416
  15.6 6.2 %collective-permute-start.5 = (bf16[128,256]{1,0:T(8,128)(2,1)S(1)}, bf16[128,256]{1,0:T(8,128)(2,1)S(1)}, u32[]{:S(2)}, u32[]{:S(2)}) collective-permute-start(bf16[128,256]{1,0:T(8,128)(2,1)S(1)} %get-tuple-element.40), channel_id=1, source_target_pairs={{0,24},{2,26},{4,28},{6,30},{8,16},{10,18},{12,20},{14,22},{16,8},... | collective-permute-start | bytes 196616 | tf_op jit(solution)/shard_map/ppermute | solution.py:416
  16.9 5.0 %collective-permute-start.4 = (bf16[128,256]{1,0:T(8,128)(2,1)S(1)}, bf16[128,256]{1,0:T(8,128)(2,1)S(1)}, u32[]{:S(2)}, u32[]{:S(2)}) collective-permute-start(bf16[128,256]{1,0:T(8,128)(2,1)S(1)} %get-tuple-element.40), channel_id=1, source_target_pairs={{0,8},{2,10},{4,12},{6,14},{8,0},{10,2},{12,4},{14,6},{16,24},{18,... | collective-permute-start | bytes 196616 | tf_op jit(solution)/shard_map/ppermute | solution.py:416
  17.1 2.1 %collective-permute-start.7 = (bf16[32,256]{1,0:T(8,128)(2,1)S(1)}, bf16[32,256]{1,0:T(8,128)(2,1)S(1)}, u32[]{:S(2)}, u32[]{:S(2)}) collective-permute-start(bf16[32,256]{1,0:T(8,128)(2,1)S(1)} %get-tuple-element.41.low_ref), channel_id=1, source_target_pairs={{0,1},{1,0},{2,3},{3,2},{4,5},{5,4},{6,7},{7,6},{8,9},{9,8},{10,11... | collective-permute-start | bytes 49160 | tf_op jit(solution)/shard_map/ppermute | solution.py:412
  21.9 5.2 %collective-permute-start.10 = (bf16[128,256]{1,0:T(8,128)(2,1)S(1)}, bf16[128,256]{1,0:T(8,128)(2,1)S(1)}, u32[]{:S(2)}, u32[]{:S(2)}) collective-permute-start(bf16[128,256]{1,0:T(8,128)(2,1)S(1)} %add_convert_fusion), channel_id=1, source_target_pairs={{0,6},{2,4},{4,2},{6,0},{8,14},{10,12},{12,10},{14,8},{16,22},{18,... | collective-permute-start | bytes 196616 | tf_op jit(solution)/shard_map/ppermute | solution.py:416
  24.3 4.2 %collective-permute-start.9 = (bf16[128,256]{1,0:T(8,128)(2,1)S(1)}, bf16[128,256]{1,0:T(8,128)(2,1)S(1)}, u32[]{:S(2)}, u32[]{:S(2)}) collective-permute-start(bf16[128,256]{1,0:T(8,128)(2,1)S(1)} %add_convert_fusion), channel_id=1, source_target_pairs={{0,3},{1,2},{2,1},{3,0},{4,7},{5,6},{6,5},{7,4},{8,11},{9,10},{10,... | collective-permute-start | bytes 196616 | tf_op jit(solution)/shard_map/ppermute | solution.py:423
  24.3 4.2 %collective-permute-start.8 = (bf16[128,256]{1,0:T(8,128)(2,1)S(1)}, bf16[128,256]{1,0:T(8,128)(2,1)S(1)}, u32[]{:S(2)}, u32[]{:S(2)}) collective-permute-start(bf16[128,256]{1,0:T(8,128)(2,1)S(1)} %add_convert_fusion), channel_id=1, source_target_pairs={{0,5},{1,4},{2,7},{3,6},{4,1},{5,0},{6,3},{7,2},{8,13},{9,12},{10,... | collective-permute-start | bytes 196616 | tf_op jit(solution)/shard_map/ppermute | solution.py:423
  28.5 1.6 %collective-permute-start.11 = (bf16[512,256]{1,0:T(8,128)(2,1)S(1)}, bf16[512,256]{1,0:T(8,128)(2,1)S(1)}, u32[]{:S(2)}, u32[]{:S(2)}) collective-permute-start(bf16[512,256]{1,0:T(8,128)(2,1)S(1)} %pad_maximum_fusion.held_ref), channel_id=1, source_target_pairs={{0,1},{1,0},{2,3},{3,2},{4,5},{5,4},{6,7},{7,6},{8,9},{9,8},{10,11... | collective-permute-start | bytes 786440 | tf_op jit(solution)/shard_map/ppermute | solution.py:412

commit v4 on v3

--- a/solution.py
+++ b/solution.py
@@ -7,8 +7,8 @@
 
 BLOCK = 256
 CHIPS = 4
-IN_PLANE = (3, 1, 2)
-ALONG = (1, 3, 2)
+IN_PLANE = (3, 2, 1)
+ALONG = (3, 2, 1)
 AROUND = ((2, False), (1, False), (3, True))
 MIB = 1024 * 1024
 VMEM = pl.BlockSpec(memory_space=pltpu.VMEM)
@@ -416,6 +416,11 @@
     return lax.ppermute(x, "sub", [(s, s ^ mask) for s in range(lax.axis_size("sub"))])
 
 
+def shifted(x, planes):
+    count = lax.axis_size("sub")
+    return lax.ppermute(x, "sub", [(s, (s + CHIPS * planes) % count) for s in range(count)])
+
+
 def partner_strip(x, mask):
     route = []
     for s in range(lax.axis_size("sub")):
@@ -436,11 +441,12 @@
     pieces = parts[:1] + [partner(parts[k], k) for k in IN_PLANE]
     direct, lift = leaf_backward(inv, cpl, tgt, half, sizes)
     far_pack = other_strip(pack)
+    solve = solve_operator(pack, far_pack, separators, parents)
+    pieces, solve = lax.optimization_barrier((pieces, solve))
     share, low = plane_sum(pieces, pack, far_pack, separators, parents)
     far_low = other_strip(low)
-    solve = solve_operator(pack, far_pack, separators, parents)
-    along = [partner(share, CHIPS * k) for k in ALONG]
-    along, far_low, direct, lift, solve = lax.optimization_barrier((along, far_low, direct, lift, solve))
+    along = [shifted(share, k) for k in ALONG]
+    along, far_low, direct, lift = lax.optimization_barrier((along, far_low, direct, lift))
     share = added(share, *along)
     operators = correction_operator(*solve, lift, sizes)
     around = [partner(share, mask) if own else partner_strip(share, mask) for mask, own in AROUND]

time: 31.5 us -> 31.2 us (level)
  waiting for transfers between devices: 8.32 us -> 5.97 us
  starting transfers between devices: 12.4 us -> 14.6 us
    ppermute x0 -> x3, starting transfers between devices: none -> 5.56 us  [shifted(): lax.ppermute(x, 'sub', [(s, (s + CHIPS * planes) % count) for s in range(...]
    ppermute x7 -> x4, starting transfers between devices: 10.8 us -> 5.74 us  [partner(): lax.ppermute(x, 'sub', [(s, s ^ mask) for s in range(lax.axis_size('sub'))])]
    ppermute x7 -> x4, waiting for transfers between devices: 6.23 us -> 2.77 us  [partner(): lax.ppermute(x, 'sub', [(s, s ^ mask) for s in range(lax.axis_size('sub'))])]
    ppermute x0 -> x3, waiting for transfers between devices: none -> 2.05 us  [shifted(): lax.ppermute(x, 'sub', [(s, (s + CHIPS * planes) % count) for s in range(...]
    ppermute x3, starting transfers between devices: 0.74 us -> 1.6 us  [other_strip(): return lax.ppermute(x, 'sep', [(0, 1), (1, 0)])]
    ppermute x2, starting transfers between devices: 0.91 us -> 1.7 us  [partner_strip(): return lax.ppermute(x, ('sub', 'sep'), route)]
    ppermute x2, waiting for transfers between devices: 1.35 us -> 0.63 us  [partner_strip(): return lax.ppermute(x, ('sub', 'sep'), route)]
  transfers between devices with their start and end apart: 12 -> 12, of which waited for: 8 -> 9; matrix products, arithmetic and copies ran while one was open for 0% -> 0% of each run, Pallas kernels for 17% -> 17%
where the time goes in v4:
time: 31.2 us; the launch traced here: 31.1 us
  starting transfers between devices  14.6 us (47%)
  Pallas kernels  9.7 us (31%)
  waiting for transfers between devices  5.97 us (19%)
  between operations  0.72 us (2%)
    pallas_call x7, Pallas kernels, call(): pl.pallas_call(kernel, out_shape=outs, in_specs=specs, out_specs=out_spec...  9.7 us
    ppermute x4, starting transfers between devices, partner(): lax.ppermute(x, 'sub', [(s, s ^ mask) for s in range(lax.axis_size('sub'))])  5.74 us
    ppermute x3, starting transfers between devices, shifted(): lax.ppermute(x, 'sub', [(s, (s + CHIPS * planes) % count) for s in range(...  5.56 us
    ppermute x4, waiting for transfers between devices, partner(): lax.ppermute(x, 'sub', [(s, s ^ mask) for s in range(lax.axis_size('sub'))])  2.77 us
    ppermute x3, waiting for transfers between devices, shifted(): lax.ppermute(x, 'sub', [(s, (s + CHIPS * planes) % count) for s in range(...  2.05 us
    ppermute x2, starting transfers between devices, partner_strip(): return lax.ppermute(x, ('sub', 'sep'), route)  1.7 us
    ppermute x3, starting transfers between devices, other_strip(): return lax.ppermute(x, 'sep', [(0, 1), (1, 0)])  1.6 us
    ppermute x2, waiting for transfers between devices, partner_strip(): return lax.ppermute(x, ('sub', 'sep'), route)  0.63 us
  transfers between devices with their start and end apart: 12, of which 9 were waited for; matrix products, arithmetic and copies ran while one was open for 0% of the time, Pallas kernels for 17%

profile of v4, /device:TPU:0, one launch (start us, length us, event | category | flops | bytes accessed | tf_op | source)
XLA Modules:
  0.0 31.1 jit_solution(11058091789161649596)
XLA Ops:
  0.6 2.9 %leaf_forward.1 = (bf16[768,256]{1,0:T(8,128)(2,1)S(1)}, bf16[144,256]{1,0:T(8,128)(2,1)S(1)}, bf16[144,256]{1,0:T(8,128)(2,1)S(1)}, bf16[144,256]{1,0:T(8,128)(...) custom-call(bf16[768,256]{1,0:T(8,128)(2,1)} %bitcast.19, bf16[768,768]{1,0:T(8,128)(2,1)} %bitcast.13, ...), custom_call_target="tpu_custom_call" | custom-call | flops 600000000 | bytes 2881536 | tf_op jit(solution)/shard_map/leaf_forward/pallas_call | solution.py:33
  3.5 0.5 %collective-permute-start.3 = (bf16[544,512]{1,0:T(8,128)(2,1)S(1)}, bf16[544,512]{1,0:T(8,128)(2,1)S(1)}, u32[]{:S(2)}, u32[]{:S(2)}) collective-permute-start(bf16[544,512]{1,0:T(8,128)(2,1)S(1)} %get-tuple-element.43.own_ref.pack_ref), channel_id=1, source_target_pairs={{0,1},{1,0},{2,3},{3,2},{4,5},{5,4},{6,7},{7,6},{8,9},{9,8},{10,11... | collective-permute-start | bytes 1671176 | tf_op jit(solution)/shard_map/ppermute | solution.py:412
  4.0 3.5 %collective-permute-start = (bf16[144,256]{1,0:T(8,128)(2,1)S(1)}, bf16[144,256]{1,0:T(8,128)(2,1)S(1)}, u32[]{:S(2)}, u32[]{:S(2)}) collective-permute-start(bf16[144,256]{1,0:T(8,128)(2,1)S(1)} %get-tuple-element.40), channel_id=1, source_target_pairs={{0,6},{2,4},{4,2},{6,0},{8,14},{10,12},{12,10},{14,8},{16,22},{18,... | collective-permute-start | bytes 221192 | tf_op jit(solution)/shard_map/ppermute | solution.py:416
  7.6 0.5 %collective-permute-start.1 = (bf16[144,256]{1,0:T(8,128)(2,1)S(1)}, bf16[144,256]{1,0:T(8,128)(2,1)S(1)}, u32[]{:S(2)}, u32[]{:S(2)}) collective-permute-start(bf16[144,256]{1,0:T(8,128)(2,1)S(1)} %get-tuple-element.41), channel_id=1, source_target_pairs={{0,4},{2,6},{4,0},{6,2},{8,12},{10,14},{12,8},{14,10},{16,20},{18,... | collective-permute-start | bytes 221192 | tf_op jit(solution)/shard_map/ppermute | solution.py:416
  8.1 0.1 collective-permute-start.2
  8.2 0.0 collective-permute-done.3.far_ref.far_pack_ref
  8.2 0.0 copy-start.1
  8.2 2.1 %solve_operator.1 = (bf16[480,512]{1,0:T(8,128)(2,1)S(1)}, bf16[480,512]{1,0:T(8,128)(2,1)S(1)}, bf16[480,64]{1,0:T(8,128)(2,1)S(1)}) custom-call(bf16[544,512]{1,0:T(8,128)(2,1)S(1)} %get-tuple-element.43.own_ref.pack_ref, bf16[544,512]{1,0:T(8,128)(2,1)S(1)} %collective-permute-done.3.far_ref.far_pack_ref), custom_call_target="tpu_custom_call" | custom-call | flops 1000000000 | bytes 1114112 | tf_op jit(solution)/shard_map/solve_operator/pallas_call | solution.py:33
  10.3 0.0 copy-start
  10.3 0.0 copy-start.2
  10.4 0.1 collective-permute-done.b
  10.4 1.6 %collective-permute-done.1.c = bf16[144,256]{1,0:T(8,128)(2,1)S(1)} collective-permute-done((bf16[144,256]{1,0:T(8,128)(2,1)S(1)}, bf16[144,256]{1,0:T(8,128)(2,1)S(1)}, u32[]{:S(2)}, u32[]{:S(2)}) %collective-permute-start.1) | collective-permute-done | bytes 73760 | tf_op jit(solution)/shard_map/ppermute | solution.py:416
  12.0 0.4 %collective-permute-done.2.d = bf16[144,256]{1,0:T(8,128)(2,1)S(1)} collective-permute-done((bf16[144,256]{1,0:T(8,128)(2,1)S(1)}, bf16[144,256]{1,0:T(8,128)(2,1)S(1)}, u32[]{:S(2)}, u32[]{:S(2)}) %collective-permute-start.2) | collective-permute-done | bytes 73760 | tf_op jit(solution)/shard_map/ppermute | solution.py:416
  12.4 0.3 plane_sum.1
  12.7 1.6 %collective-permute-start.6 = (bf16[128,256]{1,0:T(8,128)(2,1)S(1)}, bf16[128,256]{1,0:T(8,128)(2,1)S(1)}, u32[]{:S(2)}, u32[]{:S(2)}) collective-permute-start(bf16[128,256]{1,0:T(8,128)(2,1)S(1)} %get-tuple-element.51), channel_id=1, source_target_pairs={{0,8},{2,10},{4,12},{6,14},{8,16},{10,18},{12,20},{14,22},{16,24},... | collective-permute-start | bytes 196616 | tf_op jit(solution)/shard_map/ppermute | solution.py:421
  14.3 2.6 %collective-permute-start.5 = (bf16[128,256]{1,0:T(8,128)(2,1)S(1)}, bf16[128,256]{1,0:T(8,128)(2,1)S(1)}, u32[]{:S(2)}, u32[]{:S(2)}) collective-permute-start(bf16[128,256]{1,0:T(8,128)(2,1)S(1)} %get-tuple-element.51), channel_id=1, source_target_pairs={{0,16},{2,18},{4,20},{6,22},{8,24},{10,26},{12,28},{14,30},{16,0},... | collective-permute-start | bytes 196616 | tf_op jit(solution)/shard_map/ppermute | solution.py:421
  16.9 1.3 %collective-permute-start.4 = (bf16[128,256]{1,0:T(8,128)(2,1)S(1)}, bf16[128,256]{1,0:T(8,128)(2,1)S(1)}, u32[]{:S(2)}, u32[]{:S(2)}) collective-permute-start(bf16[128,256]{1,0:T(8,128)(2,1)S(1)} %get-tuple-element.51), channel_id=1, source_target_pairs={{0,24},{2,26},{4,28},{6,30},{8,0},{10,2},{12,4},{14,6},{16,8},{18,... | collective-permute-start | bytes 196616 | tf_op jit(solution)/shard_map/ppermute | solution.py:421
  18.3 0.0 collective-permute-start.7
  18.3 0.0 copy-done.1
  18.3 0.0 copy-done
  18.3 0.0 copy-done.2
  18.3 1.2 %leaf_backward.1 = (f32[768,256]{1,0:T(8,128)S(1)}, bf16[768,480]{1,0:T(8,128)(2,1)S(1)}) custom-call(bf16[768,768]{1,0:T(8,128)(2,1)S(1)} %bitcast.14, bf16[512,768]{1,0:T(8,128)(2,1)S(1)} %bitcast.16, s32[1,512]{1,0:T(1,128)S(1)} %bitcast.18, bf16[768,256]{1,0:T(8,128)(2,1)S(1)} %get-tuple-element.53.half_ref), custom_call_target="tpu_custom_call" | custom-call | flops 1000000000 | bytes 2361344 | tf_op jit(solution)/shard_map/leaf_backward/pallas_call | solution.py:33
  19.5 0.0 collective-permute-done.7.far_low_ref
  19.5 0.1 collective-permute-done.6
  19.6 2.0 %collective-permute-done.5 = bf16[128,256]{1,0:T(8,128)(2,1)S(1)} collective-permute-done((bf16[128,256]{1,0:T(8,128)(2,1)S(1)}, bf16[128,256]{1,0:T(8,128)(2,1)S(1)}, u32[]{:S(2)}, u32[]{:S(2)}) %collective-permute-start.5) | collective-permute-done | bytes 65568 | tf_op jit(solution)/shard_map/ppermute | solution.py:421
  21.6 0.0 collective-permute-done.4
  21.6 1.6 %collective-permute-start.10 = (bf16[128,256]{1,0:T(8,128)(2,1)S(1)}, bf16[128,256]{1,0:T(8,128)(2,1)S(1)}, u32[]{:S(2)}, u32[]{:S(2)}) collective-permute-start(bf16[128,256]{1,0:T(8,128)(2,1)S(1)} %add_convert_fusion), channel_id=1, source_target_pairs={{0,6},{2,4},{4,2},{6,0},{8,14},{10,12},{12,10},{14,8},{16,22},{18,... | collective-permute-start | bytes 196616 | tf_op jit(solution)/shard_map/ppermute | solution.py:416
  23.2 0.0 collective-permute-start.9
  23.2 1.7 %collective-permute-start.8 = (bf16[128,256]{1,0:T(8,128)(2,1)S(1)}, bf16[128,256]{1,0:T(8,128)(2,1)S(1)}, u32[]{:S(2)}, u32[]{:S(2)}) collective-permute-start(bf16[128,256]{1,0:T(8,128)(2,1)S(1)} %add_convert_fusion), channel_id=1, source_target_pairs={{0,5},{1,4},{2,7},{3,6},{4,1},{5,0},{6,3},{7,2},{8,13},{9,12},{10,... | collective-permute-start | bytes 196616 | tf_op jit(solution)/shard_map/ppermute | solution.py:428
  24.9 1.3 %correction_operator.1 = (bf16[1248,512]{1,0:T(8,128)(2,1)S(1)}, bf16[1248,512]{1,0:T(8,128)(2,1)S(1)}, bf16[1248,64]{1,0:T(8,128)(2,1)S(1)}) custom-call(bf16[480,512]{1,0:T(8,128)(2,1)S(1)} %get-tuple-element.59.solve_ref, bf16[480,512]{1,0:T(8,128)(2,1)S(1)} %get-tuple-element.60.far_ref, bf16[480,64]{1,0:T(8,128)(2,1)S(1)} %get-tuple-element.61.low_solve_ref, ...), custom_call_target="tpu_custom_call" | custom-call | flops 1000000000 | bytes 1781760 | tf_op jit(solution)/shard_map/correction_operator/pallas_call | solution.py:33
  26.2 0.7 %collective-permute-done.10 = bf16[128,256]{1,0:T(8,128)(2,1)S(1)} collective-permute-done((bf16[128,256]{1,0:T(8,128)(2,1)S(1)}, bf16[128,256]{1,0:T(8,128)(2,1)S(1)}, u32[]{:S(2)}, u32[]{:S(2)}) %collective-permute-start.10) | collective-permute-done | bytes 65568 | tf_op jit(solution)/shard_map/ppermute | solution.py:416
  26.9 0.5 %collective-permute-done.9 = bf16[128,256]{1,0:T(8,128)(2,1)S(1)} collective-permute-done((bf16[128,256]{1,0:T(8,128)(2,1)S(1)}, bf16[128,256]{1,0:T(8,128)(2,1)S(1)}, u32[]{:S(2)}, u32[]{:S(2)}) %collective-permute-start.9) | collective-permute-done | bytes 65568 | tf_op jit(solution)/shard_map/ppermute | solution.py:428
  27.5 0.1 collective-permute-done.8
  27.6 1.1 %collective-permute-start.11 = (bf16[512,256]{1,0:T(8,128)(2,1)S(1)}, bf16[512,256]{1,0:T(8,128)(2,1)S(1)}, u32[]{:S(2)}, u32[]{:S(2)}) collective-permute-start(bf16[512,256]{1,0:T(8,128)(2,1)S(1)} %pad_maximum_fusion.held_ref), channel_id=1, source_target_pairs={{0,1},{1,0},{2,3},{3,2},{4,5},{5,4},{6,7},{7,6},{8,9},{9,8},{10,11... | collective-permute-start | bytes 786440 | tf_op jit(solution)/shard_map/ppermute | solution.py:412
  28.7 0.6 %own_part.1.own_ref = f32[1248,256]{1,0:T(8,128)S(1)} custom-call(bf16[512,256]{1,0:T(8,128)(2,1)S(1)} %pad_maximum_fusion.held_ref, bf16[32,256]{1,0:T(8,128)(2,1)S(1)} %get-tuple-element.52.low_ref, bf16[32,256]{1,0:T(8,128)(2,1)S(1)} %collective-permute-done.7.far_low_ref, bf16[1248,512]{1,0:T(8,128)(2,1)S(1)} %get-tuple-element.71.operator_ref, ...), custom_call_target="tpu_custom_call" | custom-call | flops 400000000 | bytes 2519040 | tf_op jit(solution)/shard_map/own_part/pallas_call | solution.py:33
  29.3 0.5 %collective-permute-done.11.held_ref = bf16[512,256]{1,0:T(8,128)(2,1)S(1)} collective-permute-done((bf16[512,256]{1,0:T(8,128)(2,1)S(1)}, bf16[512,256]{1,0:T(8,128)(2,1)S(1)}, u32[]{:S(2)}, u32[]{:S(2)}) %collective-permute-start.11) | collective-permute-done | bytes 262176 | tf_op jit(solution)/shard_map/ppermute | solution.py:412
  29.8 1.2 %finish.1 = (bf16[768,256]{1,0:T(8,128)(2,1)}, bf16[480,256]{1,0:T(8,128)(2,1)}) custom-call(bf16[512,256]{1,0:T(8,128)(2,1)S(1)} %collective-permute-done.11.held_ref, bf16[1248,512]{1,0:T(8,128)(2,1)S(1)} %get-tuple-element.69.operator_ref, f32[1248,256]{1,0:T(8,128)S(1)} %own_part.1.own_ref), custom_call_target="tpu_custom_call" | custom-call | flops 400000000 | bytes 2818048 | tf_op jit(solution)/shard_map/finish/pallas_call | solution.py:33
  (2 shorter events, 0.1 us)
Async XLA Ops:
  3.5 4.7 %collective-permute-start.3 = (bf16[544,512]{1,0:T(8,128)(2,1)S(1)}, bf16[544,512]{1,0:T(8,128)(2,1)S(1)}, u32[]{:S(2)}, u32[]{:S(2)}) collective-permute-start(bf16[544,512]{1,0:T(8,128)(2,1)S(1)} %get-tuple-element.43.own_ref.pack_ref), channel_id=1, source_target_pairs={{0,1},{1,0},{2,3},{3,2},{4,5},{5,4},{6,7},{7,6},{8,9},{9,8},{10,11... | collective-permute-start | bytes 1671176 | tf_op jit(solution)/shard_map/ppermute | solution.py:412
  4.0 6.4 %collective-permute-start = (bf16[144,256]{1,0:T(8,128)(2,1)S(1)}, bf16[144,256]{1,0:T(8,128)(2,1)S(1)}, u32[]{:S(2)}, u32[]{:S(2)}) collective-permute-start(bf16[144,256]{1,0:T(8,128)(2,1)S(1)} %get-tuple-element.40), channel_id=1, source_target_pairs={{0,6},{2,4},{4,2},{6,0},{8,14},{10,12},{12,10},{14,8},{16,22},{18,... | collective-permute-start | bytes 221192 | tf_op jit(solution)/shard_map/ppermute | solution.py:416
  7.6 4.4 %collective-permute-start.1 = (bf16[144,256]{1,0:T(8,128)(2,1)S(1)}, bf16[144,256]{1,0:T(8,128)(2,1)S(1)}, u32[]{:S(2)}, u32[]{:S(2)}) collective-permute-start(bf16[144,256]{1,0:T(8,128)(2,1)S(1)} %get-tuple-element.41), channel_id=1, source_target_pairs={{0,4},{2,6},{4,0},{6,2},{8,12},{10,14},{12,8},{14,10},{16,20},{18,... | collective-permute-start | bytes 221192 | tf_op jit(solution)/shard_map/ppermute | solution.py:416
  8.1 4.4 %collective-permute-start.2 = (bf16[144,256]{1,0:T(8,128)(2,1)S(1)}, bf16[144,256]{1,0:T(8,128)(2,1)S(1)}, u32[]{:S(2)}, u32[]{:S(2)}) collective-permute-start(bf16[144,256]{1,0:T(8,128)(2,1)S(1)} %get-tuple-element.42), channel_id=1, source_target_pairs={{0,2},{2,0},{4,6},{6,4},{8,10},{10,8},{12,14},{14,12},{16,18},{18,... | collective-permute-start | bytes 221192 | tf_op jit(solution)/shard_map/ppermute | solution.py:416
  8.2 10.1 %copy-start.1 = (bf16[1,1,512,768]{3,2,1,0:T(8,128)(2,1)S(1)}, bf16[1,1,512,768]{3,2,1,0:T(8,128)(2,1)}, u32[]{:S(2)}) copy-start(bf16[1,1,512,768]{3,2,1,0:T(8,128)(2,1)} %param.13) | copy-start | bytes 2359300
  10.3 7.9 %copy-start = (bf16[1,1,768,768]{3,2,1,0:T(8,128)(2,1)S(1)}, bf16[1,1,768,768]{3,2,1,0:T(8,128)(2,1)}, u32[]{:S(2)}) copy-start(bf16[1,1,768,768]{3,2,1,0:T(8,128)(2,1)} %param.12) | copy-start | bytes 3538948
  10.3 7.9 %copy-start.2 = (s32[1,1,512]{2,1,0:T(1,128)S(1)}, s32[1,1,512]{2,1,0:T(1,128)}, u32[]{:S(2)}) copy-start(s32[1,1,512]{2,1,0:T(1,128)} %param.14) | copy-start | bytes 6148
  12.7 6.9 %collective-permute-start.6 = (bf16[128,256]{1,0:T(8,128)(2,1)S(1)}, bf16[128,256]{1,0:T(8,128)(2,1)S(1)}, u32[]{:S(2)}, u32[]{:S(2)}) collective-permute-start(bf16[128,256]{1,0:T(8,128)(2,1)S(1)} %get-tuple-element.51), channel_id=1, source_target_pairs={{0,8},{2,10},{4,12},{6,14},{8,16},{10,18},{12,20},{14,22},{16,24},... | collective-permute-start | bytes 196616 | tf_op jit(solution)/shard_map/ppermute | solution.py:421
  14.3 7.2 %collective-permute-start.5 = (bf16[128,256]{1,0:T(8,128)(2,1)S(1)}, bf16[128,256]{1,0:T(8,128)(2,1)S(1)}, u32[]{:S(2)}, u32[]{:S(2)}) collective-permute-start(bf16[128,256]{1,0:T(8,128)(2,1)S(1)} %get-tuple-element.51), channel_id=1, source_target_pairs={{0,16},{2,18},{4,20},{6,22},{8,24},{10,26},{12,28},{14,30},{16,0},... | collective-permute-start | bytes 196616 | tf_op jit(solution)/shard_map/ppermute | solution.py:421
  16.9 4.7 %collective-permute-start.4 = (bf16[128,256]{1,0:T(8,128)(2,1)S(1)}, bf16[128,256]{1,0:T(8,128)(2,1)S(1)}, u32[]{:S(2)}, u32[]{:S(2)}) collective-permute-start(bf16[128,256]{1,0:T(8,128)(2,1)S(1)} %get-tuple-element.51), channel_id=1, source_target_pairs={{0,24},{2,26},{4,28},{6,30},{8,0},{10,2},{12,4},{14,6},{16,8},{18,... | collective-permute-start | bytes 196616 | tf_op jit(solution)/shard_map/ppermute | solution.py:421
  18.3 1.3 %collective-permute-start.7 = (bf16[32,256]{1,0:T(8,128)(2,1)S(1)}, bf16[32,256]{1,0:T(8,128)(2,1)S(1)}, u32[]{:S(2)}, u32[]{:S(2)}) collective-permute-start(bf16[32,256]{1,0:T(8,128)(2,1)S(1)} %get-tuple-element.52.low_ref), channel_id=1, source_target_pairs={{0,1},{1,0},{2,3},{3,2},{4,5},{5,4},{6,7},{7,6},{8,9},{9,8},{10,11... | collective-permute-start | bytes 49160 | tf_op jit(solution)/shard_map/ppermute | solution.py:412
  21.6 5.3 %collective-permute-start.10 = (bf16[128,256]{1,0:T(8,128)(2,1)S(1)}, bf16[128,256]{1,0:T(8,128)(2,1)S(1)}, u32[]{:S(2)}, u32[]{:S(2)}) collective-permute-start(bf16[128,256]{1,0:T(8,128)(2,1)S(1)} %add_convert_fusion), channel_id=1, source_target_pairs={{0,6},{2,4},{4,2},{6,0},{8,14},{10,12},{12,10},{14,8},{16,22},{18,... | collective-permute-start | bytes 196616 | tf_op jit(solution)/shard_map/ppermute | solution.py:416
  23.2 4.3 %collective-permute-start.9 = (bf16[128,256]{1,0:T(8,128)(2,1)S(1)}, bf16[128,256]{1,0:T(8,128)(2,1)S(1)}, u32[]{:S(2)}, u32[]{:S(2)}) collective-permute-start(bf16[128,256]{1,0:T(8,128)(2,1)S(1)} %add_convert_fusion), channel_id=1, source_target_pairs={{0,3},{1,2},{2,1},{3,0},{4,7},{5,6},{6,5},{7,4},{8,11},{9,10},{10,... | collective-permute-start | bytes 196616 | tf_op jit(solution)/shard_map/ppermute | solution.py:428
  23.2 4.4 %collective-permute-start.8 = (bf16[128,256]{1,0:T(8,128)(2,1)S(1)}, bf16[128,256]{1,0:T(8,128)(2,1)S(1)}, u32[]{:S(2)}, u32[]{:S(2)}) collective-permute-start(bf16[128,256]{1,0:T(8,128)(2,1)S(1)} %add_convert_fusion), channel_id=1, source_target_pairs={{0,5},{1,4},{2,7},{3,6},{4,1},{5,0},{6,3},{7,2},{8,13},{9,12},{10,... | collective-permute-start | bytes 196616 | tf_op jit(solution)/shard_map/ppermute | solution.py:428
  27.6 2.2 %collective-permute-start.11 = (bf16[512,256]{1,0:T(8,128)(2,1)S(1)}, bf16[512,256]{1,0:T(8,128)(2,1)S(1)}, u32[]{:S(2)}, u32[]{:S(2)}) collective-permute-start(bf16[512,256]{1,0:T(8,128)(2,1)S(1)} %pad_maximum_fusion.held_ref), channel_id=1, source_target_pairs={{0,1},{1,0},{2,3},{3,2},{4,5},{5,4},{6,7},{7,6},{8,9},{9,8},{10,11... | collective-permute-start | bytes 786440 | tf_op jit(solution)/shard_map/ppermute | solution.py:412

commit v5 on v4

--- a/solution.py
+++ b/solution.py
@@ -9,7 +9,7 @@
 CHIPS = 4
 IN_PLANE = (3, 2, 1)
 ALONG = (3, 2, 1)
-AROUND = ((2, False), (1, False), (3, True))
+AROUND = ((1, False), (3, True), (2, False))
 MIB = 1024 * 1024
 VMEM = pl.BlockSpec(memory_space=pltpu.VMEM)
 HBM = pl.BlockSpec(memory_space=pltpu.HBM)

time: 31.2 us -> 31.2 us (level)
  waiting for transfers between devices: 5.97 us -> 7 us
  starting transfers between devices: 14.6 us -> 13.6 us
    ppermute x3, starting transfers between devices: 1.6 us -> 0.86 us  [other_strip(): return lax.ppermute(x, 'sep', [(0, 1), (1, 0)])]
    ppermute x2, starting transfers between devices: 1.7 us -> 0.97 us  [partner_strip(): return lax.ppermute(x, ('sub', 'sep'), route)]
    ppermute x2, waiting for transfers between devices: 0.63 us -> 1.22 us  [partner_strip(): return lax.ppermute(x, ('sub', 'sep'), route)]
    ppermute x4, starting transfers between devices: 5.74 us -> 6.19 us  [partner(): lax.ppermute(x, 'sub', [(s, s ^ mask) for s in range(lax.axis_size('sub'))])]
    ppermute x4, waiting for transfers between devices: 2.77 us -> 3.11 us  [partner(): lax.ppermute(x, 'sub', [(s, s ^ mask) for s in range(lax.axis_size('sub'))])]
  transfers between devices with their start and end apart: 12 -> 12, of which waited for: 9 -> 8; matrix products, arithmetic and copies ran while one was open for 0% -> 0% of each run, Pallas kernels for 17% -> 17%
where the time goes in v5:
time: 31.2 us; the launch traced here: 31.1 us
  starting transfers between devices  13.6 us (44%)
  Pallas kernels  9.7 us (31%)
  waiting for transfers between devices  7 us (22%)
  between operations  0.73 us (2%)
    pallas_call x7, Pallas kernels, call(): pl.pallas_call(kernel, out_shape=outs, in_specs=specs, out_specs=out_spec...  9.7 us
    ppermute x4, starting transfers between devices, partner(): lax.ppermute(x, 'sub', [(s, s ^ mask) for s in range(lax.axis_size('sub'))])  6.19 us
    ppermute x3, starting transfers between devices, shifted(): lax.ppermute(x, 'sub', [(s, (s + CHIPS * planes) % count) for s in range(...  5.56 us
    ppermute x4, waiting for transfers between devices, partner(): lax.ppermute(x, 'sub', [(s, s ^ mask) for s in range(lax.axis_size('sub'))])  3.11 us
    ppermute x3, waiting for transfers between devices, shifted(): lax.ppermute(x, 'sub', [(s, (s + CHIPS * planes) % count) for s in range(...  2.05 us
    ppermute x2, waiting for transfers between devices, partner_strip(): return lax.ppermute(x, ('sub', 'sep'), route)  1.22 us
    ppermute x2, starting transfers between devices, partner_strip(): return lax.ppermute(x, ('sub', 'sep'), route)  0.97 us
    ppermute x3, starting transfers between devices, other_strip(): return lax.ppermute(x, 'sep', [(0, 1), (1, 0)])  0.86 us
  transfers between devices with their start and end apart: 12, of which 8 were waited for; matrix products, arithmetic and copies ran while one was open for 0% of the time, Pallas kernels for 17%

profile of v5, /device:TPU:0, one launch (start us, length us, event | category | flops | bytes accessed | tf_op | source)
XLA Modules:
  0.0 31.1 jit_solution(7788379594700002288)
XLA Ops:
  0.6 2.9 %leaf_forward.1 = (bf16[768,256]{1,0:T(8,128)(2,1)S(1)}, bf16[144,256]{1,0:T(8,128)(2,1)S(1)}, bf16[144,256]{1,0:T(8,128)(2,1)S(1)}, bf16[144,256]{1,0:T(8,128)(...) custom-call(bf16[768,256]{1,0:T(8,128)(2,1)} %bitcast.19, bf16[768,768]{1,0:T(8,128)(2,1)} %bitcast.13, ...), custom_call_target="tpu_custom_call" | custom-call | flops 600000000 | bytes 2881536 | tf_op jit(solution)/shard_map/leaf_forward/pallas_call | solution.py:33
  3.5 0.5 %collective-permute-start.3 = (bf16[544,512]{1,0:T(8,128)(2,1)S(1)}, bf16[544,512]{1,0:T(8,128)(2,1)S(1)}, u32[]{:S(2)}, u32[]{:S(2)}) collective-permute-start(bf16[544,512]{1,0:T(8,128)(2,1)S(1)} %get-tuple-element.43.own_ref.pack_ref), channel_id=1, source_target_pairs={{0,1},{1,0},{2,3},{3,2},{4,5},{5,4},{6,7},{7,6},{8,9},{9,8},{10,11... | collective-permute-start | bytes 1671176 | tf_op jit(solution)/shard_map/ppermute | solution.py:412
  4.0 3.5 %collective-permute-start = (bf16[144,256]{1,0:T(8,128)(2,1)S(1)}, bf16[144,256]{1,0:T(8,128)(2,1)S(1)}, u32[]{:S(2)}, u32[]{:S(2)}) collective-permute-start(bf16[144,256]{1,0:T(8,128)(2,1)S(1)} %get-tuple-element.40), channel_id=1, source_target_pairs={{0,6},{2,4},{4,2},{6,0},{8,14},{10,12},{12,10},{14,8},{16,22},{18,... | collective-permute-start | bytes 221192 | tf_op jit(solution)/shard_map/ppermute | solution.py:416
  7.6 0.5 %collective-permute-start.1 = (bf16[144,256]{1,0:T(8,128)(2,1)S(1)}, bf16[144,256]{1,0:T(8,128)(2,1)S(1)}, u32[]{:S(2)}, u32[]{:S(2)}) collective-permute-start(bf16[144,256]{1,0:T(8,128)(2,1)S(1)} %get-tuple-element.41), channel_id=1, source_target_pairs={{0,4},{2,6},{4,0},{6,2},{8,12},{10,14},{12,8},{14,10},{16,20},{18,... | collective-permute-start | bytes 221192 | tf_op jit(solution)/shard_map/ppermute | solution.py:416
  8.1 0.1 collective-permute-start.2
  8.2 0.0 collective-permute-done.3.far_ref.far_pack_ref
  8.2 0.0 copy-start.1
  8.2 2.1 %solve_operator.1 = (bf16[480,512]{1,0:T(8,128)(2,1)S(1)}, bf16[480,512]{1,0:T(8,128)(2,1)S(1)}, bf16[480,64]{1,0:T(8,128)(2,1)S(1)}) custom-call(bf16[544,512]{1,0:T(8,128)(2,1)S(1)} %get-tuple-element.43.own_ref.pack_ref, bf16[544,512]{1,0:T(8,128)(2,1)S(1)} %collective-permute-done.3.far_ref.far_pack_ref), custom_call_target="tpu_custom_call" | custom-call | flops 1000000000 | bytes 1114112 | tf_op jit(solution)/shard_map/solve_operator/pallas_call | solution.py:33
  10.3 0.0 copy-start
  10.3 0.0 copy-start.2
  10.4 0.1 collective-permute-done.b
  10.4 1.6 %collective-permute-done.1.c = bf16[144,256]{1,0:T(8,128)(2,1)S(1)} collective-permute-done((bf16[144,256]{1,0:T(8,128)(2,1)S(1)}, bf16[144,256]{1,0:T(8,128)(2,1)S(1)}, u32[]{:S(2)}, u32[]{:S(2)}) %collective-permute-start.1) | collective-permute-done | bytes 73760 | tf_op jit(solution)/shard_map/ppermute | solution.py:416
  12.0 0.4 %collective-permute-done.2.d = bf16[144,256]{1,0:T(8,128)(2,1)S(1)} collective-permute-done((bf16[144,256]{1,0:T(8,128)(2,1)S(1)}, bf16[144,256]{1,0:T(8,128)(2,1)S(1)}, u32[]{:S(2)}, u32[]{:S(2)}) %collective-permute-start.2) | collective-permute-done | bytes 73760 | tf_op jit(solution)/shard_map/ppermute | solution.py:416
  12.4 0.3 plane_sum.1
  12.7 1.6 %collective-permute-start.6 = (bf16[128,256]{1,0:T(8,128)(2,1)S(1)}, bf16[128,256]{1,0:T(8,128)(2,1)S(1)}, u32[]{:S(2)}, u32[]{:S(2)}) collective-permute-start(bf16[128,256]{1,0:T(8,128)(2,1)S(1)} %get-tuple-element.51), channel_id=1, source_target_pairs={{0,8},{2,10},{4,12},{6,14},{8,16},{10,18},{12,20},{14,22},{16,24},... | collective-permute-start | bytes 196616 | tf_op jit(solution)/shard_map/ppermute | solution.py:421
  14.3 2.6 %collective-permute-start.5 = (bf16[128,256]{1,0:T(8,128)(2,1)S(1)}, bf16[128,256]{1,0:T(8,128)(2,1)S(1)}, u32[]{:S(2)}, u32[]{:S(2)}) collective-permute-start(bf16[128,256]{1,0:T(8,128)(2,1)S(1)} %get-tuple-element.51), channel_id=1, source_target_pairs={{0,16},{2,18},{4,20},{6,22},{8,24},{10,26},{12,28},{14,30},{16,0},... | collective-permute-start | bytes 196616 | tf_op jit(solution)/shard_map/ppermute | solution.py:421
  16.9 1.3 %collective-permute-start.4 = (bf16[128,256]{1,0:T(8,128)(2,1)S(1)}, bf16[128,256]{1,0:T(8,128)(2,1)S(1)}, u32[]{:S(2)}, u32[]{:S(2)}) collective-permute-start(bf16[128,256]{1,0:T(8,128)(2,1)S(1)} %get-tuple-element.51), channel_id=1, source_target_pairs={{0,24},{2,26},{4,28},{6,30},{8,0},{10,2},{12,4},{14,6},{16,8},{18,... | collective-permute-start | bytes 196616 | tf_op jit(solution)/shard_map/ppermute | solution.py:421
  18.3 0.0 collective-permute-start.7
  18.3 0.0 copy-done.1
  18.3 0.0 copy-done
  18.3 0.0 copy-done.2
  18.3 1.2 %leaf_backward.1 = (f32[768,256]{1,0:T(8,128)S(1)}, bf16[768,480]{1,0:T(8,128)(2,1)S(1)}) custom-call(bf16[768,768]{1,0:T(8,128)(2,1)S(1)} %bitcast.14, bf16[512,768]{1,0:T(8,128)(2,1)S(1)} %bitcast.16, s32[1,512]{1,0:T(1,128)S(1)} %bitcast.18, bf16[768,256]{1,0:T(8,128)(2,1)S(1)} %get-tuple-element.53.half_ref), custom_call_target="tpu_custom_call" | custom-call | flops 1000000000 | bytes 2361344 | tf_op jit(solution)/shard_map/leaf_backward/pallas_call | solution.py:33
  19.5 0.0 collective-permute-done.7.far_low_ref
  19.5 0.1 collective-permute-done.6
  19.6 2.0 %collective-permute-done.5 = bf16[128,256]{1,0:T(8,128)(2,1)S(1)} collective-permute-done((bf16[128,256]{1,0:T(8,128)(2,1)S(1)}, bf16[128,256]{1,0:T(8,128)(2,1)S(1)}, u32[]{:S(2)}, u32[]{:S(2)}) %collective-permute-start.5) | collective-permute-done | bytes 65568 | tf_op jit(solution)/shard_map/ppermute | solution.py:421
  21.6 0.0 collective-permute-done.4
  21.6 0.1 collective-permute-start.10
  21.8 2.0 %collective-permute-start.9 = (bf16[128,256]{1,0:T(8,128)(2,1)S(1)}, bf16[128,256]{1,0:T(8,128)(2,1)S(1)}, u32[]{:S(2)}, u32[]{:S(2)}) collective-permute-start(bf16[128,256]{1,0:T(8,128)(2,1)S(1)} %add_convert_fusion), channel_id=1, source_target_pairs={{0,6},{2,4},{4,2},{6,0},{8,14},{10,12},{12,10},{14,8},{16,22},{18,... | collective-permute-start | bytes 196616 | tf_op jit(solution)/shard_map/ppermute | solution.py:416
  23.8 0.8 %collective-permute-start.8 = (bf16[128,256]{1,0:T(8,128)(2,1)S(1)}, bf16[128,256]{1,0:T(8,128)(2,1)S(1)}, u32[]{:S(2)}, u32[]{:S(2)}) collective-permute-start(bf16[128,256]{1,0:T(8,128)(2,1)S(1)} %add_convert_fusion), channel_id=1, source_target_pairs={{0,3},{1,2},{2,1},{3,0},{4,7},{5,6},{6,5},{7,4},{8,11},{9,10},{10,... | collective-permute-start | bytes 196616 | tf_op jit(solution)/shard_map/ppermute | solution.py:428
  24.6 1.3 %correction_operator.1 = (bf16[1248,512]{1,0:T(8,128)(2,1)S(1)}, bf16[1248,512]{1,0:T(8,128)(2,1)S(1)}, bf16[1248,64]{1,0:T(8,128)(2,1)S(1)}) custom-call(bf16[480,512]{1,0:T(8,128)(2,1)S(1)} %get-tuple-element.59.solve_ref, bf16[480,512]{1,0:T(8,128)(2,1)S(1)} %get-tuple-element.60.far_ref, bf16[480,64]{1,0:T(8,128)(2,1)S(1)} %get-tuple-element.61.low_solve_ref, ...), custom_call_target="tpu_custom_call" | custom-call | flops 1000000000 | bytes 1781760 | tf_op jit(solution)/shard_map/correction_operator/pallas_call | solution.py:33
  25.9 0.0 collective-permute-done.10
  25.9 1.0 %collective-permute-done.9 = bf16[128,256]{1,0:T(8,128)(2,1)S(1)} collective-permute-done((bf16[128,256]{1,0:T(8,128)(2,1)S(1)}, bf16[128,256]{1,0:T(8,128)(2,1)S(1)}, u32[]{:S(2)}, u32[]{:S(2)}) %collective-permute-start.9) | collective-permute-done | bytes 65568 | tf_op jit(solution)/shard_map/ppermute | solution.py:416
  27.0 1.2 %collective-permute-done.8 = bf16[128,256]{1,0:T(8,128)(2,1)S(1)} collective-permute-done((bf16[128,256]{1,0:T(8,128)(2,1)S(1)}, bf16[128,256]{1,0:T(8,128)(2,1)S(1)}, u32[]{:S(2)}, u32[]{:S(2)}) %collective-permute-start.8) | collective-permute-done | bytes 65568 | tf_op jit(solution)/shard_map/ppermute | solution.py:428
  28.2 0.3 %collective-permute-start.11 = (bf16[512,256]{1,0:T(8,128)(2,1)S(1)}, bf16[512,256]{1,0:T(8,128)(2,1)S(1)}, u32[]{:S(2)}, u32[]{:S(2)}) collective-permute-start(bf16[512,256]{1,0:T(8,128)(2,1)S(1)} %pad_maximum_fusion.held_ref), channel_id=1, source_target_pairs={{0,1},{1,0},{2,3},{3,2},{4,5},{5,4},{6,7},{7,6},{8,9},{9,8},{10,11... | collective-permute-start | bytes 786440 | tf_op jit(solution)/shard_map/ppermute | solution.py:412
  28.6 0.6 %own_part.1.own_ref = f32[1248,256]{1,0:T(8,128)S(1)} custom-call(bf16[512,256]{1,0:T(8,128)(2,1)S(1)} %pad_maximum_fusion.held_ref, bf16[32,256]{1,0:T(8,128)(2,1)S(1)} %get-tuple-element.52.low_ref, bf16[32,256]{1,0:T(8,128)(2,1)S(1)} %collective-permute-done.7.far_low_ref, bf16[1248,512]{1,0:T(8,128)(2,1)S(1)} %get-tuple-element.71.operator_ref, ...), custom_call_target="tpu_custom_call" | custom-call | flops 400000000 | bytes 2519040 | tf_op jit(solution)/shard_map/own_part/pallas_call | solution.py:33
  29.2 0.6 %collective-permute-done.11.held_ref = bf16[512,256]{1,0:T(8,128)(2,1)S(1)} collective-permute-done((bf16[512,256]{1,0:T(8,128)(2,1)S(1)}, bf16[512,256]{1,0:T(8,128)(2,1)S(1)}, u32[]{:S(2)}, u32[]{:S(2)}) %collective-permute-start.11) | collective-permute-done | bytes 262176 | tf_op jit(solution)/shard_map/ppermute | solution.py:412
  29.8 1.2 %finish.1 = (bf16[768,256]{1,0:T(8,128)(2,1)}, bf16[480,256]{1,0:T(8,128)(2,1)}) custom-call(bf16[512,256]{1,0:T(8,128)(2,1)S(1)} %collective-permute-done.11.held_ref, bf16[1248,512]{1,0:T(8,128)(2,1)S(1)} %get-tuple-element.69.operator_ref, f32[1248,256]{1,0:T(8,128)S(1)} %own_part.1.own_ref), custom_call_target="tpu_custom_call" | custom-call | flops 400000000 | bytes 2818048 | tf_op jit(solution)/shard_map/finish/pallas_call | solution.py:33
  (2 shorter events, 0.1 us)
Async XLA Ops:
  3.5 4.7 %collective-permute-start.3 = (bf16[544,512]{1,0:T(8,128)(2,1)S(1)}, bf16[544,512]{1,0:T(8,128)(2,1)S(1)}, u32[]{:S(2)}, u32[]{:S(2)}) collective-permute-start(bf16[544,512]{1,0:T(8,128)(2,1)S(1)} %get-tuple-element.43.own_ref.pack_ref), channel_id=1, source_target_pairs={{0,1},{1,0},{2,3},{3,2},{4,5},{5,4},{6,7},{7,6},{8,9},{9,8},{10,11... | collective-permute-start | bytes 1671176 | tf_op jit(solution)/shard_map/ppermute | solution.py:412
  4.0 6.4 %collective-permute-start = (bf16[144,256]{1,0:T(8,128)(2,1)S(1)}, bf16[144,256]{1,0:T(8,128)(2,1)S(1)}, u32[]{:S(2)}, u32[]{:S(2)}) collective-permute-start(bf16[144,256]{1,0:T(8,128)(2,1)S(1)} %get-tuple-element.40), channel_id=1, source_target_pairs={{0,6},{2,4},{4,2},{6,0},{8,14},{10,12},{12,10},{14,8},{16,22},{18,... | collective-permute-start | bytes 221192 | tf_op jit(solution)/shard_map/ppermute | solution.py:416
  7.6 4.4 %collective-permute-start.1 = (bf16[144,256]{1,0:T(8,128)(2,1)S(1)}, bf16[144,256]{1,0:T(8,128)(2,1)S(1)}, u32[]{:S(2)}, u32[]{:S(2)}) collective-permute-start(bf16[144,256]{1,0:T(8,128)(2,1)S(1)} %get-tuple-element.41), channel_id=1, source_target_pairs={{0,4},{2,6},{4,0},{6,2},{8,12},{10,14},{12,8},{14,10},{16,20},{18,... | collective-permute-start | bytes 221192 | tf_op jit(solution)/shard_map/ppermute | solution.py:416
  8.1 4.4 %collective-permute-start.2 = (bf16[144,256]{1,0:T(8,128)(2,1)S(1)}, bf16[144,256]{1,0:T(8,128)(2,1)S(1)}, u32[]{:S(2)}, u32[]{:S(2)}) collective-permute-start(bf16[144,256]{1,0:T(8,128)(2,1)S(1)} %get-tuple-element.42), channel_id=1, source_target_pairs={{0,2},{2,0},{4,6},{6,4},{8,10},{10,8},{12,14},{14,12},{16,18},{18,... | collective-permute-start | bytes 221192 | tf_op jit(solution)/shard_map/ppermute | solution.py:416
  8.2 10.1 %copy-start.1 = (bf16[1,1,512,768]{3,2,1,0:T(8,128)(2,1)S(1)}, bf16[1,1,512,768]{3,2,1,0:T(8,128)(2,1)}, u32[]{:S(2)}) copy-start(bf16[1,1,512,768]{3,2,1,0:T(8,128)(2,1)} %param.13) | copy-start | bytes 2359300
  10.3 7.9 %copy-start = (bf16[1,1,768,768]{3,2,1,0:T(8,128)(2,1)S(1)}, bf16[1,1,768,768]{3,2,1,0:T(8,128)(2,1)}, u32[]{:S(2)}) copy-start(bf16[1,1,768,768]{3,2,1,0:T(8,128)(2,1)} %param.12) | copy-start | bytes 3538948
  10.3 7.9 %copy-start.2 = (s32[1,1,512]{2,1,0:T(1,128)S(1)}, s32[1,1,512]{2,1,0:T(1,128)}, u32[]{:S(2)}) copy-start(s32[1,1,512]{2,1,0:T(1,128)} %param.14) | copy-start | bytes 6148
  12.7 6.9 %collective-permute-start.6 = (bf16[128,256]{1,0:T(8,128)(2,1)S(1)}, bf16[128,256]{1,0:T(8,128)(2,1)S(1)}, u32[]{:S(2)}, u32[]{:S(2)}) collective-permute-start(bf16[128,256]{1,0:T(8,128)(2,1)S(1)} %get-tuple-element.51), channel_id=1, source_target_pairs={{0,8},{2,10},{4,12},{6,14},{8,16},{10,18},{12,20},{14,22},{16,24},... | collective-permute-start | bytes 196616 | tf_op jit(solution)/shard_map/ppermute | solution.py:421
  14.3 7.2 %collective-permute-start.5 = (bf16[128,256]{1,0:T(8,128)(2,1)S(1)}, bf16[128,256]{1,0:T(8,128)(2,1)S(1)}, u32[]{:S(2)}, u32[]{:S(2)}) collective-permute-start(bf16[128,256]{1,0:T(8,128)(2,1)S(1)} %get-tuple-element.51), channel_id=1, source_target_pairs={{0,16},{2,18},{4,20},{6,22},{8,24},{10,26},{12,28},{14,30},{16,0},... | collective-permute-start | bytes 196616 | tf_op jit(solution)/shard_map/ppermute | solution.py:421
  16.9 4.7 %collective-permute-start.4 = (bf16[128,256]{1,0:T(8,128)(2,1)S(1)}, bf16[128,256]{1,0:T(8,128)(2,1)S(1)}, u32[]{:S(2)}, u32[]{:S(2)}) collective-permute-start(bf16[128,256]{1,0:T(8,128)(2,1)S(1)} %get-tuple-element.51), channel_id=1, source_target_pairs={{0,24},{2,26},{4,28},{6,30},{8,0},{10,2},{12,4},{14,6},{16,8},{18,... | collective-permute-start | bytes 196616 | tf_op jit(solution)/shard_map/ppermute | solution.py:421
  18.3 1.3 %collective-permute-start.7 = (bf16[32,256]{1,0:T(8,128)(2,1)S(1)}, bf16[32,256]{1,0:T(8,128)(2,1)S(1)}, u32[]{:S(2)}, u32[]{:S(2)}) collective-permute-start(bf16[32,256]{1,0:T(8,128)(2,1)S(1)} %get-tuple-element.52.low_ref), channel_id=1, source_target_pairs={{0,1},{1,0},{2,3},{3,2},{4,5},{5,4},{6,7},{7,6},{8,9},{9,8},{10,11... | collective-permute-start | bytes 49160 | tf_op jit(solution)/shard_map/ppermute | solution.py:412
  21.6 4.3 %collective-permute-start.10 = (bf16[128,256]{1,0:T(8,128)(2,1)S(1)}, bf16[128,256]{1,0:T(8,128)(2,1)S(1)}, u32[]{:S(2)}, u32[]{:S(2)}) collective-permute-start(bf16[128,256]{1,0:T(8,128)(2,1)S(1)} %add_convert_fusion), channel_id=1, source_target_pairs={{0,5},{1,4},{2,7},{3,6},{4,1},{5,0},{6,3},{7,2},{8,13},{9,12},{10,... | collective-permute-start | bytes 196616 | tf_op jit(solution)/shard_map/ppermute | solution.py:428
  21.8 5.2 %collective-permute-start.9 = (bf16[128,256]{1,0:T(8,128)(2,1)S(1)}, bf16[128,256]{1,0:T(8,128)(2,1)S(1)}, u32[]{:S(2)}, u32[]{:S(2)}) collective-permute-start(bf16[128,256]{1,0:T(8,128)(2,1)S(1)} %add_convert_fusion), channel_id=1, source_target_pairs={{0,6},{2,4},{4,2},{6,0},{8,14},{10,12},{12,10},{14,8},{16,22},{18,... | collective-permute-start | bytes 196616 | tf_op jit(solution)/shard_map/ppermute | solution.py:416
  23.8 4.4 %collective-permute-start.8 = (bf16[128,256]{1,0:T(8,128)(2,1)S(1)}, bf16[128,256]{1,0:T(8,128)(2,1)S(1)}, u32[]{:S(2)}, u32[]{:S(2)}) collective-permute-start(bf16[128,256]{1,0:T(8,128)(2,1)S(1)} %add_convert_fusion), channel_id=1, source_target_pairs={{0,3},{1,2},{2,1},{3,0},{4,7},{5,6},{6,5},{7,4},{8,11},{9,10},{10,... | collective-permute-start | bytes 196616 | tf_op jit(solution)/shard_map/ppermute | solution.py:428
  28.2 1.6 %collective-permute-start.11 = (bf16[512,256]{1,0:T(8,128)(2,1)S(1)}, bf16[512,256]{1,0:T(8,128)(2,1)S(1)}, u32[]{:S(2)}, u32[]{:S(2)}) collective-permute-start(bf16[512,256]{1,0:T(8,128)(2,1)S(1)} %pad_maximum_fusion.held_ref), channel_id=1, source_target_pairs={{0,1},{1,0},{2,3},{3,2},{4,5},{5,4},{6,7},{7,6},{8,9},{9,8},{10,11... | collective-permute-start | bytes 786440 | tf_op jit(solution)/shard_map/ppermute | solution.py:412
